TPU v7x, 32 devices: a whole 2x2x4 slice. The times are simulated.
32 devices in a mesh: band: 16 (over z, x, core), var: 2 (over y).
Axes of the slice: x: 2, y: 2, z: 4, core: 2. Of those that a mesh axis runs over, the one named last changes fastest.
Arguments:
- pixels: bfloat16 [16, 16, 4096], P('var', None, 'band'), may hold values from -6 to 6
- embed_weight: bfloat16 [16, 16, 1024], P('var'), may hold values from -1.5 to 1.5
- variable_embed: bfloat16 [16, 1024], P('var'), may hold values from -6 to 6
- agg_key: bfloat16 [1024, 16], replicated, may hold values from -0.1875 to 0.1875
- agg_value: bfloat16 [1024, 1024], replicated, may hold values from -0.1875 to 0.1875
- position: bfloat16 [4096, 1024], P(('band', 'var')), may hold values from -6 to 6
- qkv_weight: bfloat16 [1024, 3, 1024], P(None, None, 'var'), may hold values from -0.375 to 0.375
- out_weight: bfloat16 [1024, 1024], P('var'), may hold values from -0.1875 to 0.1875
Outputs:
- block_out: bfloat16 [4096, 1024], P(('band', 'var'))
All inputs are finite; a program needn't handle non-finite values.
Results may differ from a plain program's by a relative error of at most 0.015.
The roundings to bfloat16 on the way count: a program that leaves them out, or rounds other values in their place, can miss the bound.
Values may be sent and summed in bfloat16 or wider, within the bound.
No kernel may reach another device: no remote copies, remote signals or barrier semaphores. Data moves between devices by JAX's collectives and lax.ppermute only.
A program may use at most 64 MiB of HBM per device.

v0:
```python
import jax
import jax.numpy as jnp
from jax import lax
from jax.sharding import PartitionSpec as P

D = 1024
HEADS = 16
HEAD_DIM = 64


epsilon = 1e-05


def passed_along(block, axis, distance):
    devices = range(lax.axis_size(axis))
    route = [((i - distance) % len(devices), i) for i in devices]
    return lax.ppermute(block, axis, route)


def embed_vars(pixel_rows, table, offsets):
    summed = jnp.einsum("vpt,vpd->vtd", pixel_rows, table, preferred_element_type=jnp.float32)
    return (summed + offsets.astype(jnp.float32)[:, None, :]).astype(jnp.bfloat16)


def normalize(values):
    centre = jnp.mean(values, axis=-1, keepdims=True)
    spread = jnp.mean(jnp.square(values - centre), axis=-1, keepdims=True)
    return (values - centre) * lax.rsqrt(spread + epsilon)


def aggregate(embedded, agg_key, agg_value, position):
    scores = jnp.einsum("vtd,dh->tvh", embedded, agg_key, preferred_element_type=jnp.float32)
    expos = jnp.exp(scores)
    weights = (expos / jnp.sum(expos, axis=1, keepdims=True)).astype(jnp.bfloat16)
    pooled = jnp.einsum(
        "tvh,vtd->thd", weights, embedded, preferred_element_type=jnp.float32
    ).astype(jnp.bfloat16)
    value_heads = agg_value.reshape(D, HEADS, HEAD_DIM)
    merged = jnp.einsum("thd,dhe->the", pooled, value_heads, preferred_element_type=jnp.float32)
    return merged.reshape(merged.shape[0], D) + position.astype(jnp.float32)


def shards(
    pixels, embed_weight, variable_embed, agg_key, agg_value, position, qkv_weight, out_weight
):
    band_tok = pixels.shape[2]
    local_embed = embed_vars(pixels, embed_weight, variable_embed)
    embedded = lax.all_to_all(local_embed, "var", split_axis=1, concat_axis=0, tiled=True)
    merged = aggregate(embedded, agg_key, agg_value, position)
    normed = normalize(merged).astype(jnp.bfloat16)
    qkv_band = jnp.einsum(
        "td,dcf->tcf",
        lax.all_gather(normed, "var", axis=0, tiled=True),
        qkv_weight,
        preferred_element_type=jnp.float32,
    ).astype(jnp.bfloat16)
    width = qkv_band.shape[2]
    local_heads = width // HEAD_DIM
    scale = HEAD_DIM ** (-0.5)
    query_heads = (qkv_band[:, 0] * scale).reshape(band_tok, local_heads, HEAD_DIM)
    pairs = qkv_band[:, 1:]

    def absorb(totals, block):
        numer, denom = totals
        key_heads = block[:, 0].reshape(-1, local_heads, HEAD_DIM)
        val_heads = block[:, 1].reshape(-1, local_heads, HEAD_DIM)
        scores = jnp.einsum(
            "thd,shd->hts", query_heads, key_heads, preferred_element_type=jnp.float32
        )
        expos = jnp.exp(scores)
        denom = denom + jnp.sum(expos, axis=-1)
        numer = numer + jnp.einsum(
            "hts,shd->thd",
            expos.astype(jnp.bfloat16),
            val_heads,
            preferred_element_type=jnp.float32,
        )
        return (numer, denom)

    initial = (
        jnp.zeros((band_tok, local_heads, HEAD_DIM), jnp.float32),
        jnp.zeros((local_heads, band_tok), jnp.float32),
    )
    totals = absorb(initial, pairs)
    eastward = passed_along(pairs, "band", 1)
    totals = absorb(totals, eastward)
    westward = passed_along(pairs, "band", -1)
    totals = absorb(totals, westward)
    numer, denom = totals
    context = (
        (numer / jnp.transpose(denom)[:, :, None]).astype(jnp.bfloat16).reshape(band_tok, width)
    )
    update = lax.psum_scatter(
        jnp.dot(context, out_weight, preferred_element_type=jnp.float32).astype(jnp.bfloat16),
        "var",
        scatter_dimension=0,
        tiled=True,
    ).astype(jnp.float32)
    return (merged + update).astype(jnp.bfloat16)


def solution(mesh):
    in_specs = (
        P("var", None, "band"),
        P("var", None, None),
        P("var", None),
        P(),
        P(),
        P(("band", "var"), None),
        P(None, None, "var"),
        P("var", None),
    )
    out_specs = P(("band", "var"), None)
    return jax.shard_map(shards, mesh=mesh, in_specs=in_specs, out_specs=out_specs, check_vma=False)
```

profile of v0, /device:TPU:0, one launch (start us, length us, event | category | flops | bytes accessed | tf_op | source)
XLA Modules:
  0.0 159.6 jit_solution(16752250582938534190)
XLA Ops:
  7.4 2.4 %add_convert_fusion = bf16[8,256,1024]{2,1,0:T(8,128)(2,1)S(1)} fusion(f32[8,1024]{1,0:T(8,128)S(1)} %convert_element_type.42, bf16[8,16,256]{2,1,0:T(8,128)(2,1)} %param.8, bf16[8,16,1024]{2,1,0:T(8,128)(2,1)} %param.9), kind=kOutput, calls=%fused_computation | convolution fusion | flops 71303168 | bytes 4554752 | tf_op jit(solution)/shard_map/vpt,vpd->vtd/dot_general | solution.py:21
  9.8 4.3 %copy.37 = bf16[8,256,1024]{2,0,1:T(8,128)(2,1)} copy(bf16[8,256,1024]{2,1,0:T(8,128)(2,1)S(1)} %add_convert_fusion) | data formatting | bytes 8388608 | tf_op jit(solution)/shard_map/convert_element_type | solution.py:22
  14.1 5.6 %all-to-all-start = ((bf16[8,256,1024]{2,0,1:T(8,128)(2,1)}), bf16[8,256,1024]{2,0,1:T(8,128)(2,1)}, u32[]{:S(2)}, u32[]{:S(2)}) async-start(bf16[8,256,1024]{2,0,1:T(8,128)(2,1)} %copy.37), calls=%async_computation | async-start | bytes 8388608 | tf_op jit(solution)/shard_map/all_to_all | solution.py:48
  19.9 3.9 %copy.41 = bf16[1024,1024]{0,1:T(8,128)(2,1)} copy(bf16[1024,1024]{1,0:T(8,128)(2,1)} %param.12) | data formatting | bytes 4194304 | tf_op args[4]
  23.8 44.7 %all-to-all-done = bf16[8,256,1024]{2,0,1:T(8,128)(2,1)} async-done(((bf16[8,256,1024]{2,0,1:T(8,128)(2,1)}), bf16[8,256,1024]{2,0,1:T(8,128)(2,1)}, u32[]{:S(2)}, u32[]{:S(2)}) %all-to-all-start) | async-done | bytes 4194336 | tf_op jit(solution)/shard_map/all_to_all | solution.py:48
  68.5 4.5 %copy.38 = bf16[8,2,128,1024]{3,2,0,1:T(8,128)(2,1)S(1)} copy(bf16[8,2,128,1024]{3,0,2,1:T(8,128)(2,1)} %bitcast) | data formatting | bytes 8388608 | tf_op jit(solution)/shard_map/all_to_all | solution.py:48
  73.1 1.9 %copy-done.1 = bf16[8,2,128,1024]{3,2,0,1:T(8,128)(2,1)} copy-done((bf16[8,2,128,1024]{3,2,0,1:T(8,128)(2,1)}, bf16[8,2,128,1024]{3,2,0,1:T(8,128)(2,1)S(1)}, u32[]{:S(2)}) %copy-start.1) | copy-done | bytes 4194328
  77.4 5.4 %fusion.4 = bf16[128,16,1024]{2,1,0:T(8,128)(2,1)S(1)} fusion(bf16[128,16,16]{1,2,0:T(8,128)(2,1)} %copy.39, bf16[16,128,1024]{2,1,0:T(8,128)(2,1)} %bitcast.52), kind=kOutput, calls=%fused_computation.5 | convolution fusion | flops 69206016 | bytes 8454144 | tf_op jit(solution)/shard_map/tvh,vtd->thd/dot_general | solution.py:35
  82.9 3.4 %fusion = f32[16,128,64]{1,2,0:T(8,128)} fusion(bf16[1024,16,64]{0,2,1:T(8,128)(2,1)S(1)} %bitcast.56, bf16[128,16,1024]{2,1,0:T(8,128)(2,1)S(1)} %fusion.4), kind=kOutput, calls=%fused_computation.1 | convolution fusion | flops 268435456 | bytes 6815744 | tf_op jit(solution)/shard_map/thd,dhe->the/dot_general | solution.py:39
  86.3 2.0 %copy.43 = f32[128,1024]{1,0:T(8,128)} copy(f32[128,1024]{0,1:T(8,128)} %bitcast.64) | data formatting | bytes 1048576 | tf_op jit(solution)/shard_map/reshape | solution.py:40
  92.0 8.2 %all_gather.3 = bf16[256,1024]{1,0:T(8,128)(2,1)S(1)} all-gather(bf16[128,1024]{1,0:T(8,128)(2,1)S(1)} %multiply_convert_fusion), channel_id=1, replica_groups=mesh['band'=16,'var'=2] {'var'}, dimensions={0}, use_global_device_ids=true | all-gather | bytes 786432 | tf_op jit(solution)/shard_map/all_gather | solution.py:53
  102.9 2.1 %collective-permute-start.1 = (bf16[256,2,512]{2,0,1:T(8,128)(2,1)}, bf16[256,2,512]{2,0,1:T(8,128)(2,1)}, u32[]{:S(2)}, u32[]{:S(2)}) collective-permute-start(bf16[256,2,512]{2,0,1:T(8,128)(2,1)} %slice.37), channel_id=1, source_target_pairs={{2,0},{4,2},{6,4},{8,6},{10,8},{12,10},{14,12},{16,14},{18,16},{20... | collective-permute-start | bytes 1572872 | tf_op jit(solution)/shard_map/ppermute | solution.py:17
  106.0 1.8 %copy.46 = bf16[256,1,512]{0,2,1:T(8,128)(2,1)} copy(bf16[256,1,512]{2,0,1:T(8,128)(2,1)} %get-tuple-element.5) | data formatting | bytes 524288 | tf_op jit(solution)/shard_map/slice | solution.py:65
  107.8 1.8 %copy.44 = bf16[256,1,512]{0,2,1:T(8,128)(2,1)} copy(bf16[256,1,512]{2,0,1:T(8,128)(2,1)} %get-tuple-element.7) | data formatting | bytes 524288 | tf_op jit(solution)/shard_map/slice | solution.py:66
  111.1 2.2 %fusion.11 = f32[8,64,256]{2,1,0:T(8,128)} fusion(bf16[256,8,64]{0,2,1:T(8,128)(2,1)} %bitcast.63, f32[8,256,256]{1,2,0:T(8,128)S(1)} %get-tuple-element.17), kind=kOutput, calls=%fused_computation.21 | convolution fusion | flops 67633152 | bytes 2883584 | tf_op jit(solution)/shard_map/hts,shd->thd/dot_general | solution.py:72
  113.3 1.9 %fusion.16 = (bf16[256,1,512]{2,0,1:T(8,128)(2,1)}, bf16[256,1,512]{2,0,1:T(8,128)(2,1)}) fusion(bf16[256,2,512]{2,0,1:T(8,128)(2,1)} %collective-permute-done.1), kind=kLoop, calls=%fused_computation.35 | loop fusion | bytes 1048576 | tf_op jit(solution)/shard_map/slice | solution.py:65
  117.0 2.8 %exponential_reduce_fusion = (f32[8,256]{1,0:T(8,128)S(1)}, f32[8,256,256]{1,2,0:T(8,128)}) fusion(bf16[256,8,64]{0,2,1:T(8,128)(2,1)S(1)} %bitcast.54, bf16[256,8,64]{0,2,1:T(8,128)(2,1)} %bitcast.61), kind=kOutput, calls=%fused_computation.6 | convolution fusion | flops 67631104 | bytes 2629632 | tf_op jit(solution)/shard_map/thd,shd->hts/dot_general | solution.py:67
  119.8 1.9 %fusion.17 = (bf16[256,1,512]{2,0,1:T(8,128)(2,1)}, bf16[256,1,512]{2,0,1:T(8,128)(2,1)}) fusion(bf16[256,2,512]{2,0,1:T(8,128)(2,1)} %collective-permute-done), kind=kLoop, calls=%fused_computation.36 | loop fusion | bytes 1048576 | tf_op jit(solution)/shard_map/slice | solution.py:65
  121.7 1.8 %copy.49 = bf16[256,1,512]{0,2,1:T(8,128)(2,1)} copy(bf16[256,1,512]{2,0,1:T(8,128)(2,1)} %get-tuple-element.10) | data formatting | bytes 524288 | tf_op jit(solution)/shard_map/slice | solution.py:65
  123.5 2.8 %exponential_reduce_fusion.1 = (f32[8,256]{1,0:T(8,128)S(1)}, f32[8,256,256]{1,2,0:T(8,128)}) fusion(bf16[256,8,64]{0,2,1:T(8,128)(2,1)S(1)} %bitcast.55, bf16[256,8,64]{0,2,1:T(8,128)(2,1)} %bitcast.60), kind=kOutput, calls=%fused_computation.8 | convolution fusion | flops 67631104 | bytes 2629632 | tf_op jit(solution)/shard_map/thd,shd->hts/dot_general | solution.py:67
  127.3 1.8 %copy.51 = bf16[256,1,512]{0,2,1:T(8,128)(2,1)} copy(bf16[256,1,512]{2,0,1:T(8,128)(2,1)} %get-tuple-element.9) | data formatting | bytes 524288 | tf_op jit(solution)/shard_map/slice | solution.py:66
  129.1 2.3 %convolution_add_fusion.1 = f32[8,64,256]{2,1,0:T(8,128)S(1)} fusion(f32[8,64,256]{2,1,0:T(8,128)} %fusion.11, bf16[256,8,64]{0,2,1:T(8,128)(2,1)S(1)} %bitcast.62, f32[8,256,256]{1,2,0:T(8,128)} %get-tuple-element.19), kind=kOutput, calls=%fused_computation.16 | convolution fusion | flops 67764224 | bytes 3407872 | tf_op jit(solution)/shard_map/hts,shd->thd/dot_general | solution.py:72
  133.2 17.6 %reduce-scatter.2.cloned.1.call-done = bf16[128,1024]{1,0:T(8,128)(2,1)} async-done(((bf16[256,1024]{1,0:T(8,128)(2,1)}), bf16[128,1024]{1,0:T(8,128)(2,1)}) %reduce-scatter.2.cloned.1.call-update) | async-done | bytes 262160 | tf_op jit(solution)/shard_map/reduce_scatter | solution.py:93
  150.8 1.9 %add_convert_fusion.1 = bf16[128,1024]{1,0:T(8,128)(2,1)} fusion(bf16[128,1024]{1,0:T(8,128)(2,1)} %reduce-scatter.2.cloned.1.call-done, f32[128,1024]{1,0:T(8,128)} %copy.43, bf16[128,1024]{1,0:T(8,128)(2,1)S(1)} %copy-done.4), kind=kLoop, calls=%fused_computation.23 | loop fusion | flops 655360 | bytes 1310720 | tf_op jit(solution)/shard_map/convert_element_type | solution.py:99
  (41 shorter events, 17.1 us)
Async XLA Ops:
  6.5 93.6 %copy-start = (bf16[1024,3,512]{2,0,1:T(8,128)(2,1)S(1)}, bf16[1024,3,512]{2,0,1:T(8,128)(2,1)}, u32[]{:S(2)}) copy-start(bf16[1024,3,512]{2,0,1:T(8,128)(2,1)} %param.14) | copy-start | bytes 9437188
  14.1 54.5 %all-to-all-start = ((bf16[8,256,1024]{2,0,1:T(8,128)(2,1)}), bf16[8,256,1024]{2,0,1:T(8,128)(2,1)}, u32[]{:S(2)}, u32[]{:S(2)}) async-start(bf16[8,256,1024]{2,0,1:T(8,128)(2,1)} %copy.37), calls=%async_computation | async-start | bytes 8388608 | tf_op jit(solution)/shard_map/all_to_all | solution.py:48
  19.7 131.1 %reduce-scatter.2.cloned.1.call-start = ((), (), s32[]{:S(2)}) async-start(), calls=%async_computation.2 | async-start | bytes 786432 | tf_op jit(solution)/shard_map/reduce_scatter | solution.py:93
  68.5 6.5 %copy-start.8 = (bf16[1024,16]{0,1:T(8,128)(2,1)S(1)}, bf16[1024,16]{0,1:T(8,128)(2,1)}, u32[]{:S(2)}) copy-start(bf16[1024,16]{0,1:T(8,128)(2,1)} %param.11) | copy-start | bytes 98308
  73.1 1.9 %copy-start.1 = (bf16[8,2,128,1024]{3,2,0,1:T(8,128)(2,1)}, bf16[8,2,128,1024]{3,2,0,1:T(8,128)(2,1)S(1)}, u32[]{:S(2)}) copy-start(bf16[8,2,128,1024]{3,2,0,1:T(8,128)(2,1)S(1)} %copy.38) | copy-start | bytes 12582916
  77.4 5.5 %copy-start.5 = (bf16[1024,1024]{0,1:T(8,128)(2,1)S(1)}, bf16[1024,1024]{0,1:T(8,128)(2,1)}, u32[]{:S(2)}) copy-start(bf16[1024,1024]{0,1:T(8,128)(2,1)} %copy.41) | copy-start | bytes 6291460
  82.9 5.5 %copy-start.3 = (bf16[128,1024]{1,0:T(8,128)(2,1)S(1)}, bf16[128,1024]{1,0:T(8,128)(2,1)}, u32[]{:S(2)}) copy-start(bf16[128,1024]{1,0:T(8,128)(2,1)} %param.13) | copy-start | bytes 786436
  102.9 10.5 %collective-permute-start.1 = (bf16[256,2,512]{2,0,1:T(8,128)(2,1)}, bf16[256,2,512]{2,0,1:T(8,128)(2,1)}, u32[]{:S(2)}, u32[]{:S(2)}) collective-permute-start(bf16[256,2,512]{2,0,1:T(8,128)(2,1)} %slice.37), channel_id=1, source_target_pairs={{2,0},{4,2},{6,4},{8,6},{10,8},{12,10},{14,12},{16,14},{18,16},{20... | collective-permute-start | bytes 1572872 | tf_op jit(solution)/shard_map/ppermute | solution.py:17
  105.0 14.8 %collective-permute-start = (bf16[256,2,512]{2,0,1:T(8,128)(2,1)}, bf16[256,2,512]{2,0,1:T(8,128)(2,1)}, u32[]{:S(2)}, u32[]{:S(2)}) collective-permute-start(bf16[256,2,512]{2,0,1:T(8,128)(2,1)} %slice.37), channel_id=1, source_target_pairs={{30,0},{0,2},{2,4},{4,6},{6,8},{8,10},{10,12},{12,14},{14,16},{16,... | collective-permute-start | bytes 1572872 | tf_op jit(solution)/shard_map/ppermute | solution.py:17
  129.1 2.4 %copy-start.2 = (f32[8,256,256]{1,2,0:T(8,128)S(1)}, f32[8,256,256]{1,2,0:T(8,128)}, u32[]{:S(2)}) copy-start(f32[8,256,256]{1,2,0:T(8,128)} %get-tuple-element.15) | copy-start | bytes 6291460
  129.1 2.4 %copy-start.7 = (bf16[256,1,512]{0,2,1:T(8,128)(2,1)S(1)}, bf16[256,1,512]{0,2,1:T(8,128)(2,1)}, u32[]{:S(2)}) copy-start(bf16[256,1,512]{0,2,1:T(8,128)(2,1)} %copy.51) | copy-start | bytes 786436
  129.1 2.8 %copy-start.6 = (bf16[512,1024]{1,0:T(8,128)(2,1)S(1)}, bf16[512,1024]{1,0:T(8,128)(2,1)}, u32[]{:S(2)}) copy-start(bf16[512,1024]{1,0:T(8,128)(2,1)} %param.15) | copy-start | bytes 3145732
  131.4 19.4 %copy-start.4 = (bf16[128,1024]{1,0:T(8,128)(2,1)S(1)}, bf16[128,1024]{1,0:T(8,128)(2,1)}, u32[]{:S(2)}) copy-start(bf16[128,1024]{1,0:T(8,128)(2,1)} %param.13) | copy-start | bytes 786436
Sparse Core Ops, SparseCore 0:
  133.4 17.4 reduce-scatter.1
where the time goes:
time: 160 us
  waiting for transfers between devices  62.3 us (39%)
  local copies, waits for them, and re-layouts  33.7 us (21%)
  matrix products  26.7 us (17%)
  between operations  13.5 us (8%)
  blocking collectives  8.17 us (5%)
  starting transfers between devices  7.9 us (5%)
  other arithmetic  7.32 us (5%)
    all_to_all x1, waiting for transfers between devices, shards(): lax.all_to_all(local_embed, 'var', split_axis=1, concat_axis=0, tiled=True)  44.7 us
    reduce_scatter x1, waiting for transfers between devices, shards(): lax.psum_scatter(jnp.dot(context, out_weight, preferred_element_type=jnp....  17.6 us
    slice x5, local copies, waits for them, and re-layouts, absorb(): key_heads = block[:, 0].reshape(-1, local_heads, HEAD_DIM)  9.12 us
    all_gather x1, blocking collectives, shards(): lax.all_gather(normed, 'var', axis=0, tiled=True)  8.17 us
    dot_general x3, matrix products, absorb(): jnp.einsum('thd,shd->hts', query_heads, key_heads, preferred_element_type...  7.02 us
    unnamed x19, local copies, waits for them, and re-layouts  5.95 us
    all_to_all x1, starting transfers between devices, shards(): lax.all_to_all(local_embed, 'var', split_axis=1, concat_axis=0, tiled=True)  5.6 us
    dot_general x1, matrix products, aggregate(): jnp.einsum('tvh,vtd->thd', weights, embedded, preferred_element_type=jnp....  5.44 us
  transfers between devices with their start and end apart: 4, of which 2 were waited for; matrix products, arithmetic and copies ran while one was open for 12% of the time, Pallas kernels for 0%

commit v1 on v0

v1 whole, which is shorter than its diff:
```python
import functools

import jax
import jax.numpy as jnp
from jax import lax
from jax.experimental import pallas as pl
from jax.experimental.pallas import tpu as pltpu
from jax.sharding import PartitionSpec as P

HEAD_DIM = 64
EPSILON = 1e-05
F32 = jnp.float32
BF16 = jnp.bfloat16
NT = (((1,), (1,)), ((), ()))
NN = (((1,), (0,)), ((), ()))


def dot(a, b, dims=NN):
    return lax.dot_general(a, b, dims, preferred_element_type=F32)


def shifted(block, axis, distance):
    n = lax.axis_size(axis)
    return lax.ppermute(block, axis, [((i + distance) % n, i) for i in range(n)])


def call(body, outs, args, flops, name):
    nbytes = sum(a.size * a.dtype.itemsize for a in (*args, *outs))
    return pl.pallas_call(
        body,
        out_shape=outs,
        in_specs=[pl.BlockSpec(memory_space=pltpu.VMEM) for _ in args],
        out_specs=[pl.BlockSpec(memory_space=pltpu.VMEM) for _ in outs],
        compiler_params=pltpu.CompilerParams(vmem_limit_bytes=40 * 1024 * 1024),
        cost_estimate=pl.CostEstimate(flops=flops, bytes_accessed=nbytes, transcendentals=0),
        name=name,
    )(*args)


def fold(table, offsets, key_t, agg_value):
    values = jnp.transpose(dot(table, agg_value)).astype(BF16)
    offset_values = jnp.transpose(dot(offsets, agg_value)).astype(BF16)
    return values, offset_values, dot(key_t, table, NT), dot(key_t, offsets, NT)


def fold_body(table, offsets, key_t, agg_value, *outs):
    for out, part in zip(outs, fold(table[...], offsets[...], key_t[...], agg_value[...])):
        out[...] = part


def front(pix, values, offset_values, keys, offset_keys, position):
    n_heads, n_rows = keys.shape
    n_vars = offset_keys.shape[1]
    n_pix = n_rows // n_vars
    tok = pix.shape[1]
    rows = lax.broadcasted_iota(jnp.int32, (n_vars * n_heads, n_rows), 0) // n_heads
    cols = lax.broadcasted_iota(jnp.int32, (n_vars * n_heads, n_rows), 1) // n_pix
    spread = jnp.where(rows == cols, jnp.concatenate([keys] * n_vars, axis=0), 0.0)
    high = spread.astype(BF16)
    low = (spread - high.astype(F32)).astype(BF16)
    rows = lax.broadcasted_iota(jnp.int32, (n_vars * n_heads, n_vars), 0) // n_heads
    cols = lax.broadcasted_iota(jnp.int32, (n_vars * n_heads, n_vars), 1)
    base = jnp.sum(
        jnp.where(rows == cols, jnp.concatenate([offset_keys] * n_vars, axis=0), 0.0), axis=1, keepdims=True
    )
    scores = dot(high, pix) + dot(low, pix) + base
    expos = jnp.exp(scores).reshape(n_vars, n_heads, tok)
    weights = (expos / jnp.sum(expos, axis=0, keepdims=True)).astype(BF16).astype(F32)
    points = pix.astype(F32).reshape(n_vars, n_pix, tok)
    merged = []
    for h in range(n_heads):
        head = weights[:, h, :]
        mixed = (head[:, None, :] * points).reshape(n_rows, tok).astype(BF16)
        own = slice(h * HEAD_DIM, (h + 1) * HEAD_DIM)
        merged.append(dot(values[own], mixed) + dot(offset_values[own], head.astype(BF16)))
    merged = jnp.transpose(jnp.concatenate(merged, axis=0))
    return merged + position.astype(F32)


def project(merged, weight, qkv_out):
    centre = jnp.mean(merged, axis=-1, keepdims=True)
    centred = merged - centre
    spread = jnp.mean(jnp.square(centred), axis=-1, keepdims=True)
    normed = (centred * lax.rsqrt(spread + EPSILON)).astype(BF16)
    for c in range(3):
        qkv_out[c] = dot(normed, weight[c]).astype(BF16)


def tokens_of(pix_refs, distance, tok):
    n = len(pix_refs)
    me = lax.axis_index("var")
    start = pl.multiple_of(lax.rem(me + distance, n) * tok, tok)
    return jnp.concatenate([ref[:, pl.ds(start, tok)] for ref in pix_refs], axis=0)


def first_body(n, *refs):
    tables, offsets, pix, folded = refs[: n - 1], refs[n - 1 : 2 * n - 2], refs[2 * n - 2 : 3 * n - 2], refs[3 * n - 2 : 3 * n + 2]
    key_t, agg_value, position, weight = refs[3 * n + 2 : 3 * n + 6]
    values, offset_values, keys, offset_keys, merged_out, qkv_out = refs[3 * n + 6 :]
    parts = [tuple(ref[...] for ref in folded)]
    for table, offset in zip(tables, offsets):
        parts.append(fold(table[...], offset[...], key_t[...], agg_value[...]))
    for out, shares in zip((values, offset_values, keys, offset_keys), zip(*parts)):
        out[...] = jnp.concatenate(shares, axis=1)
    tok = position.shape[0]
    merged = front(
        tokens_of(pix, 0, tok), values[...], offset_values[...], keys[...], offset_keys[...], position[...]
    )
    merged_out[...] = merged
    project(merged, weight, qkv_out)


def later_body(n, distance, *refs):
    pix, (values, offset_values, keys, offset_keys, position, weight, qkv_out) = refs[:n], refs[n:]
    tok = position.shape[0]
    merged = front(
        tokens_of(pix, distance, tok), values[...], offset_values[...], keys[...], offset_keys[...], position[...]
    )
    project(merged, weight, qkv_out)


def attend(query, pairs):
    tok, width = query.shape
    group = min(width, 128)
    per = group // HEAD_DIM
    lanes = lax.broadcasted_iota(jnp.int32, (1, group), 1) // HEAD_DIM
    out = []
    for g in range(width // group):
        cut = slice(g * group, (g + 1) * group)
        block = query[:, cut]
        done = None
        for h in range(per):
            mine = jnp.where(lanes == h, block, jnp.zeros_like(block))
            numer, denom = 0.0, 0.0
            for pair in pairs:
                expos = jnp.exp(dot(mine, pair[0, :, cut], NT))
                denom = denom + jnp.sum(expos, axis=-1, keepdims=True)
                numer = numer + dot(expos.astype(BF16), pair[1, :, cut])
            head = numer / denom
            done = head if done is None else jnp.where(lanes == h, head, done)
        out.append(done.astype(BF16))
    return jnp.concatenate(out, axis=1)


def attend_body(*refs):
    qkv, pairs, out_weight, out = refs[0], refs[1:-2], refs[-2], refs[-1]
    scale = HEAD_DIM ** (-0.5)
    query = qkv[0] * jnp.asarray(scale, BF16)
    context = attend(query, pairs)
    out[...] = dot(context, out_weight[...]).astype(out.dtype)


def shards(pixels, embed_weight, variable_embed, agg_key, agg_value, position, qkv_weight, out_weight):
    n = lax.axis_size("var")
    n_vars, n_pix, band_tok = pixels.shape
    d = embed_weight.shape[2]
    tok = position.shape[0]
    width = qkv_weight.shape[2]
    n_heads = agg_key.shape[1]
    all_vars = n_vars * n
    rows = n_vars * n_pix
    table = embed_weight.reshape(rows, d)
    pix = pixels.reshape(rows, band_tok)
    key_t = jnp.transpose(agg_key)
    weight = jnp.transpose(qkv_weight, (1, 0, 2))

    tables = [shifted(table, "var", r) for r in range(1, n)]
    pixs = [pix] + [shifted(pix, "var", r) for r in range(1, n)]
    offsets = [shifted(variable_embed, "var", r) for r in range(1, n)]
    positions = [position] + [shifted(position, "var", r) for r in range(1, n)]

    sds = jax.ShapeDtypeStruct
    folded = call(
        fold_body,
        [sds((d, rows), BF16), sds((d, n_vars), BF16), sds((n_heads, rows), F32), sds((n_heads, n_vars), F32)],
        (table, variable_embed, key_t, agg_value),
        2 * (rows + n_vars) * d * (d + n_heads),
        "fold",
    )
    *weights, merged, own = call(
        functools.partial(first_body, n),
        [
            sds((d, rows * n), BF16),
            sds((d, all_vars), BF16),
            sds((n_heads, rows * n), F32),
            sds((n_heads, all_vars), F32),
            sds((tok, d), F32),
            sds((3, tok, width), BF16),
        ],
        (*tables, *offsets, *pixs, *folded, key_t, agg_value, position, weight),
        2 * (n - 1) * (rows + n_vars) * d * d + 2 * tok * d * (3 * width + 2 * rows),
        "front_own",
    )
    qkvs = [own]
    for r in range(1, n):
        qkvs += call(
            functools.partial(later_body, n, r),
            [sds((3, tok, width), BF16)],
            (*pixs, *weights, positions[r], weight),
            2 * tok * d * (3 * width + 2 * rows),
            "front_later",
        )
    pairs = [x[1:] for x in qkvs]
    pairs += [shifted(x, "band", 1) for x in pairs] + [shifted(x, "band", -1) for x in pairs[:n]]
    flops = 4 * tok * band_tok * 3 * width + 2 * tok * width * d
    update = None
    for r in range(1, n):
        (share,) = call(attend_body, [sds((tok, d), BF16)], (qkvs[r], *pairs, out_weight), flops, "attend")
        share = shifted(share, "var", n - r).astype(F32)
        update = share if update is None else update + share
    (share,) = call(attend_body, [sds((tok, d), F32)], (own, *pairs, out_weight), flops, "attend_own")
    update = share if update is None else update + share
    return (merged + update).astype(BF16)


def solution(mesh):
    in_specs = (
        P("var", None, "band"),
        P("var", None, None),
        P("var", None),
        P(),
        P(),
        P(("band", "var"), None),
        P(None, None, "var"),
        P("var", None),
    )
    out_specs = P(("band", "var"), None)
    return jax.shard_map(shards, mesh=mesh, in_specs=in_specs, out_specs=out_specs, check_vma=False)
```

time: 160 us -> 51.5 us (0.32)
  waiting for transfers between devices: 62.3 us -> 14.5 us
  matrix products: 26.7 us -> 0 us
  local copies, waits for them, and re-layouts: 33.7 us -> 7.74 us
  between operations: 13.5 us -> 0.1 us
  Pallas kernels: 0 us -> 12.1 us
  blocking collectives: 8.17 us -> 0 us
  starting transfers between devices: 7.9 us -> 15.8 us
  other arithmetic: 7.32 us -> 0.81 us
    all_to_all x1 -> x0, waiting for transfers between devices: 44.7 us -> none  [shards(): lax.all_to_all(local_embed, 'var', split_axis=1, concat_axis=0, tiled=True)]
    dot_general x12 -> x0, matrix products: 26.7 us -> none  [the longest x3 7.02 us: absorb(): jnp.einsum('thd,shd->hts', query_heads, key_heads, preferred_element_type...]
    reduce_scatter x1 -> x0, waiting for transfers between devices: 17.6 us -> none  [shards(): lax.psum_scatter(jnp.dot(context, out_weight, preferred_element_type=jnp....]
    slice x9 -> x2, local copies, waits for them, and re-layouts: 14.6 us -> 0.04 us  [shards(): pairs = [x[1:] for x in qkvs]]
    ppermute x2 -> x9, waiting for transfers between devices: 0.01 us -> 14.5 us  [shifted(): lax.ppermute(block, axis, [((i + distance) % n, i) for i in range(n)])]
    ppermute x2 -> x9, starting transfers between devices: 2.08 us -> 15.8 us  [shifted(): lax.ppermute(block, axis, [((i + distance) % n, i) for i in range(n)])]
    pallas_call x0 -> x5, Pallas kernels: none -> 12.1 us  [call(): pl.pallas_call(body, out_shape=outs, in_specs=[pl.BlockSpec(memory_space=...]
    all_gather x1 -> x0, blocking collectives: 8.17 us -> none  [shards(): lax.all_gather(normed, 'var', axis=0, tiled=True)]
  transfers between devices with their start and end apart: 4 -> 9, of which waited for: 2 -> 3; matrix products, arithmetic and copies ran while one was open for 12% -> 0% of each run, Pallas kernels for 0% -> 17%
where the time goes in v1:
time: 51.5 us; the launch traced here: 51.1 us
  starting transfers between devices  15.8 us (31%)
  waiting for transfers between devices  14.5 us (28%)
  Pallas kernels  12.1 us (23%)
  local copies, waits for them, and re-layouts  7.74 us (15%)
  other arithmetic  0.81 us (2%)
    ppermute x9, starting transfers between devices, shifted(): lax.ppermute(block, axis, [((i + distance) % n, i) for i in range(n)])  15.8 us
    ppermute x9, waiting for transfers between devices, shifted(): lax.ppermute(block, axis, [((i + distance) % n, i) for i in range(n)])  14.5 us
    pallas_call x5, Pallas kernels, call(): pl.pallas_call(body, out_shape=outs, in_specs=[pl.BlockSpec(memory_space=...  12.1 us
    unnamed x20, local copies, waits for them, and re-layouts  7.7 us
  transfers between devices with their start and end apart: 9, of which 3 were waited for; matrix products, arithmetic and copies ran while one was open for 0% of the time, Pallas kernels for 17%

profile of v1, /device:TPU:0, one launch (start us, length us, event | category | flops | bytes accessed | tf_op | source)
XLA Modules:
  0.0 51.1 jit_solution(12856997013265814845)
XLA Ops:
  0.0 3.0 %collective-permute-start = (bf16[128,1024]{1,0:T(8,128)(2,1)}, bf16[128,1024]{1,0:T(8,128)(2,1)S(1)}, u32[]{:S(2)}, u32[]{:S(2)}) collective-permute-start(bf16[128,1024]{1,0:T(8,128)(2,1)} %bitcast.9), channel_id=1, source_target_pairs={{1,0},{0,1},{3,2},{2,3},{5,4},{4,5},{7,6},{6,7},{9,8},{8,9},{11,10... | collective-permute-start | bytes 786440 | tf_op jit(solution)/shard_map/ppermute | solution.py:24
  3.0 2.0 %collective-permute-start.2 = (bf16[128,256]{1,0:T(8,128)(2,1)}, bf16[128,256]{1,0:T(8,128)(2,1)S(1)}, u32[]{:S(2)}, u32[]{:S(2)}) collective-permute-start(bf16[128,256]{1,0:T(8,128)(2,1)} %bitcast.6), channel_id=1, source_target_pairs={{1,0},{0,1},{3,2},{2,3},{5,4},{4,5},{7,6},{6,7},{9,8},{8,9},{11,10... | collective-permute-start | bytes 196616 | tf_op jit(solution)/shard_map/ppermute | solution.py:24
  5.0 0.0 collective-permute-start.1
  5.0 1.6 %copy-done.2 = bf16[1024,1024]{1,0:T(8,128)(2,1)S(1)} copy-done((bf16[1024,1024]{1,0:T(8,128)(2,1)S(1)}, bf16[1024,1024]{1,0:T(8,128)(2,1)}, u32[]{:S(2)}) %copy-start.2) | copy-done | bytes 2097176
  6.6 0.9 %copy-done.6 = bf16[8,16,1024]{2,1,0:T(8,128)(2,1)S(1)} copy-done((bf16[8,16,1024]{2,1,0:T(8,128)(2,1)S(1)}, bf16[8,16,1024]{2,1,0:T(8,128)(2,1)}, u32[]{:S(2)}) %copy-start.6) | copy-done | bytes 262168
  7.6 0.8 %copy-done.8 = bf16[1024,16]{0,1:T(8,128)(2,1)S(1)} copy-done((bf16[1024,16]{0,1:T(8,128)(2,1)S(1)}, bf16[1024,16]{0,1:T(8,128)(2,1)}, u32[]{:S(2)}) %copy-start.8) | copy-done | bytes 32792
  8.3 0.7 %copy-done.9 = bf16[8,1024]{1,0:T(8,128)(2,1)S(1)} copy-done((bf16[8,1024]{1,0:T(8,128)(2,1)S(1)}, bf16[8,1024]{1,0:T(8,128)(2,1)}, u32[]{:S(2)}) %copy-start.9) | copy-done | bytes 16408
  9.1 0.9 %fold.1 = (bf16[1024,128]{1,0:T(8,128)(2,1)S(1)}, bf16[1024,8]{1,0:T(8,128)(2,1)S(1)}, f32[16,128]{1,0:T(8,128)S(1)}, f32[16,8]{1,0:T(8,128)S(1)}) custom-call(bf16[128,1024]{1,0:T(8,128)(2,1)S(1)} %bitcast.10, bf16[8,1024]{1,0:T(8,128)(2,1)S(1)} %copy-done.9, bf16[16,1024]{1,0:T(8,128)(2,1)S(1)} %bitcast.11, bf16[1024,1024]{1,0:T(8,128)(2,1)S(1)} %copy-done.2), custom_call_target="tpu_custom_call" | custom-call | flops 289669120 | bytes 2695680 | tf_op jit(solution)/shard_map/fold/pallas_call | solution.py:29
  9.9 6.9 %collective-permute-done.1.refs_1_ = bf16[8,1024]{1,0:T(8,128)(2,1)S(1)} collective-permute-done((bf16[8,1024]{1,0:T(8,128)(2,1)}, bf16[8,1024]{1,0:T(8,128)(2,1)S(1)}, u32[]{:S(2)}, u32[]{:S(2)}) %collective-permute-start.1) | collective-permute-done | bytes 16416 | tf_op jit(solution)/shard_map/ppermute | solution.py:24
  16.9 1.9 %copy-done = bf16[1024,3,512]{2,0,1:T(8,128)(2,1)S(1)} copy-done((bf16[1024,3,512]{2,0,1:T(8,128)(2,1)S(1)}, bf16[1024,3,512]{2,0,1:T(8,128)(2,1)}, u32[]{:S(2)}) %copy-start) | copy-done | bytes 3145752
  18.8 0.8 %copy-done.5 = bf16[8,16,256]{2,1,0:T(8,128)(2,1)S(1)} copy-done((bf16[8,16,256]{2,1,0:T(8,128)(2,1)S(1)}, bf16[8,16,256]{2,1,0:T(8,128)(2,1)}, u32[]{:S(2)}) %copy-start.5) | copy-done | bytes 65560
  19.6 0.9 %copy-done.7 = bf16[128,1024]{1,0:T(8,128)(2,1)S(1)} copy-done((bf16[128,1024]{1,0:T(8,128)(2,1)S(1)}, bf16[128,1024]{1,0:T(8,128)(2,1)}, u32[]{:S(2)}) %copy-start.7) | copy-done | bytes 262168
  20.6 2.4 %front_own.1 = (bf16[1024,256]{1,0:T(8,128)(2,1)S(1)}, bf16[1024,16]{1,0:T(8,128)(2,1)S(1)}, f32[16,256]{1,0:T(8,128)S(1)}, f32[16,16]{1,0:T(8,128)S(1)}, f32[12...) custom-call(bf16[128,1024]{1,0:T(8,128)(2,1)S(1)} %collective-permute-done.refs_0_, ...), custom_call_target="tpu_custom_call" | custom-call | flops 754974720 | bytes 7726592 | tf_op jit(solution)/shard_map/front_own/pallas_call | solution.py:29
  23.0 0.1 collective-permute-start.6
  23.1 4.4 %collective-permute-start.4 = (bf16[2,128,512]{2,1,0:T(8,128)(2,1)S(1)}, bf16[2,128,512]{2,1,0:T(8,128)(2,1)S(1)}, u32[]{:S(2)}, u32[]{:S(2)}) collective-permute-start(bf16[2,128,512]{2,1,0:T(8,128)(2,1)S(1)} %slice.6.refs_1_), channel_id=1, source_target_pairs={{2,0},{4,2},{6,4},{8,6},{10,8},{12,10},{14,12},{16,14},{18,16},{20... | collective-permute-start | bytes 786440 | tf_op jit(solution)/shard_map/ppermute | solution.py:24
  27.5 1.5 %front_later.1.refs_0_ = bf16[3,128,512]{2,1,0:T(8,128)(2,1)S(1)} custom-call(bf16[128,256]{1,0:T(8,128)(2,1)S(1)} %bitcast.8, bf16[128,256]{1,0:T(8,128)(2,1)S(1)} %collective-permute-done.2.refs_3_.refs_1_, bf16[1024,256]{1,0:T(8,128)(2,1)S(1)} %get-tuple-element.20.refs_2_, bf16[1024,16]{1,0:T(8,128)(2,1)S(1)} %get-tuple-element.21.refs_3_, ...), custom_call_target="tpu_custom_call" | custom-call | flops 469762048 | bytes 4506624 | tf_op jit(solution)/shard_map/front_later/pallas_call | solution.py:29
  29.0 0.1 collective-permute-start.7
  29.1 4.4 %collective-permute-start.5 = (bf16[2,128,512]{2,1,0:T(8,128)(2,1)S(1)}, bf16[2,128,512]{2,1,0:T(8,128)(2,1)S(1)}, u32[]{:S(2)}, u32[]{:S(2)}) collective-permute-start(bf16[2,128,512]{2,1,0:T(8,128)(2,1)S(1)} %slice.8.refs_2_), channel_id=1, source_target_pairs={{2,0},{4,2},{6,4},{8,6},{10,8},{12,10},{14,12},{16,14},{18,16},{20... | collective-permute-start | bytes 786440 | tf_op jit(solution)/shard_map/ppermute | solution.py:24
  33.5 4.2 %collective-permute-done.7.refs_6_ = bf16[2,128,512]{2,1,0:T(8,128)(2,1)S(1)} collective-permute-done((bf16[2,128,512]{2,1,0:T(8,128)(2,1)S(1)}, bf16[2,128,512]{2,1,0:T(8,128)(2,1)S(1)}, u32[]{:S(2)}, u32[]{:S(2)}) %collective-permute-start.7) | collective-permute-done | bytes 262176 | tf_op jit(solution)/shard_map/ppermute | solution.py:24
  37.7 3.7 %attend.1 = bf16[128,1024]{1,0:T(8,128)(2,1)S(1)} custom-call(bf16[3,128,512]{2,1,0:T(8,128)(2,1)S(1)} %front_later.1.refs_0_, bf16[2,128,512]{2,1,0:T(8,128)(2,1)S(1)} %slice.6.refs_1_, bf16[2,128,512]{2,1,0:T(8,128)(2,1)S(1)} %slice.8.refs_2_, bf16[2,128,512]{2,1,0:T(8,128)(2,1)S(1)} %collective-permute-done.4.refs_3_, ...), custom_call_target="tpu_custom_call" | custom-call | flops 335544320 | bytes 3276800 | tf_op jit(solution)/shard_map/attend/pallas_call | solution.py:29
  41.4 1.8 %collective-permute-start.8 = (bf16[128,1024]{1,0:T(8,128)(2,1)S(1)}, bf16[128,1024]{1,0:T(8,128)(2,1)S(1)}, u32[]{:S(2)}, u32[]{:S(2)}) collective-permute-start(bf16[128,1024]{1,0:T(8,128)(2,1)S(1)} %attend.1), channel_id=1, source_target_pairs={{1,0},{0,1},{3,2},{2,3},{5,4},{4,5},{7,6},{6,7},{9,8},{8,9},{11,10... | collective-permute-start | bytes 786440 | tf_op jit(solution)/shard_map/ppermute | solution.py:24
  43.2 3.7 %attend_own.1 = f32[128,1024]{1,0:T(8,128)S(1)} custom-call(bf16[3,128,512]{2,1,0:T(8,128)(2,1)S(1)} %get-tuple-element.24.refs_0_, bf16[2,128,512]{2,1,0:T(8,128)(2,1)S(1)} %slice.6.refs_1_, bf16[2,128,512]{2,1,0:T(8,128)(2,1)S(1)} %slice.8.refs_2_, bf16[2,128,512]{2,1,0:T(8,128)(2,1)S(1)} %collective-permute-done.4.refs_3_, ...), custom_call_target="tpu_custom_call" | custom-call | flops 335544320 | bytes 3538944 | tf_op jit(solution)/shard_map/attend_own/pallas_call | solution.py:29
  46.8 3.4 %collective-permute-done.8 = bf16[128,1024]{1,0:T(8,128)(2,1)S(1)} collective-permute-done((bf16[128,1024]{1,0:T(8,128)(2,1)S(1)}, bf16[128,1024]{1,0:T(8,128)(2,1)S(1)}, u32[]{:S(2)}, u32[]{:S(2)}) %collective-permute-start.8) | collective-permute-done | bytes 262176 | tf_op jit(solution)/shard_map/ppermute | solution.py:24
  50.2 0.8 %add_convert_fusion = bf16[128,1024]{1,0:T(8,128)(2,1)} fusion(f32[128,1024]{1,0:T(8,128)S(1)} %get-tuple-element.19, f32[128,1024]{1,0:T(8,128)S(1)} %attend_own.1, bf16[128,1024]{1,0:T(8,128)(2,1)S(1)} %collective-permute-done.8), kind=kLoop, calls=%fused_computation | loop fusion | flops 524288 | bytes 1572864 | tf_op jit(solution)/shard_map/convert_element_type | solution.py:213
  (22 shorter events, 0.1 us)
Async XLA Ops:
  0.0 16.9 %collective-permute-start = (bf16[128,1024]{1,0:T(8,128)(2,1)}, bf16[128,1024]{1,0:T(8,128)(2,1)S(1)}, u32[]{:S(2)}, u32[]{:S(2)}) collective-permute-start(bf16[128,1024]{1,0:T(8,128)(2,1)} %bitcast.9), channel_id=1, source_target_pairs={{1,0},{0,1},{3,2},{2,3},{5,4},{4,5},{7,6},{6,7},{9,8},{8,9},{11,10... | collective-permute-start | bytes 786440 | tf_op jit(solution)/shard_map/ppermute | solution.py:24
  3.0 24.5 %collective-permute-start.3 = (bf16[128,1024]{1,0:T(8,128)(2,1)}, bf16[128,1024]{1,0:T(8,128)(2,1)S(1)}, u32[]{:S(2)}, u32[]{:S(2)}) collective-permute-start(bf16[128,1024]{1,0:T(8,128)(2,1)} %refs_10_.1), channel_id=1, source_target_pairs={{1,0},{0,1},{3,2},{2,3},{5,4},{4,5},{7,6},{6,7},{9,8},{8,9},{11,10... | collective-permute-start | bytes 786440 | tf_op jit(solution)/shard_map/ppermute | solution.py:24
  3.0 13.9 %collective-permute-start.2 = (bf16[128,256]{1,0:T(8,128)(2,1)}, bf16[128,256]{1,0:T(8,128)(2,1)S(1)}, u32[]{:S(2)}, u32[]{:S(2)}) collective-permute-start(bf16[128,256]{1,0:T(8,128)(2,1)} %bitcast.6), channel_id=1, source_target_pairs={{1,0},{0,1},{3,2},{2,3},{5,4},{4,5},{7,6},{6,7},{9,8},{8,9},{11,10... | collective-permute-start | bytes 196616 | tf_op jit(solution)/shard_map/ppermute | solution.py:24
  5.0 11.9 %collective-permute-start.1 = (bf16[8,1024]{1,0:T(8,128)(2,1)}, bf16[8,1024]{1,0:T(8,128)(2,1)S(1)}, u32[]{:S(2)}, u32[]{:S(2)}) collective-permute-start(bf16[8,1024]{1,0:T(8,128)(2,1)} %offsets.1), channel_id=1, source_target_pairs={{1,0},{0,1},{3,2},{2,3},{5,4},{4,5},{7,6},{6,7},{9,8},{8,9},{11,10... | collective-permute-start | bytes 49160 | tf_op jit(solution)/shard_map/ppermute | solution.py:24
  5.0 1.6 %copy-start.2 = (bf16[1024,1024]{1,0:T(8,128)(2,1)S(1)}, bf16[1024,1024]{1,0:T(8,128)(2,1)}, u32[]{:S(2)}) copy-start(bf16[1024,1024]{1,0:T(8,128)(2,1)} %refs_9_.1) | copy-start | bytes 6291460
  6.6 0.9 %copy-start.6 = (bf16[8,16,1024]{2,1,0:T(8,128)(2,1)S(1)}, bf16[8,16,1024]{2,1,0:T(8,128)(2,1)}, u32[]{:S(2)}) copy-start(bf16[8,16,1024]{2,1,0:T(8,128)(2,1)} %param.9) | copy-start | bytes 786436
  7.6 0.8 %copy-start.8 = (bf16[1024,16]{0,1:T(8,128)(2,1)S(1)}, bf16[1024,16]{0,1:T(8,128)(2,1)}, u32[]{:S(2)}) copy-start(bf16[1024,16]{0,1:T(8,128)(2,1)} %param.11) | copy-start | bytes 98308
  8.3 0.7 %copy-start.9 = (bf16[8,1024]{1,0:T(8,128)(2,1)S(1)}, bf16[8,1024]{1,0:T(8,128)(2,1)}, u32[]{:S(2)}) copy-start(bf16[8,1024]{1,0:T(8,128)(2,1)} %offsets.1) | copy-start | bytes 49156
  9.1 7.8 %copy-start.3 = (bf16[1024,1024]{1,0:T(8,128)(2,1)S(1)}, bf16[1024,1024]{1,0:T(8,128)(2,1)}, u32[]{:S(2)}) copy-start(bf16[1024,1024]{1,0:T(8,128)(2,1)} %refs_9_.1) | copy-start | bytes 6291460
  16.9 1.9 %copy-start = (bf16[1024,3,512]{2,0,1:T(8,128)(2,1)S(1)}, bf16[1024,3,512]{2,0,1:T(8,128)(2,1)}, u32[]{:S(2)}) copy-start(bf16[1024,3,512]{2,0,1:T(8,128)(2,1)} %param.14) | copy-start | bytes 9437188
  18.8 0.8 %copy-start.5 = (bf16[8,16,256]{2,1,0:T(8,128)(2,1)S(1)}, bf16[8,16,256]{2,1,0:T(8,128)(2,1)}, u32[]{:S(2)}) copy-start(bf16[8,16,256]{2,1,0:T(8,128)(2,1)} %param.8) | copy-start | bytes 196612
  19.6 0.9 %copy-start.7 = (bf16[128,1024]{1,0:T(8,128)(2,1)S(1)}, bf16[128,1024]{1,0:T(8,128)(2,1)}, u32[]{:S(2)}) copy-start(bf16[128,1024]{1,0:T(8,128)(2,1)} %refs_10_.1) | copy-start | bytes 786436
  20.6 7.0 %copy-start.1 = (bf16[1024,3,512]{2,0,1:T(8,128)(2,1)S(1)}, bf16[1024,3,512]{2,0,1:T(8,128)(2,1)}, u32[]{:S(2)}) copy-start(bf16[1024,3,512]{2,0,1:T(8,128)(2,1)} %param.14) | copy-start | bytes 9437188
  23.0 14.7 %copy-start.4 = (bf16[512,1024]{1,0:T(8,128)(2,1)S(1)}, bf16[512,1024]{1,0:T(8,128)(2,1)}, u32[]{:S(2)}) copy-start(bf16[512,1024]{1,0:T(8,128)(2,1)} %refs_7_.3) | copy-start | bytes 3145732
  23.0 10.5 %collective-permute-start.6 = (bf16[2,128,512]{2,1,0:T(8,128)(2,1)S(1)}, bf16[2,128,512]{2,1,0:T(8,128)(2,1)S(1)}, u32[]{:S(2)}, u32[]{:S(2)}) collective-permute-start(bf16[2,128,512]{2,1,0:T(8,128)(2,1)S(1)} %slice.6.refs_1_), channel_id=1, source_target_pairs={{30,0},{0,2},{2,4},{4,6},{6,8},{8,10},{10,12},{12,14},{14,16},{16,... | collective-permute-start | bytes 786440 | tf_op jit(solution)/shard_map/ppermute | solution.py:24
  23.1 10.5 %collective-permute-start.4 = (bf16[2,128,512]{2,1,0:T(8,128)(2,1)S(1)}, bf16[2,128,512]{2,1,0:T(8,128)(2,1)S(1)}, u32[]{:S(2)}, u32[]{:S(2)}) collective-permute-start(bf16[2,128,512]{2,1,0:T(8,128)(2,1)S(1)} %slice.6.refs_1_), channel_id=1, source_target_pairs={{2,0},{4,2},{6,4},{8,6},{10,8},{12,10},{14,12},{16,14},{18,16},{20... | collective-permute-start | bytes 786440 | tf_op jit(solution)/shard_map/ppermute | solution.py:24
  29.0 8.7 %collective-permute-start.7 = (bf16[2,128,512]{2,1,0:T(8,128)(2,1)S(1)}, bf16[2,128,512]{2,1,0:T(8,128)(2,1)S(1)}, u32[]{:S(2)}, u32[]{:S(2)}) collective-permute-start(bf16[2,128,512]{2,1,0:T(8,128)(2,1)S(1)} %slice.8.refs_2_), channel_id=1, source_target_pairs={{30,0},{0,2},{2,4},{4,6},{6,8},{8,10},{10,12},{12,14},{14,16},{16,... | collective-permute-start | bytes 786440 | tf_op jit(solution)/shard_map/ppermute | solution.py:24
  29.1 8.6 %collective-permute-start.5 = (bf16[2,128,512]{2,1,0:T(8,128)(2,1)S(1)}, bf16[2,128,512]{2,1,0:T(8,128)(2,1)S(1)}, u32[]{:S(2)}, u32[]{:S(2)}) collective-permute-start(bf16[2,128,512]{2,1,0:T(8,128)(2,1)S(1)} %slice.8.refs_2_), channel_id=1, source_target_pairs={{2,0},{4,2},{6,4},{8,6},{10,8},{12,10},{14,12},{16,14},{18,16},{20... | collective-permute-start | bytes 786440 | tf_op jit(solution)/shard_map/ppermute | solution.py:24
  41.4 8.9 %collective-permute-start.8 = (bf16[128,1024]{1,0:T(8,128)(2,1)S(1)}, bf16[128,1024]{1,0:T(8,128)(2,1)S(1)}, u32[]{:S(2)}, u32[]{:S(2)}) collective-permute-start(bf16[128,1024]{1,0:T(8,128)(2,1)S(1)} %attend.1), channel_id=1, source_target_pairs={{1,0},{0,1},{3,2},{2,3},{5,4},{4,5},{7,6},{6,7},{9,8},{8,9},{11,10... | collective-permute-start | bytes 786440 | tf_op jit(solution)/shard_map/ppermute | solution.py:24

commit v2 on v1

v2 whole, which is shorter than its diff:
```python
import functools

import jax
import jax.numpy as jnp
from jax import lax
from jax.experimental import pallas as pl
from jax.experimental.pallas import tpu as pltpu
from jax.sharding import PartitionSpec as P

HEAD_DIM = 64
EPSILON = 1e-05
F32 = jnp.float32
BF16 = jnp.bfloat16
NT = (((1,), (1,)), ((), ()))
NN = (((1,), (0,)), ((), ()))


def dot(a, b, dims=NN):
    return lax.dot_general(a, b, dims, preferred_element_type=F32)


def shifted(block, axis, distance):
    n = lax.axis_size(axis)
    return lax.ppermute(block, axis, [((i + distance) % n, i) for i in range(n)])


def paired(block):
    return lax.ppermute(block, "band", [(i ^ 1, i) for i in range(lax.axis_size("band"))])


def call(body, outs, args, flops, name, spaces=None, scratch=()):
    nbytes = sum(a.size * a.dtype.itemsize for a in (*args, *outs))
    spaces = spaces or [pltpu.VMEM] * len(args)
    return pl.pallas_call(
        body,
        out_shape=outs,
        in_specs=[pl.BlockSpec(memory_space=space) for space in spaces],
        out_specs=[pl.BlockSpec(memory_space=pltpu.VMEM) for _ in outs],
        scratch_shapes=scratch,
        compiler_params=pltpu.CompilerParams(vmem_limit_bytes=32 * 1024 * 1024),
        cost_estimate=pl.CostEstimate(flops=flops, bytes_accessed=nbytes, transcendentals=0),
        name=name,
    )(*args)


def fold(table, offsets, key_t, agg_value):
    values = jnp.transpose(dot(table, agg_value)).astype(BF16)
    offset_values = jnp.transpose(dot(offsets, agg_value)).astype(BF16)
    return values, offset_values, dot(key_t, table, NT), dot(key_t, offsets, NT)


def stage_body(n_in, *refs):
    sources, staged, folded, sems = refs[:n_in], refs[n_in : 2 * n_in], refs[2 * n_in : -1], refs[-1]
    copies = [pltpu.make_async_copy(a, b, sems.at[i]) for i, (a, b) in enumerate(zip(sources, staged))]
    for copy in copies:
        copy.start()
    for copy in copies[:4]:
        copy.wait()
    for out, part in zip(folded, fold(*(ref[...] for ref in staged[:4]))):
        out[...] = part
    for copy in copies[4:]:
        copy.wait()


def front(pix, values, offset_values, keys, offset_keys, position):
    n_heads, n_rows = keys.shape
    n_vars = offset_keys.shape[1]
    n_pix = n_rows // n_vars
    tok = pix.shape[1]
    rows = lax.broadcasted_iota(jnp.int32, (n_vars * n_heads, n_rows), 0) // n_heads
    cols = lax.broadcasted_iota(jnp.int32, (n_vars * n_heads, n_rows), 1) // n_pix
    spread = jnp.where(rows == cols, jnp.concatenate([keys] * n_vars, axis=0), 0.0)
    high = spread.astype(BF16)
    low = (spread - high.astype(F32)).astype(BF16)
    rows = lax.broadcasted_iota(jnp.int32, (n_vars * n_heads, n_vars), 0) // n_heads
    cols = lax.broadcasted_iota(jnp.int32, (n_vars * n_heads, n_vars), 1)
    base = jnp.sum(
        jnp.where(rows == cols, jnp.concatenate([offset_keys] * n_vars, axis=0), 0.0), axis=1, keepdims=True
    )
    scores = dot(high, pix) + dot(low, pix) + base
    expos = jnp.exp(scores).reshape(n_vars, n_heads, tok)
    weights = (expos / jnp.sum(expos, axis=0, keepdims=True)).astype(BF16).astype(F32)
    points = pix.astype(F32).reshape(n_vars, n_pix, tok)
    merged = []
    for h in range(n_heads):
        head = weights[:, h, :]
        mixed = (head[:, None, :] * points).reshape(n_rows, tok).astype(BF16)
        own = slice(h * HEAD_DIM, (h + 1) * HEAD_DIM)
        merged.append(dot(values[own], mixed) + dot(offset_values[own], head.astype(BF16)))
    merged = jnp.transpose(jnp.concatenate(merged, axis=0))
    return merged + position.astype(F32)


def project(merged, weight, query_out, pair_out):
    centre = jnp.mean(merged, axis=-1, keepdims=True)
    centred = merged - centre
    spread = jnp.mean(jnp.square(centred), axis=-1, keepdims=True)
    normed = (centred * lax.rsqrt(spread + EPSILON)).astype(BF16)
    query_out[...] = (dot(normed, weight[0]).astype(BF16) * HEAD_DIM ** (-0.5)).astype(BF16)
    for c in range(2):
        pair_out[c] = dot(normed, weight[c + 1]).astype(BF16)


def tokens_of(pix_refs, distance, tok):
    n = len(pix_refs)
    me = lax.axis_index("var")
    start = pl.multiple_of(lax.rem(me + distance, n) * tok, tok)
    return jnp.concatenate([ref[:, pl.ds(start, tok)] for ref in pix_refs], axis=0)


def first_body(n, *refs):
    near, far, pix, folded = (refs[i : i + k] for i, k in ((0, n - 1), (n - 1, n - 1), (2 * n - 2, n), (3 * n - 2, 4)))
    key_t, agg_value, position, weight = refs[3 * n + 2 : 3 * n + 6]
    values, offset_values, keys, offset_keys, merged_out, query_out, pair_out, table = refs[3 * n + 6 :]
    half = table.shape[0] // 2
    side = lax.rem(lax.axis_index("band"), 2)
    parts = [tuple(ref[...] for ref in folded)]
    for mine, other in zip(near, far):
        table[pl.ds(pl.multiple_of(side * half, half), half)] = mine[:half]
        table[pl.ds(pl.multiple_of((1 - side) * half, half), half)] = other[:half]
        parts.append(fold(table[...], mine[half:], key_t[...], agg_value[...]))
    for out, shares in zip((values, offset_values, keys, offset_keys), zip(*parts)):
        out[...] = jnp.concatenate(shares, axis=1)
    tok = position.shape[0]
    merged = front(
        tokens_of(pix, 0, tok), values[...], offset_values[...], keys[...], offset_keys[...], position[...]
    )
    merged_out[...] = merged
    project(merged, weight, query_out, pair_out)


def later_body(n, distance, *refs):
    pix, (values, offset_values, keys, offset_keys, position, weight), rest = refs[:n], refs[n : n + 6], refs[n + 6 :]
    earlier, query_out, pair_out = rest[:-2], rest[-2], rest[-1]
    tok = position.shape[0]
    merged = front(
        tokens_of(pix, distance, tok), values[...], offset_values[...], keys[...], offset_keys[...], position[...]
    )
    for i, pair in enumerate(earlier):
        pair_out[:, i * tok : (i + 1) * tok] = pair[...]
    project(merged, weight, query_out, pair_out.at[:, pl.ds(len(earlier) * tok, tok)])


def absorb(query, pairs):
    tok, width = query.shape
    group = min(width, 128)
    per = group // HEAD_DIM
    lanes = lax.broadcasted_iota(jnp.int32, (1, group), 1) // HEAD_DIM
    numers, denoms = [], []
    for g in range(width // group):
        cut = slice(g * group, (g + 1) * group)
        block = query[:, cut]
        stack = jnp.concatenate([jnp.where(lanes == h, block, jnp.zeros_like(block)) for h in range(per)], axis=0)
        numer, denom = 0.0, 0.0
        for pair in pairs:
            expos = jnp.exp(dot(stack, pair[0, :, cut], NT))
            denom = denom + jnp.sum(expos, axis=-1, keepdims=True)
            numer = numer + dot(expos.astype(BF16), pair[1, :, cut])
        denom = jnp.broadcast_to(denom, numer.shape)
        top, low = numer[:tok], denom[:tok]
        for h in range(1, per):
            top = jnp.where(lanes == h, numer[h * tok : (h + 1) * tok], top)
            low = jnp.where(lanes == h, denom[h * tok : (h + 1) * tok], low)
        numers.append(top)
        denoms.append(low)
    return jnp.concatenate(numers, axis=1), jnp.concatenate(denoms, axis=1)


def begin_body(n, *refs):
    queries, pair, totals = refs[:n], refs[n], refs[n + 1 :]
    for i, query in enumerate(queries):
        totals[2 * i][...], totals[2 * i + 1][...] = absorb(query[...], [pair])


def finish_body(query, numer, denom, east, west, out_weight, *refs):
    top, low = absorb(query[...], [east, west])
    context = ((numer[...] + top) / (denom[...] + low)).astype(BF16)
    update = dot(context, out_weight[...])
    out = refs[-1]
    for ref in refs[:-1]:
        update = update + ref[...]
    out[...] = update.astype(out.dtype)


def shards(pixels, embed_weight, variable_embed, agg_key, agg_value, position, qkv_weight, out_weight):
    n = lax.axis_size("var")
    n_vars, n_pix, band_tok = pixels.shape
    d = embed_weight.shape[2]
    tok = position.shape[0]
    width = qkv_weight.shape[2]
    n_heads = agg_key.shape[1]
    all_vars = n_vars * n
    rows = n_vars * n_pix
    sds = jax.ShapeDtypeStruct
    table = embed_weight.reshape(rows, d)
    pix = pixels.reshape(rows, band_tok)
    key_t = jnp.transpose(agg_key)
    weight = jnp.transpose(qkv_weight, (1, 0, 2))

    pixs = [shifted(pix, "var", r) for r in range(1, n)]
    side = lax.rem(lax.axis_index("band"), 2)
    half = jnp.concatenate([lax.dynamic_slice_in_dim(table, side * (rows // 2), rows // 2, 0), variable_embed], axis=0)
    near = [shifted(half, "var", r) for r in range(1, n)]
    positions = [shifted(position, "var", r) for r in range(1, n)]
    far = [paired(x) for x in near]

    moved = (table, variable_embed, key_t, agg_value, pix, position, weight, out_weight)
    *staged, f0, f1, f2, f3 = call(
        functools.partial(stage_body, len(moved)),
        [sds(a.shape, a.dtype) for a in moved]
        + [sds((d, rows), BF16), sds((d, n_vars), BF16), sds((n_heads, rows), F32), sds((n_heads, n_vars), F32)],
        moved,
        2 * (rows + n_vars) * d * (d + n_heads),
        "stage",
        [pl.ANY] * len(moved),
        [pltpu.SemaphoreType.DMA((len(moved),))],
    )
    _, _, key_t, agg_value, pix, position, weight, out_weight = staged
    pixs = [pix] + pixs
    front_flops = 2 * tok * d * (3 * width + 2 * rows)
    *folded, merged, query, pair = call(
        functools.partial(first_body, n),
        [
            sds((d, rows * n), BF16),
            sds((d, all_vars), BF16),
            sds((n_heads, rows * n), F32),
            sds((n_heads, all_vars), F32),
            sds((tok, d), F32),
            sds((tok, width), BF16),
            sds((2, tok, width), BF16),
        ],
        (*near, *far, *pixs, f0, f1, f2, f3, key_t, agg_value, position, weight),
        2 * (n - 1) * (rows + n_vars) * d * d + front_flops,
        "front_own",
        scratch=[pltpu.VMEM((rows, d), BF16)],
    )
    queries, pairs = [query], [pair]
    for r in range(1, n):
        last = r == n - 1
        query, pair = call(
            functools.partial(later_body, n, r),
            [sds((tok, width), BF16), sds((2, band_tok if last else tok, width), BF16)],
            (*pixs, *folded, positions[r - 1], weight, *(pairs if last else ())),
            front_flops,
            "front_later",
        )
        queries.append(query)
        pairs.append(pair)
    pair = pairs[-1]
    east, west = shifted(pair, "band", 1), shifted(pair, "band", -1)
    flops = 4 * tok * band_tok * width
    totals = call(
        functools.partial(begin_body, n),
        [sds((tok, width), F32)] * (2 * n),
        (*queries, pair),
        n * flops,
        "attend_band",
    )
    flops = 2 * flops + 2 * tok * width * d
    ending = []
    for r in range(1, n):
        (share,) = call(
            finish_body,
            [sds((tok, d), BF16)],
            (queries[r], *totals[2 * r : 2 * r + 2], east, west, out_weight),
            flops,
            "attend_later",
        )
        ending.append(shifted(share, "var", n - r))
    (update,) = call(
        finish_body,
        [sds((tok, d), F32)],
        (queries[0], *totals[:2], east, west, out_weight, merged),
        flops,
        "attend_own",
    )
    for share in ending:
        update = update + share.astype(F32)
    return update.astype(BF16)


def solution(mesh):
    in_specs = (
        P("var", None, "band"),
        P("var", None, None),
        P("var", None),
        P(),
        P(),
        P(("band", "var"), None),
        P(None, None, "var"),
        P("var", None),
    )
    out_specs = P(("band", "var"), None)
    return jax.shard_map(shards, mesh=mesh, in_specs=in_specs, out_specs=out_specs, check_vma=False)
```

time: 51.5 us -> 51.3 us (level)
  starting transfers between devices: 15.8 us -> 10.2 us
  waiting for transfers between devices: 14.5 us -> 19.5 us
  Pallas kernels: 12.1 us -> 9.72 us
  local copies, waits for them, and re-layouts: 7.74 us -> 9.83 us
  other arithmetic: 0.81 us -> 1.49 us
    ppermute x9 -> x6, starting transfers between devices: 15.8 us -> 10.2 us  [shifted(): lax.ppermute(block, axis, [((i + distance) % n, i) for i in range(n)])]
    ppermute x9 -> x6, waiting for transfers between devices: 14.5 us -> 19.5 us  [shifted(): lax.ppermute(block, axis, [((i + distance) % n, i) for i in range(n)])]
    pallas_call x5 -> x6, Pallas kernels: 12.1 us -> 9.72 us  [call(): pl.pallas_call(body, out_shape=outs, in_specs=[pl.BlockSpec(memory_space=...]
    unnamed x20 -> x16, local copies, waits for them, and re-layouts: 7.7 us -> 8.92 us
    dynamic_slice x0 -> x1, local copies, waits for them, and re-layouts: none -> 0.91 us  [shards(): lax.dynamic_slice_in_dim(table, side * (rows // 2), rows // 2, 0)]
    concatenate x0 -> x1, other arithmetic: none -> 0.73 us  [shards(): jnp.concatenate([lax.dynamic_slice_in_dim(table, side * (rows // 2), rows...]
  transfers between devices with their start and end apart: 9 -> 7, of which waited for: 3 -> 4; matrix products, arithmetic and copies ran while one was open for 0% -> 0% of each run, Pallas kernels for 17% -> 14%
where the time goes in v2:
time: 51.3 us; the launch traced here: 50.8 us
  waiting for transfers between devices  19.5 us (38%)
  starting transfers between devices  10.2 us (20%)
  local copies, waits for them, and re-layouts  9.83 us (19%)
  Pallas kernels  9.72 us (19%)
  other arithmetic  1.49 us (3%)
    ppermute x6, waiting for transfers between devices, shifted(): lax.ppermute(block, axis, [((i + distance) % n, i) for i in range(n)])  19.5 us
    ppermute x6, starting transfers between devices, shifted(): lax.ppermute(block, axis, [((i + distance) % n, i) for i in range(n)])  10.2 us
    pallas_call x6, Pallas kernels, call(): pl.pallas_call(body, out_shape=outs, in_specs=[pl.BlockSpec(memory_space=...  9.72 us
    unnamed x16, local copies, waits for them, and re-layouts  8.92 us
  transfers between devices with their start and end apart: 7, of which 4 were waited for; matrix products, arithmetic and copies ran while one was open for 0% of the time, Pallas kernels for 14%

profile of v2, /device:TPU:0, one launch (start us, length us, event | category | flops | bytes accessed | tf_op | source)
XLA Modules:
  0.0 50.8 jit_solution(15575532691013758716)
XLA Ops:
  0.0 0.9 %constant_dynamic-slice_fusion = bf16[64,1024]{1,0:T(8,128)(2,1)S(1)} fusion(bf16[128,1024]{1,0:T(8,128)(2,1)} %bitcast.5, s32[]{:T(128)S(6)} %select_n.3), kind=kLoop, calls=%fused_computation.2 | loop fusion | bytes 262148 | tf_op jit(solution)/shard_map/dynamic_slice | solution.py:202
  0.9 0.7 %pad_maximum_fusion = bf16[72,1024]{1,0:T(8,128)(2,1)S(1)} fusion(bf16[8,1024]{1,0:T(8,128)(2,1)} %refs_1_.1, bf16[64,1024]{1,0:T(8,128)(2,1)S(1)} %constant_dynamic-slice_fusion), kind=kLoop, calls=%fused_computation.1 | loop fusion | flops 294912 | bytes 294912 | tf_op jit(solution)/shard_map/concatenate | solution.py:202
  1.6 3.0 %collective-permute-start = (bf16[72,1024]{1,0:T(8,128)(2,1)S(1)}, bf16[72,1024]{1,0:T(8,128)(2,1)S(1)}, u32[]{:S(2)}, u32[]{:S(2)}) collective-permute-start(bf16[72,1024]{1,0:T(8,128)(2,1)S(1)} %pad_maximum_fusion), channel_id=1, source_target_pairs={{1,0},{0,1},{3,2},{2,3},{5,4},{4,5},{7,6},{6,7},{9,8},{8,9},{11,10... | collective-permute-start | bytes 442376 | tf_op jit(solution)/shard_map/ppermute | solution.py:24
  4.8 4.6 %collective-permute-done.refs_0_ = bf16[72,1024]{1,0:T(8,128)(2,1)S(1)} collective-permute-done((bf16[72,1024]{1,0:T(8,128)(2,1)S(1)}, bf16[72,1024]{1,0:T(8,128)(2,1)S(1)}, u32[]{:S(2)}, u32[]{:S(2)}) %collective-permute-start) | collective-permute-done | bytes 147488 | tf_op jit(solution)/shard_map/ppermute | solution.py:24
  9.4 2.1 %collective-permute-start.2 = (bf16[128,256]{1,0:T(8,128)(2,1)}, bf16[128,256]{1,0:T(8,128)(2,1)S(1)}, u32[]{:S(2)}, u32[]{:S(2)}) collective-permute-start(bf16[128,256]{1,0:T(8,128)(2,1)} %bitcast.7), channel_id=1, source_target_pairs={{1,0},{0,1},{3,2},{2,3},{5,4},{4,5},{7,6},{6,7},{9,8},{8,9},{11,10... | collective-permute-start | bytes 196616 | tf_op jit(solution)/shard_map/ppermute | solution.py:24
  11.4 1.9 %copy-done = bf16[1024,3,512]{2,0,1:T(8,128)(2,1)S(1)} copy-done((bf16[1024,3,512]{2,0,1:T(8,128)(2,1)S(1)}, bf16[1024,3,512]{2,0,1:T(8,128)(2,1)}, u32[]{:S(2)}) %copy-start) | copy-done | bytes 3145752
  13.3 1.6 %copy-done.1 = bf16[1024,1024]{1,0:T(8,128)(2,1)S(1)} copy-done((bf16[1024,1024]{1,0:T(8,128)(2,1)S(1)}, bf16[1024,1024]{1,0:T(8,128)(2,1)}, u32[]{:S(2)}) %copy-start.1) | copy-done | bytes 2097176
  14.9 1.2 %copy-done.2 = bf16[512,1024]{1,0:T(8,128)(2,1)S(1)} copy-done((bf16[512,1024]{1,0:T(8,128)(2,1)S(1)}, bf16[512,1024]{1,0:T(8,128)(2,1)}, u32[]{:S(2)}) %copy-start.2) | copy-done | bytes 1048600
  16.1 0.9 %copy-done.3 = bf16[8,16,1024]{2,1,0:T(8,128)(2,1)S(1)} copy-done((bf16[8,16,1024]{2,1,0:T(8,128)(2,1)S(1)}, bf16[8,16,1024]{2,1,0:T(8,128)(2,1)}, u32[]{:S(2)}) %copy-start.3) | copy-done | bytes 262168
  17.1 0.9 %copy-done.4 = bf16[128,1024]{1,0:T(8,128)(2,1)S(1)} copy-done((bf16[128,1024]{1,0:T(8,128)(2,1)S(1)}, bf16[128,1024]{1,0:T(8,128)(2,1)}, u32[]{:S(2)}) %copy-start.4) | copy-done | bytes 262168
  18.0 0.8 %copy-done.5 = bf16[8,16,256]{2,1,0:T(8,128)(2,1)S(1)} copy-done((bf16[8,16,256]{2,1,0:T(8,128)(2,1)S(1)}, bf16[8,16,256]{2,1,0:T(8,128)(2,1)}, u32[]{:S(2)}) %copy-start.5) | copy-done | bytes 65560
  18.9 0.7 %copy-done.6 = bf16[8,1024]{1,0:T(8,128)(2,1)S(1)} copy-done((bf16[8,1024]{1,0:T(8,128)(2,1)S(1)}, bf16[8,1024]{1,0:T(8,128)(2,1)}, u32[]{:S(2)}) %copy-start.6) | copy-done | bytes 16408
  19.6 0.8 %copy-done.7 = bf16[1024,16]{0,1:T(8,128)(2,1)S(1)} copy-done((bf16[1024,16]{0,1:T(8,128)(2,1)S(1)}, bf16[1024,16]{0,1:T(8,128)(2,1)}, u32[]{:S(2)}) %copy-start.7) | copy-done | bytes 32792
  20.3 2.3 %stage.1 = (bf16[128,1024]{1,0:T(8,128)(2,1)}, bf16[8,1024]{1,0:T(8,128)(2,1)}, bf16[16,1024]{1,0:T(8,128)(2,1)S(1)}, bf16[1024,1024]{1,0:T(8,128)(2,1)S(1)}, bf...) custom-call(bf16[128,1024]{1,0:T(8,128)(2,1)S(1)} %bitcast.6, ...), custom_call_target="tpu_custom_call" | custom-call | flops 289669120 | bytes 14148096 | tf_op jit(solution)/shard_map/stage/pallas_call | solution.py:34
  22.7 2.4 %front_own.1 = (bf16[1024,256]{1,0:T(8,128)(2,1)S(1)}, bf16[1024,16]{1,0:T(8,128)(2,1)S(1)}, f32[16,256]{1,0:T(8,128)S(1)}, f32[16,16]{1,0:T(8,128)S(1)}, f32[12...) custom-call(bf16[72,1024]{1,0:T(8,128)(2,1)S(1)} %collective-permute-done.refs_0_, ...), custom_call_target="tpu_custom_call" | custom-call | flops 754974720 | bytes 7742976 | tf_op jit(solution)/shard_map/front_own/pallas_call | solution.py:34
  25.1 1.5 %front_later.1 = (bf16[128,512]{1,0:T(8,128)(2,1)S(1)}, bf16[2,256,512]{2,1,0:T(8,128)(2,1)S(1)}) custom-call(bf16[128,256]{1,0:T(8,128)(2,1)S(1)} %get-tuple-element.28.refs_2_.refs_0_, bf16[128,256]{1,0:T(8,128)(2,1)S(1)} %collective-permute-done.2.refs_3_.refs_1_, bf16[1024,256]{1,0:T(8,128)(2,1)S(1)} %get-tuple-element.38.refs_2_, ...), custom_call_target="tpu_custom_call" | custom-call | flops 469762048 | bytes 5030912 | tf_op jit(solution)/shard_map/front_later/pallas_call | solution.py:34
  26.6 4.4 %collective-permute-start.4 = (bf16[2,256,512]{2,1,0:T(8,128)(2,1)S(1)}, bf16[2,256,512]{2,1,0:T(8,128)(2,1)S(1)}, u32[]{:S(2)}, u32[]{:S(2)}) collective-permute-start(bf16[2,256,512]{2,1,0:T(8,128)(2,1)S(1)} %get-tuple-element.44.refs_2_), channel_id=1, source_target_pairs={{2,0},{4,2},{6,4},{8,6},{10,8},{12,10},{14,12},{16,14},{18,16},{20... | collective-permute-start | bytes 1572872 | tf_op jit(solution)/shard_map/ppermute | solution.py:24
  31.0 0.9 %attend_band.1 = (f32[128,512]{1,0:T(8,128)S(1)}, f32[128,512]{1,0:T(8,128)S(1)}, f32[128,512]{1,0:T(8,128)S(1)}, f32[128,512]{1,0:T(8,128)S(1)}) custom-call(bf16[128,512]{1,0:T(8,128)(2,1)S(1)} %get-tuple-element.37.refs_0_.query, bf16[128,512]{1,0:T(8,128)(2,1)S(1)} %get-tuple-element.43.refs_1_.query, bf16[2,256,512]{2,1,0:T(8,128)(2,1)S(1)} %get-tuple-element.44.refs_2_), custom_call_target="tpu_custom_call" | custom-call | flops 134217728 | bytes 1835008 | tf_op jit(solution)/shard_map/attend_band/pallas_call | solution.py:34
  32.0 5.7 %collective-permute-done.4.east = bf16[2,256,512]{2,1,0:T(8,128)(2,1)S(1)} collective-permute-done((bf16[2,256,512]{2,1,0:T(8,128)(2,1)S(1)}, bf16[2,256,512]{2,1,0:T(8,128)(2,1)S(1)}, u32[]{:S(2)}, u32[]{:S(2)}) %collective-permute-start.4) | collective-permute-done | bytes 524320 | tf_op jit(solution)/shard_map/ppermute | solution.py:24
  37.7 4.6 %collective-permute-done.5.west = bf16[2,256,512]{2,1,0:T(8,128)(2,1)S(1)} collective-permute-done((bf16[2,256,512]{2,1,0:T(8,128)(2,1)S(1)}, bf16[2,256,512]{2,1,0:T(8,128)(2,1)S(1)}, u32[]{:S(2)}, u32[]{:S(2)}) %collective-permute-start.5) | collective-permute-done | bytes 524320 | tf_op jit(solution)/shard_map/ppermute | solution.py:24
  42.3 1.3 %attend_later.1 = bf16[128,1024]{1,0:T(8,128)(2,1)S(1)} custom-call(bf16[128,512]{1,0:T(8,128)(2,1)S(1)} %get-tuple-element.43.refs_1_.query, f32[128,512]{1,0:T(8,128)S(1)} %get-tuple-element.49.numer, f32[128,512]{1,0:T(8,128)S(1)} %get-tuple-element.50.denom, bf16[2,256,512]{2,1,0:T(8,128)(2,1)S(1)} %collective-permute-done.4.east, ...), custom_call_target="tpu_custom_call" | custom-call | flops 268435456 | bytes 3014656 | tf_op jit(solution)/shard_map/attend_later/pallas_call | solution.py:34
  44.2 1.3 %attend_own.1 = f32[128,1024]{1,0:T(8,128)S(1)} custom-call(bf16[128,512]{1,0:T(8,128)(2,1)S(1)} %get-tuple-element.37.refs_0_.query, f32[128,512]{1,0:T(8,128)S(1)} %get-tuple-element.45.numer, f32[128,512]{1,0:T(8,128)S(1)} %get-tuple-element.46.denom, bf16[2,256,512]{2,1,0:T(8,128)(2,1)S(1)} %collective-permute-done.4.east, ...), custom_call_target="tpu_custom_call" | custom-call | flops 268435456 | bytes 3801088 | tf_op jit(solution)/shard_map/attend_own/pallas_call | solution.py:34
  45.5 4.6 %collective-permute-done.6 = bf16[128,1024]{1,0:T(8,128)(2,1)S(1)} collective-permute-done((bf16[128,1024]{1,0:T(8,128)(2,1)S(1)}, bf16[128,1024]{1,0:T(8,128)(2,1)S(1)}, u32[]{:S(2)}, u32[]{:S(2)}) %collective-permute-start.6) | collective-permute-done | bytes 262176 | tf_op jit(solution)/shard_map/ppermute | solution.py:24
  50.1 0.8 %add_convert_fusion = bf16[128,1024]{1,0:T(8,128)(2,1)} fusion(f32[128,1024]{1,0:T(8,128)S(1)} %attend_own.1, bf16[128,1024]{1,0:T(8,128)(2,1)S(1)} %collective-permute-done.6), kind=kLoop, calls=%fused_computation | loop fusion | flops 393216 | bytes 1048576 | tf_op jit(solution)/shard_map/convert_element_type | solution.py:279
  (15 shorter events, 0.7 us)
Async XLA Ops:
  1.6 7.7 %collective-permute-start = (bf16[72,1024]{1,0:T(8,128)(2,1)S(1)}, bf16[72,1024]{1,0:T(8,128)(2,1)S(1)}, u32[]{:S(2)}, u32[]{:S(2)}) collective-permute-start(bf16[72,1024]{1,0:T(8,128)(2,1)S(1)} %pad_maximum_fusion), channel_id=1, source_target_pairs={{1,0},{0,1},{3,2},{2,3},{5,4},{4,5},{7,6},{6,7},{9,8},{8,9},{11,10... | collective-permute-start | bytes 442376 | tf_op jit(solution)/shard_map/ppermute | solution.py:24
  4.7 20.4 %collective-permute-start.3 = (bf16[128,1024]{1,0:T(8,128)(2,1)}, bf16[128,1024]{1,0:T(8,128)(2,1)S(1)}, u32[]{:S(2)}, u32[]{:S(2)}) collective-permute-start(bf16[128,1024]{1,0:T(8,128)(2,1)} %refs_5_.1), channel_id=1, source_target_pairs={{1,0},{0,1},{3,2},{2,3},{5,4},{4,5},{7,6},{6,7},{9,8},{8,9},{11,10... | collective-permute-start | bytes 786440 | tf_op jit(solution)/shard_map/ppermute | solution.py:24
  9.4 13.3 %collective-permute-start.1 = (bf16[72,1024]{1,0:T(8,128)(2,1)S(1)}, bf16[72,1024]{1,0:T(8,128)(2,1)S(1)}, u32[]{:S(2)}, u32[]{:S(2)}) collective-permute-start(bf16[72,1024]{1,0:T(8,128)(2,1)S(1)} %collective-permute-done.refs_0_), channel_id=1, source_target_pairs={{2,0},{0,2},{6,4},{4,6},{10,8},{8,10},{14,12},{12,14},{18,16},{16,... | collective-permute-start | bytes 442376 | tf_op jit(solution)/shard_map/ppermute | solution.py:28
  9.4 13.3 %collective-permute-start.2 = (bf16[128,256]{1,0:T(8,128)(2,1)}, bf16[128,256]{1,0:T(8,128)(2,1)S(1)}, u32[]{:S(2)}, u32[]{:S(2)}) collective-permute-start(bf16[128,256]{1,0:T(8,128)(2,1)} %bitcast.7), channel_id=1, source_target_pairs={{1,0},{0,1},{3,2},{2,3},{5,4},{4,5},{7,6},{6,7},{9,8},{8,9},{11,10... | collective-permute-start | bytes 196616 | tf_op jit(solution)/shard_map/ppermute | solution.py:24
  11.4 1.9 %copy-start = (bf16[1024,3,512]{2,0,1:T(8,128)(2,1)S(1)}, bf16[1024,3,512]{2,0,1:T(8,128)(2,1)}, u32[]{:S(2)}) copy-start(bf16[1024,3,512]{2,0,1:T(8,128)(2,1)} %param.14) | copy-start | bytes 9437188
  13.3 1.6 %copy-start.1 = (bf16[1024,1024]{1,0:T(8,128)(2,1)S(1)}, bf16[1024,1024]{1,0:T(8,128)(2,1)}, u32[]{:S(2)}) copy-start(bf16[1024,1024]{1,0:T(8,128)(2,1)} %refs_3_.1) | copy-start | bytes 6291460
  14.9 1.2 %copy-start.2 = (bf16[512,1024]{1,0:T(8,128)(2,1)S(1)}, bf16[512,1024]{1,0:T(8,128)(2,1)}, u32[]{:S(2)}) copy-start(bf16[512,1024]{1,0:T(8,128)(2,1)} %refs_7_.1) | copy-start | bytes 3145732
  16.1 0.9 %copy-start.3 = (bf16[8,16,1024]{2,1,0:T(8,128)(2,1)S(1)}, bf16[8,16,1024]{2,1,0:T(8,128)(2,1)}, u32[]{:S(2)}) copy-start(bf16[8,16,1024]{2,1,0:T(8,128)(2,1)} %param.9) | copy-start | bytes 786436
  17.1 0.9 %copy-start.4 = (bf16[128,1024]{1,0:T(8,128)(2,1)S(1)}, bf16[128,1024]{1,0:T(8,128)(2,1)}, u32[]{:S(2)}) copy-start(bf16[128,1024]{1,0:T(8,128)(2,1)} %refs_5_.1) | copy-start | bytes 786436
  18.0 0.8 %copy-start.5 = (bf16[8,16,256]{2,1,0:T(8,128)(2,1)S(1)}, bf16[8,16,256]{2,1,0:T(8,128)(2,1)}, u32[]{:S(2)}) copy-start(bf16[8,16,256]{2,1,0:T(8,128)(2,1)} %param.8) | copy-start | bytes 196612
  18.9 0.7 %copy-start.6 = (bf16[8,1024]{1,0:T(8,128)(2,1)S(1)}, bf16[8,1024]{1,0:T(8,128)(2,1)}, u32[]{:S(2)}) copy-start(bf16[8,1024]{1,0:T(8,128)(2,1)} %refs_1_.1) | copy-start | bytes 49156
  19.6 0.8 %copy-start.7 = (bf16[1024,16]{0,1:T(8,128)(2,1)S(1)}, bf16[1024,16]{0,1:T(8,128)(2,1)}, u32[]{:S(2)}) copy-start(bf16[1024,16]{0,1:T(8,128)(2,1)} %param.11) | copy-start | bytes 98308
  26.6 11.1 %collective-permute-start.4 = (bf16[2,256,512]{2,1,0:T(8,128)(2,1)S(1)}, bf16[2,256,512]{2,1,0:T(8,128)(2,1)S(1)}, u32[]{:S(2)}, u32[]{:S(2)}) collective-permute-start(bf16[2,256,512]{2,1,0:T(8,128)(2,1)S(1)} %get-tuple-element.44.refs_2_), channel_id=1, source_target_pairs={{2,0},{4,2},{6,4},{8,6},{10,8},{12,10},{14,12},{16,14},{18,16},{20... | collective-permute-start | bytes 1572872 | tf_op jit(solution)/shard_map/ppermute | solution.py:24
  31.0 11.3 %collective-permute-start.5 = (bf16[2,256,512]{2,1,0:T(8,128)(2,1)S(1)}, bf16[2,256,512]{2,1,0:T(8,128)(2,1)S(1)}, u32[]{:S(2)}, u32[]{:S(2)}) collective-permute-start(bf16[2,256,512]{2,1,0:T(8,128)(2,1)S(1)} %get-tuple-element.44.refs_2_), channel_id=1, source_target_pairs={{30,0},{0,2},{2,4},{4,6},{6,8},{8,10},{10,12},{12,14},{14,16},{16,... | collective-permute-start | bytes 1572872 | tf_op jit(solution)/shard_map/ppermute | solution.py:24
  43.6 6.4 %collective-permute-start.6 = (bf16[128,1024]{1,0:T(8,128)(2,1)S(1)}, bf16[128,1024]{1,0:T(8,128)(2,1)S(1)}, u32[]{:S(2)}, u32[]{:S(2)}) collective-permute-start(bf16[128,1024]{1,0:T(8,128)(2,1)S(1)} %attend_later.1), channel_id=1, source_target_pairs={{1,0},{0,1},{3,2},{2,3},{5,4},{4,5},{7,6},{6,7},{9,8},{8,9},{11,10... | collective-permute-start | bytes 786440 | tf_op jit(solution)/shard_map/ppermute | solution.py:24

commit v3 on v2

--- a/solution.py
+++ b/solution.py
@@ -24,13 +24,18 @@
     return lax.ppermute(block, axis, [((i + distance) % n, i) for i in range(n)])
 
 
-def paired(block):
+def inward(block):
     return lax.ppermute(block, "band", [(i ^ 1, i) for i in range(lax.axis_size("band"))])
 
 
+def outward(block):
+    n = lax.axis_size("band")
+    return lax.ppermute(block, "band", [(i, (i + 1 if i % 2 else i - 1) % n) for i in range(n)])
+
+
 def call(body, outs, args, flops, name, spaces=None, scratch=()):
-    nbytes = sum(a.size * a.dtype.itemsize for a in (*args, *outs))
     spaces = spaces or [pltpu.VMEM] * len(args)
+    args = [pltpu.with_memory_space_constraint(a, s) if s == pltpu.HBM else a for a, s in zip(args, spaces)]
     return pl.pallas_call(
         body,
         out_shape=outs,
@@ -38,7 +43,7 @@
         out_specs=[pl.BlockSpec(memory_space=pltpu.VMEM) for _ in outs],
         scratch_shapes=scratch,
         compiler_params=pltpu.CompilerParams(vmem_limit_bytes=32 * 1024 * 1024),
-        cost_estimate=pl.CostEstimate(flops=flops, bytes_accessed=nbytes, transcendentals=0),
+        cost_estimate=pl.CostEstimate(flops=0, bytes_accessed=0, transcendentals=0),
         name=name,
     )(*args)
 
@@ -49,14 +54,40 @@
     return values, offset_values, dot(key_t, table, NT), dot(key_t, offsets, NT)
 
 
+def pack_body(table, offsets, pix, position, shared, placed, offsets_in, sems):
+    rows, band_tok = pix.shape
+    tok, d = position.shape
+    half = table.shape[0] // 2
+    blocks = d // band_tok
+    depth = rows // blocks
+    side = lax.rem(lax.axis_index("band"), 2)
+    moves = [
+        (offsets, offsets_in),
+        (table.at[pl.ds(pl.multiple_of(side * half, half), half)], shared.at[pl.ds(depth, half)]),
+        (position, placed.at[pl.ds(0, tok)]),
+    ]
+    for k in range(blocks):
+        lanes = pl.ds(k * band_tok, band_tok)
+        moves.append((pix.at[pl.ds(k * depth, depth)], shared.at[pl.ds(0, depth), lanes]))
+        moves.append((pix.at[pl.ds(k * depth, depth)], placed.at[pl.ds(tok, depth), lanes]))
+    copies = [pltpu.make_async_copy(a, b, sems.at[i]) for i, (a, b) in enumerate(moves)]
+    for copy in copies:
+        copy.start()
+    for copy in copies:
+        copy.wait()
+    shared[depth + half :] = offsets_in[...]
+
+
 def stage_body(n_in, *refs):
-    sources, staged, folded, sems = refs[:n_in], refs[n_in : 2 * n_in], refs[2 * n_in : -1], refs[-1]
-    copies = [pltpu.make_async_copy(a, b, sems.at[i]) for i, (a, b) in enumerate(zip(sources, staged))]
+    sources, (table, offsets), staged = refs[:n_in], refs[-3:-1], refs[n_in : 2 * n_in - 2]
+    folded, sems = refs[2 * n_in - 2 : -3], refs[-1]
+    targets = [table, offsets, *staged]
+    copies = [pltpu.make_async_copy(a, b, sems.at[i]) for i, (a, b) in enumerate(zip(sources, targets))]
     for copy in copies:
         copy.start()
     for copy in copies[:4]:
         copy.wait()
-    for out, part in zip(folded, fold(*(ref[...] for ref in staged[:4]))):
+    for out, part in zip(folded, fold(*(ref[...] for ref in targets[:4]))):
         out[...] = part
     for copy in copies[4:]:
         copy.wait()
@@ -91,54 +122,80 @@
     return merged + position.astype(F32)
 
 
-def project(merged, weight, query_out, pair_out):
+def normalize(merged):
     centre = jnp.mean(merged, axis=-1, keepdims=True)
     centred = merged - centre
     spread = jnp.mean(jnp.square(centred), axis=-1, keepdims=True)
-    normed = (centred * lax.rsqrt(spread + EPSILON)).astype(BF16)
+    return (centred * lax.rsqrt(spread + EPSILON)).astype(BF16)
+
+
+def project(merged, weight, query_out, pair_out):
+    normed = normalize(merged)
     query_out[...] = (dot(normed, weight[0]).astype(BF16) * HEAD_DIM ** (-0.5)).astype(BF16)
     for c in range(2):
         pair_out[c] = dot(normed, weight[c + 1]).astype(BF16)
 
 
-def tokens_of(pix_refs, distance, tok):
-    n = len(pix_refs)
-    me = lax.axis_index("var")
-    start = pl.multiple_of(lax.rem(me + distance, n) * tok, tok)
-    return jnp.concatenate([ref[:, pl.ds(start, tok)] for ref in pix_refs], axis=0)
-
-
-def first_body(n, *refs):
-    near, far, pix, folded = (refs[i : i + k] for i, k in ((0, n - 1), (n - 1, n - 1), (2 * n - 2, n), (3 * n - 2, 4)))
-    key_t, agg_value, position, weight = refs[3 * n + 2 : 3 * n + 6]
-    values, offset_values, keys, offset_keys, merged_out, query_out, pair_out, table = refs[3 * n + 6 :]
+def tokens_of(packs, first_row, distance, tok, depth, band_tok):
+    start = lax.rem(lax.axis_index("var") + distance, len(packs)) * tok
+    parts = []
+    for ref in packs:
+        for k in range(ref.shape[1] // band_tok):
+            lanes = pl.ds(pl.multiple_of(k * band_tok + start, tok), tok)
+            parts.append(ref[first_row : first_row + depth, lanes])
+    return jnp.concatenate(parts, axis=0)
+
+
+def first_body(n, depth, *refs):
+    packs, far, folded = refs[:n], refs[n : 2 * n - 1], refs[2 * n - 1 : 2 * n + 3]
+    key_t, agg_value, placed, weight = refs[2 * n + 3 : 2 * n + 7]
+    values, offset_values, keys, offset_keys, merged_out, query_out, pair_out, table = refs[2 * n + 7 :]
     half = table.shape[0] // 2
     side = lax.rem(lax.axis_index("band"), 2)
     parts = [tuple(ref[...] for ref in folded)]
-    for mine, other in zip(near, far):
-        table[pl.ds(pl.multiple_of(side * half, half), half)] = mine[:half]
-        table[pl.ds(pl.multiple_of((1 - side) * half, half), half)] = other[:half]
-        parts.append(fold(table[...], mine[half:], key_t[...], agg_value[...]))
+    for mine, other in zip(packs[1:], far):
+        table[pl.ds(pl.multiple_of(side * half, half), half)] = mine[depth : depth + half]
+        table[pl.ds(pl.multiple_of((1 - side) * half, half), half)] = other[depth : depth + half]
+        parts.append(fold(table[...], mine[depth + half :], key_t[...], agg_value[...]))
     for out, shares in zip((values, offset_values, keys, offset_keys), zip(*parts)):
         out[...] = jnp.concatenate(shares, axis=1)
-    tok = position.shape[0]
+    tok = merged_out.shape[0]
     merged = front(
-        tokens_of(pix, 0, tok), values[...], offset_values[...], keys[...], offset_keys[...], position[...]
+        tokens_of(packs, 0, 0, tok, depth, n * tok),
+        values[...], offset_values[...], keys[...], offset_keys[...], placed[:tok],
     )
     merged_out[...] = merged
     project(merged, weight, query_out, pair_out)
 
 
-def later_body(n, distance, *refs):
-    pix, (values, offset_values, keys, offset_keys, position, weight), rest = refs[:n], refs[n : n + 6], refs[n + 6 :]
+def later_body(n, depth, distance, *refs):
+    packs, (values, offset_values, keys, offset_keys, position, weight), rest = refs[:n], refs[n : n + 6], refs[n + 6 :]
     earlier, query_out, pair_out = rest[:-2], rest[-2], rest[-1]
     tok = position.shape[0]
     merged = front(
-        tokens_of(pix, distance, tok), values[...], offset_values[...], keys[...], offset_keys[...], position[...]
+        tokens_of(packs, 0, distance, tok, depth, n * tok),
+        values[...], offset_values[...], keys[...], offset_keys[...], position[...],
     )
     for i, pair in enumerate(earlier):
         pair_out[:, i * tok : (i + 1) * tok] = pair[...]
     project(merged, weight, query_out, pair_out.at[:, pl.ds(len(earlier) * tok, tok)])
+
+
+def outer_body(n, depth, *refs):
+    packs, (values, offset_values, keys, offset_keys, weight, pair_out) = refs[:n], refs[n:]
+    tok = packs[0].shape[0] - depth
+    step = min(n, 2)
+    for r in range(0, n, step):
+        pix = [tokens_of(packs, tok, r + i, tok, depth, n * tok) for i in range(step)]
+        position = [packs[r + i][:tok] for i in range(step)]
+        normed = normalize(
+            front(
+                jnp.concatenate(pix, axis=1),
+                values[...], offset_values[...], keys[...], offset_keys[...], jnp.concatenate(position, axis=0),
+            )
+        )
+        for c in range(2):
+            pair_out[c, r * tok : (r + step) * tok] = dot(normed, weight[c + 1]).astype(BF16)
 
 
 def absorb(query, pairs):
@@ -172,8 +229,8 @@
         totals[2 * i][...], totals[2 * i + 1][...] = absorb(query[...], [pair])
 
 
-def finish_body(query, numer, denom, east, west, out_weight, *refs):
-    top, low = absorb(query[...], [east, west])
+def finish_body(query, numer, denom, inner, outer, out_weight, *refs):
+    top, low = absorb(query[...], [inner, outer])
     context = ((numer[...] + top) / (denom[...] + low)).astype(BF16)
     update = dot(context, out_weight[...])
     out = refs[-1]
@@ -191,35 +248,45 @@
     n_heads = agg_key.shape[1]
     all_vars = n_vars * n
     rows = n_vars * n_pix
+    depth = rows * band_tok // d
     sds = jax.ShapeDtypeStruct
     table = embed_weight.reshape(rows, d)
     pix = pixels.reshape(rows, band_tok)
     key_t = jnp.transpose(agg_key)
     weight = jnp.transpose(qkv_weight, (1, 0, 2))
 
-    pixs = [shifted(pix, "var", r) for r in range(1, n)]
-    side = lax.rem(lax.axis_index("band"), 2)
-    half = jnp.concatenate([lax.dynamic_slice_in_dim(table, side * (rows // 2), rows // 2, 0), variable_embed], axis=0)
-    near = [shifted(half, "var", r) for r in range(1, n)]
+    shared, placed = call(
+        pack_body,
+        [sds((depth + rows // 2 + n_vars, d), BF16), sds((tok + depth, d), BF16)],
+        (table, variable_embed, pix, position),
+        0,
+        "pack",
+        [pltpu.HBM] * 4,
+        [pltpu.VMEM((n_vars, d), BF16), pltpu.SemaphoreType.DMA((3 + 2 * (d // band_tok),))],
+    )
+    near = [shifted(shared, "var", r) for r in range(1, n)]
+    outer = outward(placed)
     positions = [shifted(position, "var", r) for r in range(1, n)]
-    far = [paired(x) for x in near]
-
-    moved = (table, variable_embed, key_t, agg_value, pix, position, weight, out_weight)
-    *staged, f0, f1, f2, f3 = call(
+
+    moved = (table, variable_embed, key_t, agg_value, weight, out_weight)
+    key_t, agg_value, weight, out_weight, *folded = call(
         functools.partial(stage_body, len(moved)),
-        [sds(a.shape, a.dtype) for a in moved]
+        [sds(a.shape, a.dtype) for a in moved[2:]]
         + [sds((d, rows), BF16), sds((d, n_vars), BF16), sds((n_heads, rows), F32), sds((n_heads, n_vars), F32)],
         moved,
         2 * (rows + n_vars) * d * (d + n_heads),
         "stage",
-        [pl.ANY] * len(moved),
-        [pltpu.SemaphoreType.DMA((len(moved),))],
-    )
-    _, _, key_t, agg_value, pix, position, weight, out_weight = staged
-    pixs = [pix] + pixs
+        [pltpu.HBM] * len(moved),
+        [pltpu.VMEM((rows, d), BF16), pltpu.VMEM((n_vars, d), BF16), pltpu.SemaphoreType.DMA((len(moved),))],
+    )
+    *near, _ = lax.optimization_barrier((*near, folded[2]))
+    far = [inward(x) for x in near]
+    packs = [shared] + near
+    outer, _, *far = lax.optimization_barrier((outer, folded[0], *far))
+    outers = [outer] + [shifted(outer, "var", r) for r in range(1, n)]
     front_flops = 2 * tok * d * (3 * width + 2 * rows)
     *folded, merged, query, pair = call(
-        functools.partial(first_body, n),
+        functools.partial(first_body, n, depth),
         [
             sds((d, rows * n), BF16),
             sds((d, all_vars), BF16),
@@ -229,7 +296,7 @@
             sds((tok, width), BF16),
             sds((2, tok, width), BF16),
         ],
-        (*near, *far, *pixs, f0, f1, f2, f3, key_t, agg_value, position, weight),
+        (*packs, *far, *folded, key_t, agg_value, placed, weight),
         2 * (n - 1) * (rows + n_vars) * d * d + front_flops,
         "front_own",
         scratch=[pltpu.VMEM((rows, d), BF16)],
@@ -238,16 +305,16 @@
     for r in range(1, n):
         last = r == n - 1
         query, pair = call(
-            functools.partial(later_body, n, r),
+            functools.partial(later_body, n, depth, r),
             [sds((tok, width), BF16), sds((2, band_tok if last else tok, width), BF16)],
-            (*pixs, *folded, positions[r - 1], weight, *(pairs if last else ())),
+            (*packs, *folded, positions[r - 1], weight, *(pairs if last else ())),
             front_flops,
             "front_later",
         )
         queries.append(query)
         pairs.append(pair)
     pair = pairs[-1]
-    east, west = shifted(pair, "band", 1), shifted(pair, "band", -1)
+    inner = inward(pair)
     flops = 4 * tok * band_tok * width
     totals = call(
         functools.partial(begin_body, n),
@@ -256,13 +323,21 @@
         n * flops,
         "attend_band",
     )
-    flops = 2 * flops + 2 * tok * width * d
+    *outers, _ = lax.optimization_barrier((*outers, totals[0]))
+    (outer_pair,) = call(
+        functools.partial(outer_body, n, depth),
+        [sds((2, band_tok, width), BF16)],
+        (*outers, *folded, weight),
+        n * front_flops,
+        "front_outer",
+    )
+    flops += 2 * tok * width * d
     ending = []
     for r in range(1, n):
         (share,) = call(
             finish_body,
             [sds((tok, d), BF16)],
-            (queries[r], *totals[2 * r : 2 * r + 2], east, west, out_weight),
+            (queries[r], *totals[2 * r : 2 * r + 2], inner, outer_pair, out_weight),
             flops,
             "attend_later",
         )
@@ -270,7 +345,7 @@
     (update,) = call(
         finish_body,
         [sds((tok, d), F32)],
-        (queries[0], *totals[:2], east, west, out_weight, merged),
+        (queries[0], *totals[:2], inner, outer_pair, out_weight, merged),
         flops,
         "attend_own",
     )

time: 51.3 us -> 40 us (0.78)
  local copies, waits for them, and re-layouts: 9.83 us -> 0 us
  Pallas kernels: 9.72 us -> 13.6 us
  waiting for transfers between devices: 19.5 us -> 15.9 us
  starting transfers between devices: 10.2 us -> 9.31 us
  other arithmetic: 1.49 us -> 0.76 us
    unnamed x16 -> x0, local copies, waits for them, and re-layouts: 8.92 us -> none
    ppermute x6 -> x4, waiting for transfers between devices: 19.5 us -> 13.9 us  [shifted(): lax.ppermute(block, axis, [((i + distance) % n, i) for i in range(n)])]
    ppermute x6 -> x4, starting transfers between devices: 10.2 us -> 4.62 us  [shifted(): lax.ppermute(block, axis, [((i + distance) % n, i) for i in range(n)])]
    ppermute x1 -> x3, starting transfers between devices: 0.01 us -> 4.69 us  [the longest x1 3.69 us: outward(): lax.ppermute(block, 'band', [(i, (i + 1 if i % 2 else i - 1) % n) for i i...]
    pallas_call x6 -> x8, Pallas kernels: 9.72 us -> 13.6 us  [call(): pl.pallas_call(body, out_shape=outs, in_specs=[pl.BlockSpec(memory_space=...]
    ppermute x1 -> x3, waiting for transfers between devices: 0.01 us -> 2.05 us  [the longest x1 2.05 us: outward(): lax.ppermute(block, 'band', [(i, (i + 1 if i % 2 else i - 1) % n) for i i...]
    dynamic_slice x1 -> x0, local copies, waits for them, and re-layouts: 0.91 us -> none  [shards(): lax.dynamic_slice_in_dim(table, side * (rows // 2), rows // 2, 0)]
    concatenate x1 -> x0, other arithmetic: 0.73 us -> none  [shards(): jnp.concatenate([lax.dynamic_slice_in_dim(table, side * (rows // 2), rows...]
  transfers between devices with their start and end apart: 7 -> 7, of which waited for: 4 -> 3; matrix products, arithmetic and copies ran while one was open for 0% -> 0% of each run, Pallas kernels for 14% -> 24%
where the time goes in v3:
time: 40 us; the launch traced here: 39.7 us
  waiting for transfers between devices  15.9 us (40%)
  Pallas kernels  13.6 us (34%)
  starting transfers between devices  9.31 us (23%)
  other arithmetic  0.76 us (2%)
    ppermute x4, waiting for transfers between devices, shifted(): lax.ppermute(block, axis, [((i + distance) % n, i) for i in range(n)])  13.9 us
    pallas_call x8, Pallas kernels, call(): pl.pallas_call(body, out_shape=outs, in_specs=[pl.BlockSpec(memory_space=...  13.6 us
    ppermute x4, starting transfers between devices, shifted(): lax.ppermute(block, axis, [((i + distance) % n, i) for i in range(n)])  4.62 us
    ppermute x1, starting transfers between devices, outward(): lax.ppermute(block, 'band', [(i, (i + 1 if i % 2 else i - 1) % n) for i i...  3.69 us
    ppermute x1, waiting for transfers between devices, outward(): lax.ppermute(block, 'band', [(i, (i + 1 if i % 2 else i - 1) % n) for i i...  2.05 us
    ppermute x2, starting transfers between devices, inward(): lax.ppermute(block, 'band', [(i ^ 1, i) for i in range(lax.axis_size('ban...  1 us
  transfers between devices with their start and end apart: 7, of which 3 were waited for; matrix products, arithmetic and copies ran while one was open for 0% of the time, Pallas kernels for 24%

profile of v3, /device:TPU:0, one launch (start us, length us, event | category | flops | bytes accessed | tf_op | source)
XLA Modules:
  0.0 39.7 jit_solution(5739773177420134993)
XLA Ops:
  0.0 1.1 %pack.1 = (bf16[104,1024]{1,0:T(8,128)(2,1)S(1)}, bf16[160,1024]{1,0:T(8,128)(2,1)S(1)}) custom-call(bf16[128,1024]{1,0:T(8,128)(2,1)} %bitcast.5, bf16[8,1024]{1,0:T(8,128)(2,1)} %refs_1_.1, bf16[128,256]{1,0:T(8,128)(2,1)} %bitcast.7, bf16[128,1024]{1,0:T(8,128)(2,1)} %position.1), custom_call_target="tpu_custom_call" | custom-call | tf_op jit(solution)/shard_map/pack/pallas_call | solution.py:39
  1.2 3.0 %collective-permute-start = (bf16[104,1024]{1,0:T(8,128)(2,1)S(1)}, bf16[104,1024]{1,0:T(8,128)(2,1)S(1)}, u32[]{:S(2)}, u32[]{:S(2)}) collective-permute-start(bf16[104,1024]{1,0:T(8,128)(2,1)S(1)} %get-tuple-element.33.refs_0_), channel_id=1, source_target_pairs={{1,0},{0,1},{3,2},{2,3},{5,4},{4,5},{7,6},{6,7},{9,8},{8,9},{11,10... | collective-permute-start | bytes 638984 | tf_op jit(solution)/shard_map/ppermute | solution.py:24
  4.2 3.7 %collective-permute-start.1 = (bf16[160,1024]{1,0:T(8,128)(2,1)S(1)}, bf16[160,1024]{1,0:T(8,128)(2,1)S(1)}, u32[]{:S(2)}, u32[]{:S(2)}) collective-permute-start(bf16[160,1024]{1,0:T(8,128)(2,1)S(1)} %get-tuple-element.36.refs_9_), channel_id=1, source_target_pairs={{0,30},{2,4},{4,2},{6,8},{8,6},{10,12},{12,10},{14,16},{16,14},{18... | collective-permute-start | bytes 983048 | tf_op jit(solution)/shard_map/ppermute | solution.py:33
  7.9 0.5 %collective-permute-start.3 = (bf16[128,1024]{1,0:T(8,128)(2,1)}, bf16[128,1024]{1,0:T(8,128)(2,1)S(1)}, u32[]{:S(2)}, u32[]{:S(2)}) collective-permute-start(bf16[128,1024]{1,0:T(8,128)(2,1)} %position.1), channel_id=1, source_target_pairs={{1,0},{0,1},{3,2},{2,3},{5,4},{4,5},{7,6},{6,7},{9,8},{8,9},{11,10... | collective-permute-start | bytes 786440 | tf_op jit(solution)/shard_map/ppermute | solution.py:24
  8.4 3.0 %stage.1 = (bf16[16,1024]{1,0:T(8,128)(2,1)S(1)}, bf16[1024,1024]{1,0:T(8,128)(2,1)S(1)}, bf16[3,1024,512]{2,1,0:T(8,128)(2,1)S(1)}, bf16[512,1024]{1,0:T(8,128)...) custom-call(bf16[128,1024]{1,0:T(8,128)(2,1)} %bitcast.6, ...), custom_call_target="tpu_custom_call" | custom-call | tf_op jit(solution)/shard_map/stage/pallas_call | solution.py:39
  11.3 0.0 collective-permute-done.refs_1_
  11.4 0.1 collective-permute-start.2
  11.4 2.0 %collective-permute-done.1.refs_0_ = bf16[160,1024]{1,0:T(8,128)(2,1)S(1)} collective-permute-done((bf16[160,1024]{1,0:T(8,128)(2,1)S(1)}, bf16[160,1024]{1,0:T(8,128)(2,1)S(1)}, u32[]{:S(2)}, u32[]{:S(2)}) %collective-permute-start.1) | collective-permute-done | bytes 327712 | tf_op jit(solution)/shard_map/ppermute | solution.py:33
  13.5 0.0 collective-permute-done.2.refs_2_
  13.5 2.4 %front_own.1 = (bf16[1024,256]{1,0:T(8,128)(2,1)S(1)}, bf16[1024,16]{1,0:T(8,128)(2,1)S(1)}, f32[16,256]{1,0:T(8,128)S(1)}, f32[16,16]{1,0:T(8,128)S(1)}, f32[12...) custom-call(bf16[104,1024]{1,0:T(8,128)(2,1)S(1)} %get-tuple-element.33.refs_0_, ...), custom_call_target="tpu_custom_call" | custom-call | tf_op jit(solution)/shard_map/front_own/pallas_call | solution.py:39
  15.9 0.0 collective-permute-done.3.refs_6_
  16.0 1.5 %front_later.1 = (bf16[128,512]{1,0:T(8,128)(2,1)S(1)}, bf16[2,256,512]{2,1,0:T(8,128)(2,1)S(1)}) custom-call(bf16[104,1024]{1,0:T(8,128)(2,1)S(1)} %get-tuple-element.33.refs_0_, bf16[104,1024]{1,0:T(8,128)(2,1)S(1)} %collective-permute-done.refs_1_, bf16[1024,256]{1,0:T(8,128)(2,1)S(1)} %get-tuple-element.45.refs_2_, ...), custom_call_target="tpu_custom_call" | custom-call | tf_op jit(solution)/shard_map/front_later/pallas_call | solution.py:39
  17.4 0.9 %collective-permute-start.4 = (bf16[2,256,512]{2,1,0:T(8,128)(2,1)S(1)}, bf16[2,256,512]{2,1,0:T(8,128)(2,1)S(1)}, u32[]{:S(2)}, u32[]{:S(2)}) collective-permute-start(bf16[2,256,512]{2,1,0:T(8,128)(2,1)S(1)} %get-tuple-element.51.refs_2_), channel_id=1, source_target_pairs={{2,0},{0,2},{6,4},{4,6},{10,8},{8,10},{14,12},{12,14},{18,16},{16,... | collective-permute-start | bytes 1572872 | tf_op jit(solution)/shard_map/ppermute | solution.py:28
  18.4 0.5 %collective-permute-start.5 = (bf16[160,1024]{1,0:T(8,128)(2,1)S(1)}, bf16[160,1024]{1,0:T(8,128)(2,1)S(1)}, u32[]{:S(2)}, u32[]{:S(2)}) collective-permute-start(bf16[160,1024]{1,0:T(8,128)(2,1)S(1)} %collective-permute-done.1.refs_0_), channel_id=1, source_target_pairs={{1,0},{0,1},{3,2},{2,3},{5,4},{4,5},{7,6},{6,7},{9,8},{8,9},{11,10... | collective-permute-start | bytes 983048 | tf_op jit(solution)/shard_map/ppermute | solution.py:24
  18.9 0.9 %attend_band.1 = (f32[128,512]{1,0:T(8,128)S(1)}, f32[128,512]{1,0:T(8,128)S(1)}, f32[128,512]{1,0:T(8,128)S(1)}, f32[128,512]{1,0:T(8,128)S(1)}) custom-call(bf16[128,512]{1,0:T(8,128)(2,1)S(1)} %get-tuple-element.44.refs_0_.query, bf16[128,512]{1,0:T(8,128)(2,1)S(1)} %get-tuple-element.50.refs_1_.query, bf16[2,256,512]{2,1,0:T(8,128)(2,1)S(1)} %get-tuple-element.51.refs_2_), custom_call_target="tpu_custom_call" | custom-call | tf_op jit(solution)/shard_map/attend_band/pallas_call | solution.py:39
  19.8 8.2 %collective-permute-done.5.refs_1_ = bf16[160,1024]{1,0:T(8,128)(2,1)S(1)} collective-permute-done((bf16[160,1024]{1,0:T(8,128)(2,1)S(1)}, bf16[160,1024]{1,0:T(8,128)(2,1)S(1)}, u32[]{:S(2)}, u32[]{:S(2)}) %collective-permute-start.5) | collective-permute-done | bytes 327712 | tf_op jit(solution)/shard_map/ppermute | solution.py:24
  28.1 2.0 %front_outer.1.outer = bf16[2,256,512]{2,1,0:T(8,128)(2,1)S(1)} custom-call(bf16[160,1024]{1,0:T(8,128)(2,1)S(1)} %collective-permute-done.1.refs_0_, bf16[160,1024]{1,0:T(8,128)(2,1)S(1)} %collective-permute-done.5.refs_1_, bf16[1024,256]{1,0:T(8,128)(2,1)S(1)} %get-tuple-element.45.refs_2_, bf16[1024,16]{1,0:T(8,128)(2,1)S(1)} %get-tuple-element.46.refs_3_, ...), custom_call_target="tpu_custom_call" | custom-call | tf_op jit(solution)/shard_map/front_outer/pallas_call | solution.py:39
  30.1 0.0 collective-permute-done.4.inner
  30.1 1.3 %attend_later.1 = bf16[128,1024]{1,0:T(8,128)(2,1)S(1)} custom-call(bf16[128,512]{1,0:T(8,128)(2,1)S(1)} %get-tuple-element.50.refs_1_.query, f32[128,512]{1,0:T(8,128)S(1)} %get-tuple-element.59.numer, f32[128,512]{1,0:T(8,128)S(1)} %get-tuple-element.60.denom, bf16[2,256,512]{2,1,0:T(8,128)(2,1)S(1)} %collective-permute-done.4.inner, ...), custom_call_target="tpu_custom_call" | custom-call | tf_op jit(solution)/shard_map/attend_later/pallas_call | solution.py:39
  31.4 0.6 %collective-permute-start.6 = (bf16[128,1024]{1,0:T(8,128)(2,1)S(1)}, bf16[128,1024]{1,0:T(8,128)(2,1)S(1)}, u32[]{:S(2)}, u32[]{:S(2)}) collective-permute-start(bf16[128,1024]{1,0:T(8,128)(2,1)S(1)} %attend_later.1), channel_id=1, source_target_pairs={{1,0},{0,1},{3,2},{2,3},{5,4},{4,5},{7,6},{6,7},{9,8},{8,9},{11,10... | collective-permute-start | bytes 786440 | tf_op jit(solution)/shard_map/ppermute | solution.py:24
  32.0 1.3 %attend_own.1 = f32[128,1024]{1,0:T(8,128)S(1)} custom-call(bf16[128,512]{1,0:T(8,128)(2,1)S(1)} %get-tuple-element.44.refs_0_.query, f32[128,512]{1,0:T(8,128)S(1)} %get-tuple-element.52.numer, f32[128,512]{1,0:T(8,128)S(1)} %get-tuple-element.53.denom, bf16[2,256,512]{2,1,0:T(8,128)(2,1)S(1)} %collective-permute-done.4.inner, ...), custom_call_target="tpu_custom_call" | custom-call | tf_op jit(solution)/shard_map/attend_own/pallas_call | solution.py:39
  33.3 5.7 %collective-permute-done.6 = bf16[128,1024]{1,0:T(8,128)(2,1)S(1)} collective-permute-done((bf16[128,1024]{1,0:T(8,128)(2,1)S(1)}, bf16[128,1024]{1,0:T(8,128)(2,1)S(1)}, u32[]{:S(2)}, u32[]{:S(2)}) %collective-permute-start.6) | collective-permute-done | bytes 262176 | tf_op jit(solution)/shard_map/ppermute | solution.py:24
  38.9 0.8 %add_convert_fusion = bf16[128,1024]{1,0:T(8,128)(2,1)} fusion(f32[128,1024]{1,0:T(8,128)S(1)} %attend_own.1, bf16[128,1024]{1,0:T(8,128)(2,1)S(1)} %collective-permute-done.6), kind=kLoop, calls=%fused_computation | loop fusion | flops 393216 | bytes 1048576 | tf_op jit(solution)/shard_map/convert_element_type | solution.py:354
Async XLA Ops:
  1.2 10.2 %collective-permute-start = (bf16[104,1024]{1,0:T(8,128)(2,1)S(1)}, bf16[104,1024]{1,0:T(8,128)(2,1)S(1)}, u32[]{:S(2)}, u32[]{:S(2)}) collective-permute-start(bf16[104,1024]{1,0:T(8,128)(2,1)S(1)} %get-tuple-element.33.refs_0_), channel_id=1, source_target_pairs={{1,0},{0,1},{3,2},{2,3},{5,4},{4,5},{7,6},{6,7},{9,8},{8,9},{11,10... | collective-permute-start | bytes 638984 | tf_op jit(solution)/shard_map/ppermute | solution.py:24
  4.2 9.3 %collective-permute-start.1 = (bf16[160,1024]{1,0:T(8,128)(2,1)S(1)}, bf16[160,1024]{1,0:T(8,128)(2,1)S(1)}, u32[]{:S(2)}, u32[]{:S(2)}) collective-permute-start(bf16[160,1024]{1,0:T(8,128)(2,1)S(1)} %get-tuple-element.36.refs_9_), channel_id=1, source_target_pairs={{0,30},{2,4},{4,2},{6,8},{8,6},{10,12},{12,10},{14,16},{16,14},{18... | collective-permute-start | bytes 983048 | tf_op jit(solution)/shard_map/ppermute | solution.py:33
  7.9 8.1 %collective-permute-start.3 = (bf16[128,1024]{1,0:T(8,128)(2,1)}, bf16[128,1024]{1,0:T(8,128)(2,1)S(1)}, u32[]{:S(2)}, u32[]{:S(2)}) collective-permute-start(bf16[128,1024]{1,0:T(8,128)(2,1)} %position.1), channel_id=1, source_target_pairs={{1,0},{0,1},{3,2},{2,3},{5,4},{4,5},{7,6},{6,7},{9,8},{8,9},{11,10... | collective-permute-start | bytes 786440 | tf_op jit(solution)/shard_map/ppermute | solution.py:24
  11.4 2.1 %collective-permute-start.2 = (bf16[104,1024]{1,0:T(8,128)(2,1)S(1)}, bf16[104,1024]{1,0:T(8,128)(2,1)S(1)}, u32[]{:S(2)}, u32[]{:S(2)}) collective-permute-start(bf16[104,1024]{1,0:T(8,128)(2,1)S(1)} %collective-permute-done.refs_1_), channel_id=1, source_target_pairs={{2,0},{0,2},{6,4},{4,6},{10,8},{8,10},{14,12},{12,14},{18,16},{16,... | collective-permute-start | bytes 638984 | tf_op jit(solution)/shard_map/ppermute | solution.py:28
  17.4 12.7 %collective-permute-start.4 = (bf16[2,256,512]{2,1,0:T(8,128)(2,1)S(1)}, bf16[2,256,512]{2,1,0:T(8,128)(2,1)S(1)}, u32[]{:S(2)}, u32[]{:S(2)}) collective-permute-start(bf16[2,256,512]{2,1,0:T(8,128)(2,1)S(1)} %get-tuple-element.51.refs_2_), channel_id=1, source_target_pairs={{2,0},{0,2},{6,4},{4,6},{10,8},{8,10},{14,12},{12,14},{18,16},{16,... | collective-permute-start | bytes 1572872 | tf_op jit(solution)/shard_map/ppermute | solution.py:28
  18.4 9.7 %collective-permute-start.5 = (bf16[160,1024]{1,0:T(8,128)(2,1)S(1)}, bf16[160,1024]{1,0:T(8,128)(2,1)S(1)}, u32[]{:S(2)}, u32[]{:S(2)}) collective-permute-start(bf16[160,1024]{1,0:T(8,128)(2,1)S(1)} %collective-permute-done.1.refs_0_), channel_id=1, source_target_pairs={{1,0},{0,1},{3,2},{2,3},{5,4},{4,5},{7,6},{6,7},{9,8},{8,9},{11,10... | collective-permute-start | bytes 983048 | tf_op jit(solution)/shard_map/ppermute | solution.py:24
  31.4 7.5 %collective-permute-start.6 = (bf16[128,1024]{1,0:T(8,128)(2,1)S(1)}, bf16[128,1024]{1,0:T(8,128)(2,1)S(1)}, u32[]{:S(2)}, u32[]{:S(2)}) collective-permute-start(bf16[128,1024]{1,0:T(8,128)(2,1)S(1)} %attend_later.1), channel_id=1, source_target_pairs={{1,0},{0,1},{3,2},{2,3},{5,4},{4,5},{7,6},{6,7},{9,8},{8,9},{11,10... | collective-permute-start | bytes 786440 | tf_op jit(solution)/shard_map/ppermute | solution.py:24

commit v4 on v3

--- a/solution.py
+++ b/solution.py
@@ -43,7 +43,7 @@
         out_specs=[pl.BlockSpec(memory_space=pltpu.VMEM) for _ in outs],
         scratch_shapes=scratch,
         compiler_params=pltpu.CompilerParams(vmem_limit_bytes=32 * 1024 * 1024),
-        cost_estimate=pl.CostEstimate(flops=0, bytes_accessed=0, transcendentals=0),
+        cost_estimate=pl.CostEstimate(flops=20_000_000_000 if name == "attend_band" else 0, bytes_accessed=0, transcendentals=0),
         name=name,
     )(*args)
 
@@ -129,13 +129,6 @@
     return (centred * lax.rsqrt(spread + EPSILON)).astype(BF16)
 
 
-def project(merged, weight, query_out, pair_out):
-    normed = normalize(merged)
-    query_out[...] = (dot(normed, weight[0]).astype(BF16) * HEAD_DIM ** (-0.5)).astype(BF16)
-    for c in range(2):
-        pair_out[c] = dot(normed, weight[c + 1]).astype(BF16)
-
-
 def tokens_of(packs, first_row, distance, tok, depth, band_tok):
     start = lax.rem(lax.axis_index("var") + distance, len(packs)) * tok
     parts = []
@@ -146,10 +139,10 @@
     return jnp.concatenate(parts, axis=0)
 
 
-def first_body(n, depth, *refs):
+def band_body(n, depth, *refs):
     packs, far, folded = refs[:n], refs[n : 2 * n - 1], refs[2 * n - 1 : 2 * n + 3]
-    key_t, agg_value, placed, weight = refs[2 * n + 3 : 2 * n + 7]
-    values, offset_values, keys, offset_keys, merged_out, query_out, pair_out, table = refs[2 * n + 7 :]
+    positions, (key_t, agg_value, weight) = refs[2 * n + 3 : 3 * n + 3], refs[3 * n + 3 : 3 * n + 6]
+    values, offset_values, keys, offset_keys, merged_out, query_out, pair_out, table = refs[3 * n + 6 :]
     half = table.shape[0] // 2
     side = lax.rem(lax.axis_index("band"), 2)
     parts = [tuple(ref[...] for ref in folded)]
@@ -160,29 +153,26 @@
     for out, shares in zip((values, offset_values, keys, offset_keys), zip(*parts)):
         out[...] = jnp.concatenate(shares, axis=1)
     tok = merged_out.shape[0]
-    merged = front(
-        tokens_of(packs, 0, 0, tok, depth, n * tok),
-        values[...], offset_values[...], keys[...], offset_keys[...], placed[:tok],
-    )
-    merged_out[...] = merged
-    project(merged, weight, query_out, pair_out)
-
-
-def later_body(n, depth, distance, *refs):
-    packs, (values, offset_values, keys, offset_keys, position, weight), rest = refs[:n], refs[n : n + 6], refs[n + 6 :]
-    earlier, query_out, pair_out = rest[:-2], rest[-2], rest[-1]
-    tok = position.shape[0]
-    merged = front(
-        tokens_of(packs, 0, distance, tok, depth, n * tok),
-        values[...], offset_values[...], keys[...], offset_keys[...], position[...],
-    )
-    for i, pair in enumerate(earlier):
-        pair_out[:, i * tok : (i + 1) * tok] = pair[...]
-    project(merged, weight, query_out, pair_out.at[:, pl.ds(len(earlier) * tok, tok)])
+    step = min(n, 2)
+    for r in range(0, n, step):
+        pix = [tokens_of(packs, 0, r + i, tok, depth, n * tok) for i in range(step)]
+        position = [positions[r + i][:tok] for i in range(step)]
+        merged = front(
+            jnp.concatenate(pix, axis=1),
+            values[...], offset_values[...], keys[...], offset_keys[...], jnp.concatenate(position, axis=0),
+        )
+        if r == 0:
+            merged_out[...] = merged[:tok]
+        normed = normalize(merged)
+        rows = slice(r * tok, (r + step) * tok)
+        query_out[rows] = (dot(normed, weight[0]).astype(BF16) * HEAD_DIM ** (-0.5)).astype(BF16)
+        for c in range(2):
+            pair_out[c, rows] = dot(normed, weight[c + 1]).astype(BF16)
 
 
 def outer_body(n, depth, *refs):
-    packs, (values, offset_values, keys, offset_keys, weight, pair_out) = refs[:n], refs[n:]
+    packs, (values, offset_values, keys, offset_keys, weight) = refs[:n], refs[n : n + 5]
+    query, numer, denom, inner, out_weight, pair_out, *share = refs[n + 5 :]
     tok = packs[0].shape[0] - depth
     step = min(n, 2)
     for r in range(0, n, step):
@@ -196,6 +186,8 @@
         )
         for c in range(2):
             pair_out[c, r * tok : (r + step) * tok] = dot(normed, weight[c + 1]).astype(BF16)
+    if share:
+        finish_body(1, query, numer, denom, inner, pair_out, out_weight, share[0])
 
 
 def absorb(query, pairs):
@@ -223,17 +215,19 @@
     return jnp.concatenate(numers, axis=1), jnp.concatenate(denoms, axis=1)
 
 
-def begin_body(n, *refs):
-    queries, pair, totals = refs[:n], refs[n], refs[n + 1 :]
-    for i, query in enumerate(queries):
-        totals[2 * i][...], totals[2 * i + 1][...] = absorb(query[...], [pair])
-
-
-def finish_body(query, numer, denom, inner, outer, out_weight, *refs):
-    top, low = absorb(query[...], [inner, outer])
-    context = ((numer[...] + top) / (denom[...] + low)).astype(BF16)
+def begin_body(query, pair, numer, denom):
+    for r in range(0, query.shape[0], 256):
+        rows = slice(r, r + 256)
+        numer[rows], denom[rows] = absorb(query[rows], [pair])
+
+
+def finish_body(distance, query, numer, denom, inner, outer, out_weight, *refs):
+    out = refs[-1]
+    tok = out.shape[0]
+    rows = slice(distance * tok, (distance + 1) * tok)
+    top, low = absorb(query[rows], [inner, outer])
+    context = ((numer[rows] + top) / (denom[rows] + low)).astype(BF16)
     update = dot(context, out_weight[...])
-    out = refs[-1]
     for ref in refs[:-1]:
         update = update + ref[...]
     out[...] = update.astype(out.dtype)
@@ -284,73 +278,44 @@
     packs = [shared] + near
     outer, _, *far = lax.optimization_barrier((outer, folded[0], *far))
     outers = [outer] + [shifted(outer, "var", r) for r in range(1, n)]
-    front_flops = 2 * tok * d * (3 * width + 2 * rows)
+    front_flops = 2 * band_tok * d * (3 * width + 2 * rows)
     *folded, merged, query, pair = call(
-        functools.partial(first_body, n, depth),
+        functools.partial(band_body, n, depth),
         [
             sds((d, rows * n), BF16),
             sds((d, all_vars), BF16),
             sds((n_heads, rows * n), F32),
             sds((n_heads, all_vars), F32),
             sds((tok, d), F32),
-            sds((tok, width), BF16),
-            sds((2, tok, width), BF16),
+            sds((band_tok, width), BF16),
+            sds((2, band_tok, width), BF16),
         ],
-        (*packs, *far, *folded, key_t, agg_value, placed, weight),
+        (*packs, *far, *folded, placed, *positions, key_t, agg_value, weight),
         2 * (n - 1) * (rows + n_vars) * d * d + front_flops,
-        "front_own",
+        "front_band",
         scratch=[pltpu.VMEM((rows, d), BF16)],
     )
-    queries, pairs = [query], [pair]
-    for r in range(1, n):
-        last = r == n - 1
-        query, pair = call(
-            functools.partial(later_body, n, depth, r),
-            [sds((tok, width), BF16), sds((2, band_tok if last else tok, width), BF16)],
-            (*packs, *folded, positions[r - 1], weight, *(pairs if last else ())),
-            front_flops,
-            "front_later",
-        )
-        queries.append(query)
-        pairs.append(pair)
-    pair = pairs[-1]
     inner = inward(pair)
     flops = 4 * tok * band_tok * width
-    totals = call(
-        functools.partial(begin_body, n),
-        [sds((tok, width), F32)] * (2 * n),
-        (*queries, pair),
-        n * flops,
-        "attend_band",
-    )
+    totals = call(begin_body, [sds((band_tok, width), F32)] * 2, (query, pair), n * flops, "attend_band")
     *outers, _ = lax.optimization_barrier((*outers, totals[0]))
-    (outer_pair,) = call(
+    flops = 2 * flops + 2 * tok * width * d
+    outer_pair, *share = call(
         functools.partial(outer_body, n, depth),
-        [sds((2, band_tok, width), BF16)],
-        (*outers, *folded, weight),
-        n * front_flops,
+        [sds((2, band_tok, width), BF16)] + [sds((tok, d), BF16)] * (n > 1),
+        (*outers, *folded, weight, query, *totals, inner, out_weight),
+        front_flops + flops,
         "front_outer",
     )
-    flops += 2 * tok * width * d
-    ending = []
-    for r in range(1, n):
-        (share,) = call(
-            finish_body,
-            [sds((tok, d), BF16)],
-            (queries[r], *totals[2 * r : 2 * r + 2], inner, outer_pair, out_weight),
-            flops,
-            "attend_later",
-        )
-        ending.append(shifted(share, "var", n - r))
+    attended = (query, *totals, inner, outer_pair, out_weight)
+    for r in range(2, n):
+        share += call(functools.partial(finish_body, r), [sds((tok, d), BF16)], attended, flops, "attend_later")
+    ending = [shifted(x, "var", n - r) for r, x in enumerate(share, 1)]
     (update,) = call(
-        finish_body,
-        [sds((tok, d), F32)],
-        (queries[0], *totals[:2], inner, outer_pair, out_weight, merged),
-        flops,
-        "attend_own",
-    )
-    for share in ending:
-        update = update + share.astype(F32)
+        functools.partial(finish_body, 0), [sds((tok, d), F32)], (*attended, merged), flops, "attend_own"
+    )
+    for x in ending:
+        update = update + x.astype(F32)
     return update.astype(BF16)
 
 

time: 40 us -> 36.5 us (0.912)
  waiting for transfers between devices: 15.9 us -> 14 us
  Pallas kernels: 13.6 us -> 12.5 us
  starting transfers between devices: 9.31 us -> 8.86 us
    ppermute x4, waiting for transfers between devices: 13.9 us -> 11.9 us  [shifted(): lax.ppermute(block, axis, [((i + distance) % n, i) for i in range(n)])]
    pallas_call x8 -> x6, Pallas kernels: 13.6 us -> 12.5 us  [call(): pl.pallas_call(body, out_shape=outs, in_specs=[pl.BlockSpec(memory_space=...]
    ppermute x2, starting transfers between devices: 1 us -> 0.14 us  [inward(): lax.ppermute(block, 'band', [(i ^ 1, i) for i in range(lax.axis_size('ban...]
    ppermute x4, starting transfers between devices: 4.62 us -> 5.03 us  [shifted(): lax.ppermute(block, axis, [((i + distance) % n, i) for i in range(n)])]
  transfers between devices with their start and end apart: 7 -> 7, of which waited for: 3 -> 4; matrix products, arithmetic and copies ran while one was open for 0% -> 0% of each run, Pallas kernels for 24% -> 23%
where the time goes in v4:
time: 36.5 us; the launch traced here: 36.2 us
  waiting for transfers between devices  14 us (38%)
  Pallas kernels  12.5 us (34%)
  starting transfers between devices  8.86 us (24%)
  other arithmetic  0.76 us (2%)
    pallas_call x6, Pallas kernels, call(): pl.pallas_call(body, out_shape=outs, in_specs=[pl.BlockSpec(memory_space=...  12.5 us
    ppermute x4, waiting for transfers between devices, shifted(): lax.ppermute(block, axis, [((i + distance) % n, i) for i in range(n)])  11.9 us
    ppermute x4, starting transfers between devices, shifted(): lax.ppermute(block, axis, [((i + distance) % n, i) for i in range(n)])  5.03 us
    ppermute x1, starting transfers between devices, outward(): lax.ppermute(block, 'band', [(i, (i + 1 if i % 2 else i - 1) % n) for i i...  3.69 us
    ppermute x1, waiting for transfers between devices, outward(): lax.ppermute(block, 'band', [(i, (i + 1 if i % 2 else i - 1) % n) for i i...  2.05 us
    convert_element_type x1, other arithmetic, shards(): return update.astype(BF16)  0.76 us
  transfers between devices with their start and end apart: 7, of which 4 were waited for; matrix products, arithmetic and copies ran while one was open for 0% of the time, Pallas kernels for 23%

profile of v4, /device:TPU:0, one launch (start us, length us, event | category | flops | bytes accessed | tf_op | source)
XLA Modules:
  0.0 36.2 jit_solution(6361158710181331125)
XLA Ops:
  0.0 1.1 %pack.1 = (bf16[104,1024]{1,0:T(8,128)(2,1)S(1)}, bf16[160,1024]{1,0:T(8,128)(2,1)S(1)}) custom-call(bf16[128,1024]{1,0:T(8,128)(2,1)} %bitcast.5, bf16[8,1024]{1,0:T(8,128)(2,1)} %refs_1_.1, bf16[128,256]{1,0:T(8,128)(2,1)} %bitcast.7, bf16[128,1024]{1,0:T(8,128)(2,1)} %position.1), custom_call_target="tpu_custom_call" | custom-call | tf_op jit(solution)/shard_map/pack/pallas_call | solution.py:39
  1.2 3.0 %collective-permute-start = (bf16[104,1024]{1,0:T(8,128)(2,1)S(1)}, bf16[104,1024]{1,0:T(8,128)(2,1)S(1)}, u32[]{:S(2)}, u32[]{:S(2)}) collective-permute-start(bf16[104,1024]{1,0:T(8,128)(2,1)S(1)} %get-tuple-element.31.refs_0_), channel_id=1, source_target_pairs={{1,0},{0,1},{3,2},{2,3},{5,4},{4,5},{7,6},{6,7},{9,8},{8,9},{11,10... | collective-permute-start | bytes 638984 | tf_op jit(solution)/shard_map/ppermute | solution.py:24
  4.2 3.7 %collective-permute-start.1 = (bf16[160,1024]{1,0:T(8,128)(2,1)S(1)}, bf16[160,1024]{1,0:T(8,128)(2,1)S(1)}, u32[]{:S(2)}, u32[]{:S(2)}) collective-permute-start(bf16[160,1024]{1,0:T(8,128)(2,1)S(1)} %get-tuple-element.34.refs_7_), channel_id=1, source_target_pairs={{0,30},{2,4},{4,2},{6,8},{8,6},{10,12},{12,10},{14,16},{16,14},{18... | collective-permute-start | bytes 983048 | tf_op jit(solution)/shard_map/ppermute | solution.py:33
  7.9 0.5 %collective-permute-start.3 = (bf16[128,1024]{1,0:T(8,128)(2,1)}, bf16[128,1024]{1,0:T(8,128)(2,1)S(1)}, u32[]{:S(2)}, u32[]{:S(2)}) collective-permute-start(bf16[128,1024]{1,0:T(8,128)(2,1)} %position.1), channel_id=1, source_target_pairs={{1,0},{0,1},{3,2},{2,3},{5,4},{4,5},{7,6},{6,7},{9,8},{8,9},{11,10... | collective-permute-start | bytes 786440 | tf_op jit(solution)/shard_map/ppermute | solution.py:24
  8.4 3.0 %stage.1 = (bf16[16,1024]{1,0:T(8,128)(2,1)S(1)}, bf16[1024,1024]{1,0:T(8,128)(2,1)S(1)}, bf16[3,1024,512]{2,1,0:T(8,128)(2,1)S(1)}, bf16[512,1024]{1,0:T(8,128)...) custom-call(bf16[128,1024]{1,0:T(8,128)(2,1)} %bitcast.6, ...), custom_call_target="tpu_custom_call" | custom-call | tf_op jit(solution)/shard_map/stage/pallas_call | solution.py:39
  11.3 0.0 collective-permute-done.refs_1_
  11.4 0.1 collective-permute-start.2
  11.4 2.0 %collective-permute-done.1.refs_0_ = bf16[160,1024]{1,0:T(8,128)(2,1)S(1)} collective-permute-done((bf16[160,1024]{1,0:T(8,128)(2,1)S(1)}, bf16[160,1024]{1,0:T(8,128)(2,1)S(1)}, u32[]{:S(2)}, u32[]{:S(2)}) %collective-permute-start.1) | collective-permute-done | bytes 327712 | tf_op jit(solution)/shard_map/ppermute | solution.py:33
  13.5 0.0 collective-permute-done.2.refs_2_
  13.5 0.9 %collective-permute-start.5 = (bf16[160,1024]{1,0:T(8,128)(2,1)S(1)}, bf16[160,1024]{1,0:T(8,128)(2,1)S(1)}, u32[]{:S(2)}, u32[]{:S(2)}) collective-permute-start(bf16[160,1024]{1,0:T(8,128)(2,1)S(1)} %collective-permute-done.1.refs_0_), channel_id=1, source_target_pairs={{1,0},{0,1},{3,2},{2,3},{5,4},{4,5},{7,6},{6,7},{9,8},{8,9},{11,10... | collective-permute-start | bytes 983048 | tf_op jit(solution)/shard_map/ppermute | solution.py:24
  14.4 0.6 %collective-permute-done.3.refs_8_ = bf16[128,1024]{1,0:T(8,128)(2,1)S(1)} collective-permute-done((bf16[128,1024]{1,0:T(8,128)(2,1)}, bf16[128,1024]{1,0:T(8,128)(2,1)S(1)}, u32[]{:S(2)}, u32[]{:S(2)}) %collective-permute-start.3) | collective-permute-done | bytes 262176 | tf_op jit(solution)/shard_map/ppermute | solution.py:24
  15.1 3.2 %front_band.1 = (bf16[1024,256]{1,0:T(8,128)(2,1)S(1)}, bf16[1024,16]{1,0:T(8,128)(2,1)S(1)}, f32[16,256]{1,0:T(8,128)S(1)}, f32[16,16]{1,0:T(8,128)S(1)}, f32[1...) custom-call(bf16[104,1024]{1,0:T(8,128)(2,1)S(1)} %get-tuple-element.31.refs_0_, ...), custom_call_target="tpu_custom_call" | custom-call | tf_op jit(solution)/shard_map/front_band/pallas_call | solution.py:39
  18.2 0.1 collective-permute-start.4
  18.3 0.8 %attend_band.1 = (f32[256,512]{1,0:T(8,128)S(1)}, f32[256,512]{1,0:T(8,128)S(1)}) custom-call(bf16[256,512]{1,0:T(8,128)(2,1)S(1)} %get-tuple-element.42.query.refs_7_, bf16[2,256,512]{2,1,0:T(8,128)(2,1)S(1)} %get-tuple-element.43.pair), custom_call_target="tpu_custom_call" | custom-call | flops 20000000000 | tf_op jit(solution)/shard_map/attend_band/pallas_call | solution.py:39
  19.1 4.8 %collective-permute-done.5.refs_1_ = bf16[160,1024]{1,0:T(8,128)(2,1)S(1)} collective-permute-done((bf16[160,1024]{1,0:T(8,128)(2,1)S(1)}, bf16[160,1024]{1,0:T(8,128)(2,1)S(1)}, u32[]{:S(2)}, u32[]{:S(2)}) %collective-permute-start.5) | collective-permute-done | bytes 327712 | tf_op jit(solution)/shard_map/ppermute | solution.py:24
  24.0 0.0 collective-permute-done.4.refs_10_.inner
  24.0 3.2 %front_outer.1 = (bf16[2,256,512]{2,1,0:T(8,128)(2,1)S(1)}, bf16[128,1024]{1,0:T(8,128)(2,1)S(1)}) custom-call(bf16[160,1024]{1,0:T(8,128)(2,1)S(1)} %collective-permute-done.1.refs_0_, bf16[160,1024]{1,0:T(8,128)(2,1)S(1)} %collective-permute-done.5.refs_1_, bf16[1024,256]{1,0:T(8,128)(2,1)S(1)} %get-tuple-element.49.refs_2_, ...), custom_call_target="tpu_custom_call" | custom-call | tf_op jit(solution)/shard_map/front_outer/pallas_call | solution.py:39
  27.2 0.6 %collective-permute-start.6 = (bf16[128,1024]{1,0:T(8,128)(2,1)S(1)}, bf16[128,1024]{1,0:T(8,128)(2,1)S(1)}, u32[]{:S(2)}, u32[]{:S(2)}) collective-permute-start(bf16[128,1024]{1,0:T(8,128)(2,1)S(1)} %get-tuple-element.56), channel_id=1, source_target_pairs={{1,0},{0,1},{3,2},{2,3},{5,4},{4,5},{7,6},{6,7},{9,8},{8,9},{11,10... | collective-permute-start | bytes 786440 | tf_op jit(solution)/shard_map/ppermute | solution.py:24
  27.7 1.3 %attend_own.1 = f32[128,1024]{1,0:T(8,128)S(1)} custom-call(bf16[256,512]{1,0:T(8,128)(2,1)S(1)} %get-tuple-element.42.query.refs_7_, f32[256,512]{1,0:T(8,128)S(1)} %get-tuple-element.44.refs_8_.numer, f32[256,512]{1,0:T(8,128)S(1)} %get-tuple-element.45.refs_9_.denom, bf16[2,256,512]{2,1,0:T(8,128)(2,1)S(1)} %collective-permute-done.4.refs_10_.inner, ...), custom_call_target="tpu_custom_call" | custom-call | tf_op jit(solution)/shard_map/attend_own/pallas_call | solution.py:39
  29.0 6.4 %collective-permute-done.6 = bf16[128,1024]{1,0:T(8,128)(2,1)S(1)} collective-permute-done((bf16[128,1024]{1,0:T(8,128)(2,1)S(1)}, bf16[128,1024]{1,0:T(8,128)(2,1)S(1)}, u32[]{:S(2)}, u32[]{:S(2)}) %collective-permute-start.6) | collective-permute-done | bytes 262176 | tf_op jit(solution)/shard_map/ppermute | solution.py:24
  35.4 0.8 %add_convert_fusion = bf16[128,1024]{1,0:T(8,128)(2,1)} fusion(f32[128,1024]{1,0:T(8,128)S(1)} %attend_own.1, bf16[128,1024]{1,0:T(8,128)(2,1)S(1)} %collective-permute-done.6), kind=kLoop, calls=%fused_computation | loop fusion | flops 393216 | bytes 1048576 | tf_op jit(solution)/shard_map/convert_element_type | solution.py:319
Async XLA Ops:
  1.2 10.2 %collective-permute-start = (bf16[104,1024]{1,0:T(8,128)(2,1)S(1)}, bf16[104,1024]{1,0:T(8,128)(2,1)S(1)}, u32[]{:S(2)}, u32[]{:S(2)}) collective-permute-start(bf16[104,1024]{1,0:T(8,128)(2,1)S(1)} %get-tuple-element.31.refs_0_), channel_id=1, source_target_pairs={{1,0},{0,1},{3,2},{2,3},{5,4},{4,5},{7,6},{6,7},{9,8},{8,9},{11,10... | collective-permute-start | bytes 638984 | tf_op jit(solution)/shard_map/ppermute | solution.py:24
  4.2 9.3 %collective-permute-start.1 = (bf16[160,1024]{1,0:T(8,128)(2,1)S(1)}, bf16[160,1024]{1,0:T(8,128)(2,1)S(1)}, u32[]{:S(2)}, u32[]{:S(2)}) collective-permute-start(bf16[160,1024]{1,0:T(8,128)(2,1)S(1)} %get-tuple-element.34.refs_7_), channel_id=1, source_target_pairs={{0,30},{2,4},{4,2},{6,8},{8,6},{10,12},{12,10},{14,16},{16,14},{18... | collective-permute-start | bytes 983048 | tf_op jit(solution)/shard_map/ppermute | solution.py:33
  7.9 7.2 %collective-permute-start.3 = (bf16[128,1024]{1,0:T(8,128)(2,1)}, bf16[128,1024]{1,0:T(8,128)(2,1)S(1)}, u32[]{:S(2)}, u32[]{:S(2)}) collective-permute-start(bf16[128,1024]{1,0:T(8,128)(2,1)} %position.1), channel_id=1, source_target_pairs={{1,0},{0,1},{3,2},{2,3},{5,4},{4,5},{7,6},{6,7},{9,8},{8,9},{11,10... | collective-permute-start | bytes 786440 | tf_op jit(solution)/shard_map/ppermute | solution.py:24
  11.4 2.1 %collective-permute-start.2 = (bf16[104,1024]{1,0:T(8,128)(2,1)S(1)}, bf16[104,1024]{1,0:T(8,128)(2,1)S(1)}, u32[]{:S(2)}, u32[]{:S(2)}) collective-permute-start(bf16[104,1024]{1,0:T(8,128)(2,1)S(1)} %collective-permute-done.refs_1_), channel_id=1, source_target_pairs={{2,0},{0,2},{6,4},{4,6},{10,8},{8,10},{14,12},{12,14},{18,16},{16,... | collective-permute-start | bytes 638984 | tf_op jit(solution)/shard_map/ppermute | solution.py:28
  13.5 10.5 %collective-permute-start.5 = (bf16[160,1024]{1,0:T(8,128)(2,1)S(1)}, bf16[160,1024]{1,0:T(8,128)(2,1)S(1)}, u32[]{:S(2)}, u32[]{:S(2)}) collective-permute-start(bf16[160,1024]{1,0:T(8,128)(2,1)S(1)} %collective-permute-done.1.refs_0_), channel_id=1, source_target_pairs={{1,0},{0,1},{3,2},{2,3},{5,4},{4,5},{7,6},{6,7},{9,8},{8,9},{11,10... | collective-permute-start | bytes 983048 | tf_op jit(solution)/shard_map/ppermute | solution.py:24
  18.2 5.7 %collective-permute-start.4 = (bf16[2,256,512]{2,1,0:T(8,128)(2,1)S(1)}, bf16[2,256,512]{2,1,0:T(8,128)(2,1)S(1)}, u32[]{:S(2)}, u32[]{:S(2)}) collective-permute-start(bf16[2,256,512]{2,1,0:T(8,128)(2,1)S(1)} %get-tuple-element.43.pair), channel_id=1, source_target_pairs={{2,0},{0,2},{6,4},{4,6},{10,8},{8,10},{14,12},{12,14},{18,16},{16,... | collective-permute-start | bytes 1572872 | tf_op jit(solution)/shard_map/ppermute | solution.py:28
  27.2 8.3 %collective-permute-start.6 = (bf16[128,1024]{1,0:T(8,128)(2,1)S(1)}, bf16[128,1024]{1,0:T(8,128)(2,1)S(1)}, u32[]{:S(2)}, u32[]{:S(2)}) collective-permute-start(bf16[128,1024]{1,0:T(8,128)(2,1)S(1)} %get-tuple-element.56), channel_id=1, source_target_pairs={{1,0},{0,1},{3,2},{2,3},{5,4},{4,5},{7,6},{6,7},{9,8},{8,9},{11,10... | collective-permute-start | bytes 786440 | tf_op jit(solution)/shard_map/ppermute | solution.py:24

commit v5 on v4

--- a/solution.py
+++ b/solution.py
@@ -33,7 +33,10 @@
     return lax.ppermute(block, "band", [(i, (i + 1 if i % 2 else i - 1) % n) for i in range(n)])
 
 
-def call(body, outs, args, flops, name, spaces=None, scratch=()):
+COST = {"mix_outer": 20.0, "front_band": 0.3}
+
+
+def call(body, outs, args, name, spaces=None, scratch=()):
     spaces = spaces or [pltpu.VMEM] * len(args)
     args = [pltpu.with_memory_space_constraint(a, s) if s == pltpu.HBM else a for a, s in zip(args, spaces)]
     return pl.pallas_call(
@@ -43,7 +46,7 @@
         out_specs=[pl.BlockSpec(memory_space=pltpu.VMEM) for _ in outs],
         scratch_shapes=scratch,
         compiler_params=pltpu.CompilerParams(vmem_limit_bytes=32 * 1024 * 1024),
-        cost_estimate=pl.CostEstimate(flops=20_000_000_000 if name == "attend_band" else 0, bytes_accessed=0, transcendentals=0),
+        cost_estimate=pl.CostEstimate(flops=int(COST.get(name, 0.0) * 1e9), bytes_accessed=0, transcendentals=0),
         name=name,
     )(*args)
 
@@ -54,28 +57,31 @@
     return values, offset_values, dot(key_t, table, NT), dot(key_t, offsets, NT)
 
 
-def pack_body(table, offsets, pix, position, shared, placed, offsets_in, sems):
+def pack_body(table, offsets, pix, position, half_out, shared, first, second, offsets_in, sems):
     rows, band_tok = pix.shape
     tok, d = position.shape
     half = table.shape[0] // 2
     blocks = d // band_tok
     depth = rows // blocks
+    cut = first.shape[0] - depth
     side = lax.rem(lax.axis_index("band"), 2)
     moves = [
         (offsets, offsets_in),
-        (table.at[pl.ds(pl.multiple_of(side * half, half), half)], shared.at[pl.ds(depth, half)]),
-        (position, placed.at[pl.ds(0, tok)]),
+        (table.at[pl.ds(pl.multiple_of(side * half, half), half)], half_out),
+        (position, shared.at[pl.ds(depth, tok)]),
+        (position.at[pl.ds(0, cut)], first.at[pl.ds(depth, cut)]),
+        (position.at[pl.ds(cut, tok - cut)], second),
     ]
     for k in range(blocks):
         lanes = pl.ds(k * band_tok, band_tok)
         moves.append((pix.at[pl.ds(k * depth, depth)], shared.at[pl.ds(0, depth), lanes]))
-        moves.append((pix.at[pl.ds(k * depth, depth)], placed.at[pl.ds(tok, depth), lanes]))
+        moves.append((pix.at[pl.ds(k * depth, depth)], first.at[pl.ds(0, depth), lanes]))
     copies = [pltpu.make_async_copy(a, b, sems.at[i]) for i, (a, b) in enumerate(moves)]
     for copy in copies:
         copy.start()
     for copy in copies:
         copy.wait()
-    shared[depth + half :] = offsets_in[...]
+    shared[depth + tok :] = offsets_in[...]
 
 
 def stage_body(n_in, *refs):
@@ -93,7 +99,7 @@
         copy.wait()
 
 
-def front(pix, values, offset_values, keys, offset_keys, position):
+def aggregate(pix, values, offset_values, keys, offset_keys):
     n_heads, n_rows = keys.shape
     n_vars = offset_keys.shape[1]
     n_pix = n_rows // n_vars
@@ -118,8 +124,7 @@
         mixed = (head[:, None, :] * points).reshape(n_rows, tok).astype(BF16)
         own = slice(h * HEAD_DIM, (h + 1) * HEAD_DIM)
         merged.append(dot(values[own], mixed) + dot(offset_values[own], head.astype(BF16)))
-    merged = jnp.transpose(jnp.concatenate(merged, axis=0))
-    return merged + position.astype(F32)
+    return jnp.transpose(jnp.concatenate(merged, axis=0))
 
 
 def normalize(merged):
@@ -129,63 +134,63 @@
     return (centred * lax.rsqrt(spread + EPSILON)).astype(BF16)
 
 
-def tokens_of(packs, first_row, distance, tok, depth, band_tok):
-    start = lax.rem(lax.axis_index("var") + distance, len(packs)) * tok
-    parts = []
-    for ref in packs:
-        for k in range(ref.shape[1] // band_tok):
-            lanes = pl.ds(pl.multiple_of(k * band_tok + start, tok), tok)
-            parts.append(ref[first_row : first_row + depth, lanes])
-    return jnp.concatenate(parts, axis=0)
+def aggregates(packs, folded, tok, depth):
+    n = len(packs)
+    step = min(n, 2)
+    for r in range(0, n, step):
+        parts = []
+        for ref in packs:
+            for k in range(ref.shape[1] // (n * tok)):
+                pieces = []
+                for i in range(step):
+                    start = k * n * tok + lax.rem(lax.axis_index("var") + r + i, n) * tok
+                    pieces.append(ref[:depth, pl.ds(pl.multiple_of(start, tok), tok)])
+                parts.append(jnp.concatenate(pieces, axis=1))
+        pix = jnp.concatenate(parts, axis=0)
+        yield slice(r * tok, (r + step) * tok), aggregate(pix, *(ref[...] for ref in folded))
 
 
 def band_body(n, depth, *refs):
-    packs, far, folded = refs[:n], refs[n : 2 * n - 1], refs[2 * n - 1 : 2 * n + 3]
-    positions, (key_t, agg_value, weight) = refs[2 * n + 3 : 3 * n + 3], refs[3 * n + 3 : 3 * n + 6]
-    values, offset_values, keys, offset_keys, merged_out, query_out, pair_out, table = refs[3 * n + 6 :]
+    packs, near, far, mine = refs[:n], refs[n : 2 * n - 1], refs[2 * n - 1 : 3 * n - 2], refs[3 * n - 2 : 3 * n + 2]
+    key_t, agg_value, weight, *folded, merged_out, query_out, pair_out, table = refs[3 * n + 2 :]
+    tok = merged_out.shape[0]
     half = table.shape[0] // 2
     side = lax.rem(lax.axis_index("band"), 2)
-    parts = [tuple(ref[...] for ref in folded)]
-    for mine, other in zip(packs[1:], far):
-        table[pl.ds(pl.multiple_of(side * half, half), half)] = mine[depth : depth + half]
-        table[pl.ds(pl.multiple_of((1 - side) * half, half), half)] = other[depth : depth + half]
-        parts.append(fold(table[...], mine[depth + half :], key_t[...], agg_value[...]))
-    for out, shares in zip((values, offset_values, keys, offset_keys), zip(*parts)):
+    parts = [tuple(ref[...] for ref in mine)]
+    for pack, own, other in zip(packs[1:], near, far):
+        table[pl.ds(pl.multiple_of(side * half, half), half)] = own[...]
+        table[pl.ds(pl.multiple_of((1 - side) * half, half), half)] = other[...]
+        parts.append(fold(table[...], pack[depth + tok :], key_t[...], agg_value[...]))
+    for out, shares in zip(folded, zip(*parts)):
         out[...] = jnp.concatenate(shares, axis=1)
-    tok = merged_out.shape[0]
-    step = min(n, 2)
-    for r in range(0, n, step):
-        pix = [tokens_of(packs, 0, r + i, tok, depth, n * tok) for i in range(step)]
-        position = [positions[r + i][:tok] for i in range(step)]
-        merged = front(
-            jnp.concatenate(pix, axis=1),
-            values[...], offset_values[...], keys[...], offset_keys[...], jnp.concatenate(position, axis=0),
-        )
-        if r == 0:
+    for rows, merged in aggregates(packs, folded, tok, depth):
+        spots = packs[rows.start // tok : rows.stop // tok]
+        merged = merged + jnp.concatenate([ref[depth : depth + tok] for ref in spots], axis=0).astype(F32)
+        if rows.start == 0:
             merged_out[...] = merged[:tok]
         normed = normalize(merged)
-        rows = slice(r * tok, (r + step) * tok)
         query_out[rows] = (dot(normed, weight[0]).astype(BF16) * HEAD_DIM ** (-0.5)).astype(BF16)
         for c in range(2):
             pair_out[c, rows] = dot(normed, weight[c + 1]).astype(BF16)
 
 
+def outer_mix_body(n, depth, *refs):
+    packs, folded, out = refs[:n], refs[n:-1], refs[-1]
+    for rows, merged in aggregates(packs, folded, out.shape[0] // n, depth):
+        out[rows] = merged
+
+
 def outer_body(n, depth, *refs):
-    packs, (values, offset_values, keys, offset_keys, weight) = refs[:n], refs[n : n + 5]
-    query, numer, denom, inner, out_weight, pair_out, *share = refs[n + 5 :]
-    tok = packs[0].shape[0] - depth
+    firsts, seconds, (mixed, weight) = refs[:n], refs[n : 2 * n], refs[2 * n : 2 * n + 2]
+    query, numer, denom, inner, out_weight, pair_out, *share = refs[2 * n + 2 :]
+    tok = mixed.shape[0] // n
     step = min(n, 2)
     for r in range(0, n, step):
-        pix = [tokens_of(packs, tok, r + i, tok, depth, n * tok) for i in range(step)]
-        position = [packs[r + i][:tok] for i in range(step)]
-        normed = normalize(
-            front(
-                jnp.concatenate(pix, axis=1),
-                values[...], offset_values[...], keys[...], offset_keys[...], jnp.concatenate(position, axis=0),
-            )
-        )
+        rows = slice(r * tok, (r + step) * tok)
+        spots = [piece for i in range(r, r + step) for piece in (firsts[i][depth:], seconds[i][...])]
+        normed = normalize(mixed[rows] + jnp.concatenate(spots, axis=0).astype(F32))
         for c in range(2):
-            pair_out[c, r * tok : (r + step) * tok] = dot(normed, weight[c + 1]).astype(BF16)
+            pair_out[c, rows] = dot(normed, weight[c + 1]).astype(BF16)
     if share:
         finish_body(1, query, numer, denom, inner, pair_out, out_weight, share[0])
 
@@ -249,18 +254,19 @@
     key_t = jnp.transpose(agg_key)
     weight = jnp.transpose(qkv_weight, (1, 0, 2))
 
-    shared, placed = call(
+    cut = (tok - depth) // 2
+    half, shared, *placed = call(
         pack_body,
-        [sds((depth + rows // 2 + n_vars, d), BF16), sds((tok + depth, d), BF16)],
+        [sds((size, d), BF16) for size in (rows // 2, depth + tok + n_vars, depth + cut, tok - cut)],
         (table, variable_embed, pix, position),
-        0,
         "pack",
         [pltpu.HBM] * 4,
-        [pltpu.VMEM((n_vars, d), BF16), pltpu.SemaphoreType.DMA((3 + 2 * (d // band_tok),))],
-    )
-    near = [shifted(shared, "var", r) for r in range(1, n)]
-    outer = outward(placed)
-    positions = [shifted(position, "var", r) for r in range(1, n)]
+        [pltpu.VMEM((n_vars, d), BF16), pltpu.SemaphoreType.DMA((5 + 2 * (d // band_tok),))],
+    )
+    others = range(1, n)
+    near = [shifted(half, "var", r) for r in others]
+    first, second = (outward(x) for x in placed)
+    packs = [shared] + [shifted(shared, "var", r) for r in others]
 
     moved = (table, variable_embed, key_t, agg_value, weight, out_weight)
     key_t, agg_value, weight, out_weight, *folded = call(
@@ -268,17 +274,15 @@
         [sds(a.shape, a.dtype) for a in moved[2:]]
         + [sds((d, rows), BF16), sds((d, n_vars), BF16), sds((n_heads, rows), F32), sds((n_heads, n_vars), F32)],
         moved,
-        2 * (rows + n_vars) * d * (d + n_heads),
         "stage",
         [pltpu.HBM] * len(moved),
         [pltpu.VMEM((rows, d), BF16), pltpu.VMEM((n_vars, d), BF16), pltpu.SemaphoreType.DMA((len(moved),))],
     )
     *near, _ = lax.optimization_barrier((*near, folded[2]))
     far = [inward(x) for x in near]
-    packs = [shared] + near
-    outer, _, *far = lax.optimization_barrier((outer, folded[0], *far))
-    outers = [outer] + [shifted(outer, "var", r) for r in range(1, n)]
-    front_flops = 2 * band_tok * d * (3 * width + 2 * rows)
+    first, second, _ = lax.optimization_barrier((first, second, folded[0]))
+    firsts = [first] + [shifted(first, "var", r) for r in others]
+    seconds = [second] + [shifted(second, "var", r) for r in others]
     *folded, merged, query, pair = call(
         functools.partial(band_body, n, depth),
         [
@@ -290,29 +294,29 @@
             sds((band_tok, width), BF16),
             sds((2, band_tok, width), BF16),
         ],
-        (*packs, *far, *folded, placed, *positions, key_t, agg_value, weight),
-        2 * (n - 1) * (rows + n_vars) * d * d + front_flops,
+        (*packs, *near, *far, *folded, key_t, agg_value, weight),
         "front_band",
         scratch=[pltpu.VMEM((rows, d), BF16)],
     )
     inner = inward(pair)
-    flops = 4 * tok * band_tok * width
-    totals = call(begin_body, [sds((band_tok, width), F32)] * 2, (query, pair), n * flops, "attend_band")
-    *outers, _ = lax.optimization_barrier((*outers, totals[0]))
-    flops = 2 * flops + 2 * tok * width * d
+    totals = call(begin_body, [sds((band_tok, width), F32)] * 2, (query, pair), "attend_band")
+    *firsts, _ = lax.optimization_barrier((*firsts, totals[0]))
+    (mixed,) = call(
+        functools.partial(outer_mix_body, n, depth), [sds((band_tok, d), F32)], (*firsts, *folded), "mix_outer"
+    )
+    *seconds, mixed = lax.optimization_barrier((*seconds, mixed))
     outer_pair, *share = call(
         functools.partial(outer_body, n, depth),
         [sds((2, band_tok, width), BF16)] + [sds((tok, d), BF16)] * (n > 1),
-        (*outers, *folded, weight, query, *totals, inner, out_weight),
-        front_flops + flops,
+        (*firsts, *seconds, mixed, weight, query, *totals, inner, out_weight),
         "front_outer",
     )
     attended = (query, *totals, inner, outer_pair, out_weight)
     for r in range(2, n):
-        share += call(functools.partial(finish_body, r), [sds((tok, d), BF16)], attended, flops, "attend_later")
+        share += call(functools.partial(finish_body, r), [sds((tok, d), BF16)], attended, "attend_later")
     ending = [shifted(x, "var", n - r) for r, x in enumerate(share, 1)]
     (update,) = call(
-        functools.partial(finish_body, 0), [sds((tok, d), F32)], (*attended, merged), flops, "attend_own"
+        functools.partial(finish_body, 0), [sds((tok, d), F32)], (*attended, merged), "attend_own"
     )
     for x in ending:
         update = update + x.astype(F32)

time: 36.5 us -> 34.6 us (0.948)
  waiting for transfers between devices: 14 us -> 10.4 us
  starting transfers between devices: 8.86 us -> 10.4 us
    ppermute x4 -> x5, waiting for transfers between devices: 11.9 us -> 6.73 us  [shifted(): lax.ppermute(block, axis, [((i + distance) % n, i) for i in range(n)])]
    ppermute x1 -> x2, waiting for transfers between devices: 2.05 us -> 3.64 us  [outward(): lax.ppermute(block, 'band', [(i, (i + 1 if i % 2 else i - 1) % n) for i i...]
    ppermute x1 -> x2, starting transfers between devices: 3.69 us -> 4.44 us  [outward(): lax.ppermute(block, 'band', [(i, (i + 1 if i % 2 else i - 1) % n) for i i...]
    ppermute x4 -> x5, starting transfers between devices: 5.03 us -> 5.71 us  [shifted(): lax.ppermute(block, axis, [((i + distance) % n, i) for i in range(n)])]
    pallas_call x6 -> x7, Pallas kernels: 12.5 us -> 12.7 us  [call(): pl.pallas_call(body, out_shape=outs, in_specs=[pl.BlockSpec(memory_space=...]
  transfers between devices with their start and end apart: 7 -> 9, of which waited for: 4 -> 5; matrix products, arithmetic and copies ran while one was open for 0% -> 0% of each run, Pallas kernels for 23% -> 27%
where the time goes in v5:
time: 34.6 us; the launch traced here: 34.3 us
  Pallas kernels  12.7 us (37%)
  starting transfers between devices  10.4 us (30%)
  waiting for transfers between devices  10.4 us (30%)
  other arithmetic  0.76 us (2%)
    pallas_call x7, Pallas kernels, call(): pl.pallas_call(body, out_shape=outs, in_specs=[pl.BlockSpec(memory_space=...  12.7 us
    ppermute x5, waiting for transfers between devices, shifted(): lax.ppermute(block, axis, [((i + distance) % n, i) for i in range(n)])  6.73 us
    ppermute x5, starting transfers between devices, shifted(): lax.ppermute(block, axis, [((i + distance) % n, i) for i in range(n)])  5.71 us
    ppermute x2, starting transfers between devices, outward(): lax.ppermute(block, 'band', [(i, (i + 1 if i % 2 else i - 1) % n) for i i...  4.44 us
    ppermute x2, waiting for transfers between devices, outward(): lax.ppermute(block, 'band', [(i, (i + 1 if i % 2 else i - 1) % n) for i i...  3.64 us
    convert_element_type x1, other arithmetic, shards(): return update.astype(BF16)  0.76 us
  transfers between devices with their start and end apart: 9, of which 5 were waited for; matrix products, arithmetic and copies ran while one was open for 0% of the time, Pallas kernels for 27%

profile of v5, /device:TPU:0, one launch (start us, length us, event | category | flops | bytes accessed | tf_op | source)
XLA Modules:
  0.0 34.3 jit_solution(13352790663411181951)
XLA Ops:
  0.0 1.2 %pack.1 = (bf16[64,1024]{1,0:T(8,128)(2,1)S(1)}, bf16[168,1024]{1,0:T(8,128)(2,1)S(1)}, bf16[80,1024]{1,0:T(8,128)(2,1)S(1)}, bf16[80,1024]{1,0:T(8,128)(2,1)S(1)}) custom-call(bf16[128,1024]{1,0:T(8,128)(2,1)} %bitcast.5, bf16[8,1024]{1,0:T(8,128)(2,1)} %refs_1_.1, bf16[128,256]{1,0:T(8,128)(2,1)} %bitcast.7, bf16[128,1024]{1,0:T(8,128)(2,1)} %position.1), custom_call_target="tpu_custom_call" | custom-call | tf_op jit(solution)/shard_map/pack/pallas_call | solution.py:42
  1.3 3.0 %collective-permute-start = (bf16[168,1024]{1,0:T(8,128)(2,1)S(1)}, bf16[168,1024]{1,0:T(8,128)(2,1)S(1)}, u32[]{:S(2)}, u32[]{:S(2)}) collective-permute-start(bf16[168,1024]{1,0:T(8,128)(2,1)S(1)} %get-tuple-element.36.refs_0_), channel_id=1, source_target_pairs={{1,0},{0,1},{3,2},{2,3},{5,4},{4,5},{7,6},{6,7},{9,8},{8,9},{11,10... | collective-permute-start | bytes 1032200 | tf_op jit(solution)/shard_map/ppermute | solution.py:24
  4.3 3.7 %collective-permute-start.4 = (bf16[80,1024]{1,0:T(8,128)(2,1)S(1)}, bf16[80,1024]{1,0:T(8,128)(2,1)S(1)}, u32[]{:S(2)}, u32[]{:S(2)}) collective-permute-start(bf16[80,1024]{1,0:T(8,128)(2,1)S(1)} %get-tuple-element.50), channel_id=1, source_target_pairs={{0,30},{2,4},{4,2},{6,8},{8,6},{10,12},{12,10},{14,16},{16,14},{18... | collective-permute-start | bytes 491528 | tf_op jit(solution)/shard_map/ppermute | solution.py:33
  8.0 0.8 %collective-permute-start.5 = (bf16[80,1024]{1,0:T(8,128)(2,1)S(1)}, bf16[80,1024]{1,0:T(8,128)(2,1)S(1)}, u32[]{:S(2)}, u32[]{:S(2)}) collective-permute-start(bf16[80,1024]{1,0:T(8,128)(2,1)S(1)} %get-tuple-element.51), channel_id=1, source_target_pairs={{0,30},{2,4},{4,2},{6,8},{8,6},{10,12},{12,10},{14,16},{16,14},{18... | collective-permute-start | bytes 491528 | tf_op jit(solution)/shard_map/ppermute | solution.py:33
  8.7 0.1 collective-permute-start.1
  8.8 3.0 %stage.1 = (bf16[16,1024]{1,0:T(8,128)(2,1)S(1)}, bf16[1024,1024]{1,0:T(8,128)(2,1)S(1)}, bf16[3,1024,512]{2,1,0:T(8,128)(2,1)S(1)}, bf16[512,1024]{1,0:T(8,128)...) custom-call(bf16[128,1024]{1,0:T(8,128)(2,1)} %bitcast.6, ...), custom_call_target="tpu_custom_call" | custom-call | tf_op jit(solution)/shard_map/stage/pallas_call | solution.py:42
  11.8 0.1 collective-permute-done.4.refs_0_
  11.8 3.6 %collective-permute-done.5.refs_2_ = bf16[80,1024]{1,0:T(8,128)(2,1)S(1)} collective-permute-done((bf16[80,1024]{1,0:T(8,128)(2,1)S(1)}, bf16[80,1024]{1,0:T(8,128)(2,1)S(1)}, u32[]{:S(2)}, u32[]{:S(2)}) %collective-permute-start.5) | collective-permute-done | bytes 163872 | tf_op jit(solution)/shard_map/ppermute | solution.py:33
  15.4 0.5 %collective-permute-start.6 = (bf16[80,1024]{1,0:T(8,128)(2,1)S(1)}, bf16[80,1024]{1,0:T(8,128)(2,1)S(1)}, u32[]{:S(2)}, u32[]{:S(2)}) collective-permute-start(bf16[80,1024]{1,0:T(8,128)(2,1)S(1)} %collective-permute-done.4.refs_0_), channel_id=1, source_target_pairs={{1,0},{0,1},{3,2},{2,3},{5,4},{4,5},{7,6},{6,7},{9,8},{8,9},{11,10... | collective-permute-start | bytes 491528 | tf_op jit(solution)/shard_map/ppermute | solution.py:24
  15.9 0.0 collective-permute-done.1.refs_2_
  15.9 0.0 collective-permute-start.2
  15.9 1.5 %collective-permute-start.7 = (bf16[80,1024]{1,0:T(8,128)(2,1)S(1)}, bf16[80,1024]{1,0:T(8,128)(2,1)S(1)}, u32[]{:S(2)}, u32[]{:S(2)}) collective-permute-start(bf16[80,1024]{1,0:T(8,128)(2,1)S(1)} %collective-permute-done.5.refs_2_), channel_id=1, source_target_pairs={{1,0},{0,1},{3,2},{2,3},{5,4},{4,5},{7,6},{6,7},{9,8},{8,9},{11,10... | collective-permute-start | bytes 491528 | tf_op jit(solution)/shard_map/ppermute | solution.py:24
  17.5 0.0 collective-permute-done.2.refs_3_
  17.5 3.2 %front_band.1 = (bf16[1024,256]{1,0:T(8,128)(2,1)S(1)}, bf16[1024,16]{1,0:T(8,128)(2,1)S(1)}, f32[16,256]{1,0:T(8,128)S(1)}, f32[16,16]{1,0:T(8,128)S(1)}, f32[1...) custom-call(bf16[168,1024]{1,0:T(8,128)(2,1)S(1)} %get-tuple-element.36.refs_0_, ...), custom_call_target="tpu_custom_call" | custom-call | flops 300000000 | tf_op jit(solution)/shard_map/front_band/pallas_call | solution.py:42
  20.6 0.3 collective-permute-start.3
  20.9 0.8 %attend_band.1 = (f32[256,512]{1,0:T(8,128)S(1)}, f32[256,512]{1,0:T(8,128)S(1)}) custom-call(bf16[256,512]{1,0:T(8,128)(2,1)S(1)} %get-tuple-element.46.query.refs_6_, bf16[2,256,512]{2,1,0:T(8,128)(2,1)S(1)} %get-tuple-element.47.pair), custom_call_target="tpu_custom_call" | custom-call | tf_op jit(solution)/shard_map/attend_band/pallas_call | solution.py:42
  21.7 0.7 %collective-permute-done.6.refs_1_ = bf16[80,1024]{1,0:T(8,128)(2,1)S(1)} collective-permute-done((bf16[80,1024]{1,0:T(8,128)(2,1)S(1)}, bf16[80,1024]{1,0:T(8,128)(2,1)S(1)}, u32[]{:S(2)}, u32[]{:S(2)}) %collective-permute-start.6) | collective-permute-done | bytes 163872 | tf_op jit(solution)/shard_map/ppermute | solution.py:24
  22.4 1.1 %mix_outer.1.refs_4_ = f32[256,1024]{1,0:T(8,128)S(1)} custom-call(bf16[80,1024]{1,0:T(8,128)(2,1)S(1)} %collective-permute-done.4.refs_0_, bf16[80,1024]{1,0:T(8,128)(2,1)S(1)} %collective-permute-done.6.refs_1_, bf16[1024,256]{1,0:T(8,128)(2,1)S(1)} %get-tuple-element.56.refs_2_, bf16[1024,16]{1,0:T(8,128)(2,1)S(1)} %get-tuple-element.57.refs_3_, ...), custom_call_target="tpu_custom_call" | custom-call | flops 20000000000 | tf_op jit(solution)/shard_map/mix_outer/pallas_call | solution.py:42
  23.5 0.7 %collective-permute-done.7.refs_3_ = bf16[80,1024]{1,0:T(8,128)(2,1)S(1)} collective-permute-done((bf16[80,1024]{1,0:T(8,128)(2,1)S(1)}, bf16[80,1024]{1,0:T(8,128)(2,1)S(1)}, u32[]{:S(2)}, u32[]{:S(2)}) %collective-permute-start.7) | collective-permute-done | bytes 163872 | tf_op jit(solution)/shard_map/ppermute | solution.py:24
  24.3 2.1 %front_outer.1 = (bf16[2,256,512]{2,1,0:T(8,128)(2,1)S(1)}, bf16[128,1024]{1,0:T(8,128)(2,1)S(1)}) custom-call(bf16[80,1024]{1,0:T(8,128)(2,1)S(1)} %collective-permute-done.4.refs_0_, bf16[80,1024]{1,0:T(8,128)(2,1)S(1)} %collective-permute-done.6.refs_1_, bf16[80,1024]{1,0:T(8,128)(2,1)S(1)} %collective-permute-done.5.refs_2_, ...), custom_call_target="tpu_custom_call" | custom-call | tf_op jit(solution)/shard_map/front_outer/pallas_call | solution.py:42
  26.4 0.6 %collective-permute-start.8 = (bf16[128,1024]{1,0:T(8,128)(2,1)S(1)}, bf16[128,1024]{1,0:T(8,128)(2,1)S(1)}, u32[]{:S(2)}, u32[]{:S(2)}) collective-permute-start(bf16[128,1024]{1,0:T(8,128)(2,1)S(1)} %get-tuple-element.66), channel_id=1, source_target_pairs={{1,0},{0,1},{3,2},{2,3},{5,4},{4,5},{7,6},{6,7},{9,8},{8,9},{11,10... | collective-permute-start | bytes 786440 | tf_op jit(solution)/shard_map/ppermute | solution.py:24
  27.0 1.3 %attend_own.1 = f32[128,1024]{1,0:T(8,128)S(1)} custom-call(bf16[256,512]{1,0:T(8,128)(2,1)S(1)} %get-tuple-element.46.query.refs_6_, f32[256,512]{1,0:T(8,128)S(1)} %get-tuple-element.48.refs_7_.numer, f32[256,512]{1,0:T(8,128)S(1)} %get-tuple-element.49.refs_8_.denom, bf16[2,256,512]{2,1,0:T(8,128)(2,1)S(1)} %collective-permute-done.3.refs_9_.inner, ...), custom_call_target="tpu_custom_call" | custom-call | tf_op jit(solution)/shard_map/attend_own/pallas_call | solution.py:42
  28.2 5.3 %collective-permute-done.8 = bf16[128,1024]{1,0:T(8,128)(2,1)S(1)} collective-permute-done((bf16[128,1024]{1,0:T(8,128)(2,1)S(1)}, bf16[128,1024]{1,0:T(8,128)(2,1)S(1)}, u32[]{:S(2)}, u32[]{:S(2)}) %collective-permute-start.8) | collective-permute-done | bytes 262176 | tf_op jit(solution)/shard_map/ppermute | solution.py:24
  33.5 0.8 %add_convert_fusion = bf16[128,1024]{1,0:T(8,128)(2,1)} fusion(f32[128,1024]{1,0:T(8,128)S(1)} %attend_own.1, bf16[128,1024]{1,0:T(8,128)(2,1)S(1)} %collective-permute-done.8), kind=kLoop, calls=%fused_computation | loop fusion | flops 393216 | bytes 1048576 | tf_op jit(solution)/shard_map/convert_element_type | solution.py:323
  (2 shorter events, 0.0 us)
Async XLA Ops:
  1.3 16.2 %collective-permute-start = (bf16[168,1024]{1,0:T(8,128)(2,1)S(1)}, bf16[168,1024]{1,0:T(8,128)(2,1)S(1)}, u32[]{:S(2)}, u32[]{:S(2)}) collective-permute-start(bf16[168,1024]{1,0:T(8,128)(2,1)S(1)} %get-tuple-element.36.refs_0_), channel_id=1, source_target_pairs={{1,0},{0,1},{3,2},{2,3},{5,4},{4,5},{7,6},{6,7},{9,8},{8,9},{11,10... | collective-permute-start | bytes 1032200 | tf_op jit(solution)/shard_map/ppermute | solution.py:24
  4.3 7.5 %collective-permute-start.4 = (bf16[80,1024]{1,0:T(8,128)(2,1)S(1)}, bf16[80,1024]{1,0:T(8,128)(2,1)S(1)}, u32[]{:S(2)}, u32[]{:S(2)}) collective-permute-start(bf16[80,1024]{1,0:T(8,128)(2,1)S(1)} %get-tuple-element.50), channel_id=1, source_target_pairs={{0,30},{2,4},{4,2},{6,8},{8,6},{10,12},{12,10},{14,16},{16,14},{18... | collective-permute-start | bytes 491528 | tf_op jit(solution)/shard_map/ppermute | solution.py:33
  8.0 7.4 %collective-permute-start.5 = (bf16[80,1024]{1,0:T(8,128)(2,1)S(1)}, bf16[80,1024]{1,0:T(8,128)(2,1)S(1)}, u32[]{:S(2)}, u32[]{:S(2)}) collective-permute-start(bf16[80,1024]{1,0:T(8,128)(2,1)S(1)} %get-tuple-element.51), channel_id=1, source_target_pairs={{0,30},{2,4},{4,2},{6,8},{8,6},{10,12},{12,10},{14,16},{16,14},{18... | collective-permute-start | bytes 491528 | tf_op jit(solution)/shard_map/ppermute | solution.py:33
  8.7 7.2 %collective-permute-start.1 = (bf16[64,1024]{1,0:T(8,128)(2,1)S(1)}, bf16[64,1024]{1,0:T(8,128)(2,1)S(1)}, u32[]{:S(2)}, u32[]{:S(2)}) collective-permute-start(bf16[64,1024]{1,0:T(8,128)(2,1)S(1)} %get-tuple-element.37), channel_id=1, source_target_pairs={{1,0},{0,1},{3,2},{2,3},{5,4},{4,5},{7,6},{6,7},{9,8},{8,9},{11,10... | collective-permute-start | bytes 393224 | tf_op jit(solution)/shard_map/ppermute | solution.py:24
  15.4 7.0 %collective-permute-start.6 = (bf16[80,1024]{1,0:T(8,128)(2,1)S(1)}, bf16[80,1024]{1,0:T(8,128)(2,1)S(1)}, u32[]{:S(2)}, u32[]{:S(2)}) collective-permute-start(bf16[80,1024]{1,0:T(8,128)(2,1)S(1)} %collective-permute-done.4.refs_0_), channel_id=1, source_target_pairs={{1,0},{0,1},{3,2},{2,3},{5,4},{4,5},{7,6},{6,7},{9,8},{8,9},{11,10... | collective-permute-start | bytes 491528 | tf_op jit(solution)/shard_map/ppermute | solution.py:24
  15.9 1.5 %collective-permute-start.2 = (bf16[64,1024]{1,0:T(8,128)(2,1)S(1)}, bf16[64,1024]{1,0:T(8,128)(2,1)S(1)}, u32[]{:S(2)}, u32[]{:S(2)}) collective-permute-start(bf16[64,1024]{1,0:T(8,128)(2,1)S(1)} %collective-permute-done.1.refs_2_), channel_id=1, source_target_pairs={{2,0},{0,2},{6,4},{4,6},{10,8},{8,10},{14,12},{12,14},{18,16},{16,... | collective-permute-start | bytes 393224 | tf_op jit(solution)/shard_map/ppermute | solution.py:28
  15.9 8.3 %collective-permute-start.7 = (bf16[80,1024]{1,0:T(8,128)(2,1)S(1)}, bf16[80,1024]{1,0:T(8,128)(2,1)S(1)}, u32[]{:S(2)}, u32[]{:S(2)}) collective-permute-start(bf16[80,1024]{1,0:T(8,128)(2,1)S(1)} %collective-permute-done.5.refs_2_), channel_id=1, source_target_pairs={{1,0},{0,1},{3,2},{2,3},{5,4},{4,5},{7,6},{6,7},{9,8},{8,9},{11,10... | collective-permute-start | bytes 491528 | tf_op jit(solution)/shard_map/ppermute | solution.py:24
  20.6 3.6 %collective-permute-start.3 = (bf16[2,256,512]{2,1,0:T(8,128)(2,1)S(1)}, bf16[2,256,512]{2,1,0:T(8,128)(2,1)S(1)}, u32[]{:S(2)}, u32[]{:S(2)}) collective-permute-start(bf16[2,256,512]{2,1,0:T(8,128)(2,1)S(1)} %get-tuple-element.47.pair), channel_id=1, source_target_pairs={{2,0},{0,2},{6,4},{4,6},{10,8},{8,10},{14,12},{12,14},{18,16},{16,... | collective-permute-start | bytes 1572872 | tf_op jit(solution)/shard_map/ppermute | solution.py:28
  26.4 7.2 %collective-permute-start.8 = (bf16[128,1024]{1,0:T(8,128)(2,1)S(1)}, bf16[128,1024]{1,0:T(8,128)(2,1)S(1)}, u32[]{:S(2)}, u32[]{:S(2)}) collective-permute-start(bf16[128,1024]{1,0:T(8,128)(2,1)S(1)} %get-tuple-element.66), channel_id=1, source_target_pairs={{1,0},{0,1},{3,2},{2,3},{5,4},{4,5},{7,6},{6,7},{9,8},{8,9},{11,10... | collective-permute-start | bytes 786440 | tf_op jit(solution)/shard_map/ppermute | solution.py:24

commit v6 on v5

--- a/solution.py
+++ b/solution.py
@@ -57,7 +57,7 @@
     return values, offset_values, dot(key_t, table, NT), dot(key_t, offsets, NT)
 
 
-def pack_body(table, offsets, pix, position, half_out, shared, first, second, offsets_in, sems):
+def pack_body(table, offsets, pix, position, shared, first, second, offsets_in, sems):
     rows, band_tok = pix.shape
     tok, d = position.shape
     half = table.shape[0] // 2
@@ -67,8 +67,7 @@
     side = lax.rem(lax.axis_index("band"), 2)
     moves = [
         (offsets, offsets_in),
-        (table.at[pl.ds(pl.multiple_of(side * half, half), half)], half_out),
-        (position, shared.at[pl.ds(depth, tok)]),
+        (table.at[pl.ds(pl.multiple_of(side * half, half), half)], shared.at[pl.ds(depth, half)]),
         (position.at[pl.ds(0, cut)], first.at[pl.ds(depth, cut)]),
         (position.at[pl.ds(cut, tok - cut)], second),
     ]
@@ -81,7 +80,7 @@
         copy.start()
     for copy in copies:
         copy.wait()
-    shared[depth + tok :] = offsets_in[...]
+    shared[depth + half :] = offsets_in[...]
 
 
 def stage_body(n_in, *refs):
@@ -151,21 +150,22 @@
 
 
 def band_body(n, depth, *refs):
-    packs, near, far, mine = refs[:n], refs[n : 2 * n - 1], refs[2 * n - 1 : 3 * n - 2], refs[3 * n - 2 : 3 * n + 2]
-    key_t, agg_value, weight, *folded, merged_out, query_out, pair_out, table = refs[3 * n + 2 :]
+    packs, far, mine = refs[:n], refs[n : 2 * n - 1], refs[2 * n - 1 : 2 * n + 3]
+    positions, (key_t, agg_value, weight) = refs[2 * n + 3 : 3 * n + 3], refs[3 * n + 3 : 3 * n + 6]
+    *folded, merged_out, query_out, pair_out, table = refs[3 * n + 6 :]
     tok = merged_out.shape[0]
     half = table.shape[0] // 2
     side = lax.rem(lax.axis_index("band"), 2)
     parts = [tuple(ref[...] for ref in mine)]
-    for pack, own, other in zip(packs[1:], near, far):
-        table[pl.ds(pl.multiple_of(side * half, half), half)] = own[...]
+    for pack, other in zip(packs[1:], far):
+        table[pl.ds(pl.multiple_of(side * half, half), half)] = pack[depth : depth + half]
         table[pl.ds(pl.multiple_of((1 - side) * half, half), half)] = other[...]
-        parts.append(fold(table[...], pack[depth + tok :], key_t[...], agg_value[...]))
+        parts.append(fold(table[...], pack[depth + half :], key_t[...], agg_value[...]))
     for out, shares in zip(folded, zip(*parts)):
         out[...] = jnp.concatenate(shares, axis=1)
     for rows, merged in aggregates(packs, folded, tok, depth):
-        spots = packs[rows.start // tok : rows.stop // tok]
-        merged = merged + jnp.concatenate([ref[depth : depth + tok] for ref in spots], axis=0).astype(F32)
+        spots = positions[rows.start // tok : rows.stop // tok]
+        merged = merged + jnp.concatenate([ref[...] for ref in spots], axis=0).astype(F32)
         if rows.start == 0:
             merged_out[...] = merged[:tok]
         normed = normalize(merged)
@@ -255,21 +255,21 @@
     weight = jnp.transpose(qkv_weight, (1, 0, 2))
 
     cut = (tok - depth) // 2
-    half, shared, *placed = call(
+    shared, *placed = call(
         pack_body,
-        [sds((size, d), BF16) for size in (rows // 2, depth + tok + n_vars, depth + cut, tok - cut)],
+        [sds((size, d), BF16) for size in (depth + rows // 2 + n_vars, depth + cut, tok - cut)],
         (table, variable_embed, pix, position),
         "pack",
         [pltpu.HBM] * 4,
-        [pltpu.VMEM((n_vars, d), BF16), pltpu.SemaphoreType.DMA((5 + 2 * (d // band_tok),))],
+        [pltpu.VMEM((n_vars, d), BF16), pltpu.SemaphoreType.DMA((4 + 2 * (d // band_tok),))],
     )
     others = range(1, n)
-    near = [shifted(half, "var", r) for r in others]
+    near = [shifted(shared, "var", r) for r in others]
     first, second = (outward(x) for x in placed)
-    packs = [shared] + [shifted(shared, "var", r) for r in others]
-
-    moved = (table, variable_embed, key_t, agg_value, weight, out_weight)
-    key_t, agg_value, weight, out_weight, *folded = call(
+    positions = [shifted(position, "var", r) for r in others]
+
+    moved = (table, variable_embed, key_t, agg_value, weight, out_weight, position)
+    key_t, agg_value, weight, out_weight, position, *folded = call(
         functools.partial(stage_body, len(moved)),
         [sds(a.shape, a.dtype) for a in moved[2:]]
         + [sds((d, rows), BF16), sds((d, n_vars), BF16), sds((n_heads, rows), F32), sds((n_heads, n_vars), F32)],
@@ -278,9 +278,11 @@
         [pltpu.HBM] * len(moved),
         [pltpu.VMEM((rows, d), BF16), pltpu.VMEM((n_vars, d), BF16), pltpu.SemaphoreType.DMA((len(moved),))],
     )
-    *near, _ = lax.optimization_barrier((*near, folded[2]))
-    far = [inward(x) for x in near]
-    first, second, _ = lax.optimization_barrier((first, second, folded[0]))
+    near, positions, _ = lax.optimization_barrier((near, positions, folded[2]))
+    packs = [shared] + near
+    far = [inward(x[depth : depth + rows // 2]) for x in near]
+    first, _ = lax.optimization_barrier((first, folded[0]))
+    second, _ = lax.optimization_barrier((second, folded[1]))
     firsts = [first] + [shifted(first, "var", r) for r in others]
     seconds = [second] + [shifted(second, "var", r) for r in others]
     *folded, merged, query, pair = call(
@@ -294,7 +296,7 @@
             sds((band_tok, width), BF16),
             sds((2, band_tok, width), BF16),
         ],
-        (*packs, *near, *far, *folded, key_t, agg_value, weight),
+        (*packs, *far, *folded, position, *positions, key_t, agg_value, weight),
         "front_band",
         scratch=[pltpu.VMEM((rows, d), BF16)],
     )

time: 34.6 us -> 34.3 us (level)
  waiting for transfers between devices: 10.4 us -> 8.36 us
  starting transfers between devices: 10.4 us -> 12.1 us
    ppermute x2, waiting for transfers between devices: 3.64 us -> 1.53 us  [outward(): lax.ppermute(block, 'band', [(i, (i + 1 if i % 2 else i - 1) % n) for i i...]
    ppermute x5, starting transfers between devices: 5.71 us -> 7.46 us  [shifted(): lax.ppermute(block, axis, [((i + distance) % n, i) for i in range(n)])]
  transfers between devices with their start and end apart: 9 -> 9, of which waited for: 5 -> 4; matrix products, arithmetic and copies ran while one was open for 0% -> 0% of each run, Pallas kernels for 27% -> 31%
where the time goes in v6:
time: 34.3 us; the launch traced here: 34 us
  Pallas kernels  12.7 us (37%)
  starting transfers between devices  12.1 us (35%)
  waiting for transfers between devices  8.36 us (24%)
  other arithmetic  0.76 us (2%)
    pallas_call x7, Pallas kernels, call(): pl.pallas_call(body, out_shape=outs, in_specs=[pl.BlockSpec(memory_space=...  12.7 us
    ppermute x5, starting transfers between devices, shifted(): lax.ppermute(block, axis, [((i + distance) % n, i) for i in range(n)])  7.46 us
    ppermute x5, waiting for transfers between devices, shifted(): lax.ppermute(block, axis, [((i + distance) % n, i) for i in range(n)])  6.83 us
    ppermute x2, starting transfers between devices, outward(): lax.ppermute(block, 'band', [(i, (i + 1 if i % 2 else i - 1) % n) for i i...  4.51 us
    ppermute x2, waiting for transfers between devices, outward(): lax.ppermute(block, 'band', [(i, (i + 1 if i % 2 else i - 1) % n) for i i...  1.53 us
    convert_element_type x1, other arithmetic, shards(): return update.astype(BF16)  0.76 us
  transfers between devices with their start and end apart: 9, of which 4 were waited for; matrix products, arithmetic and copies ran while one was open for 0% of the time, Pallas kernels for 31%

profile of v6, /device:TPU:0, one launch (start us, length us, event | category | flops | bytes accessed | tf_op | source)
XLA Modules:
  0.0 34.0 jit_solution(5550126095702538164)
XLA Ops:
  0.0 3.0 %collective-permute-start.1 = (bf16[128,1024]{1,0:T(8,128)(2,1)}, bf16[128,1024]{1,0:T(8,128)(2,1)S(1)}, u32[]{:S(2)}, u32[]{:S(2)}) collective-permute-start(bf16[128,1024]{1,0:T(8,128)(2,1)} %refs_6_.1), channel_id=1, source_target_pairs={{1,0},{0,1},{3,2},{2,3},{5,4},{4,5},{7,6},{6,7},{9,8},{8,9},{11,10... | collective-permute-start | bytes 786440 | tf_op jit(solution)/shard_map/ppermute | solution.py:24
  3.0 1.2 %pack.1 = (bf16[104,1024]{1,0:T(8,128)(2,1)S(1)}, bf16[80,1024]{1,0:T(8,128)(2,1)S(1)}, bf16[80,1024]{1,0:T(8,128)(2,1)S(1)}) custom-call(bf16[128,1024]{1,0:T(8,128)(2,1)} %bitcast.5, bf16[8,1024]{1,0:T(8,128)(2,1)} %refs_1_.1, bf16[128,256]{1,0:T(8,128)(2,1)} %bitcast.7, bf16[128,1024]{1,0:T(8,128)(2,1)} %refs_6_.1), custom_call_target="tpu_custom_call" | custom-call | tf_op jit(solution)/shard_map/pack/pallas_call | solution.py:42
  4.1 0.1 collective-permute-start
  4.2 3.9 %collective-permute-start.4 = (bf16[80,1024]{1,0:T(8,128)(2,1)S(1)}, bf16[80,1024]{1,0:T(8,128)(2,1)S(1)}, u32[]{:S(2)}, u32[]{:S(2)}) collective-permute-start(bf16[80,1024]{1,0:T(8,128)(2,1)S(1)} %get-tuple-element.52), channel_id=1, source_target_pairs={{0,30},{2,4},{4,2},{6,8},{8,6},{10,12},{12,10},{14,16},{16,14},{18... | collective-permute-start | bytes 491528 | tf_op jit(solution)/shard_map/ppermute | solution.py:33
  8.1 0.6 %collective-permute-start.6 = (bf16[80,1024]{1,0:T(8,128)(2,1)S(1)}, bf16[80,1024]{1,0:T(8,128)(2,1)S(1)}, u32[]{:S(2)}, u32[]{:S(2)}) collective-permute-start(bf16[80,1024]{1,0:T(8,128)(2,1)S(1)} %get-tuple-element.56), channel_id=1, source_target_pairs={{0,30},{2,4},{4,2},{6,8},{8,6},{10,12},{12,10},{14,16},{16,14},{18... | collective-permute-start | bytes 491528 | tf_op jit(solution)/shard_map/ppermute | solution.py:33
  8.7 3.0 %stage.1 = (bf16[16,1024]{1,0:T(8,128)(2,1)S(1)}, bf16[1024,1024]{1,0:T(8,128)(2,1)S(1)}, bf16[3,1024,512]{2,1,0:T(8,128)(2,1)S(1)}, bf16[512,1024]{1,0:T(8,128)...) custom-call(bf16[128,1024]{1,0:T(8,128)(2,1)} %bitcast.6, ...), custom_call_target="tpu_custom_call" | custom-call | tf_op jit(solution)/shard_map/stage/pallas_call | solution.py:42
  11.7 0.1 collective-permute-done.4.refs_0_
  11.8 1.9 %collective-permute-start.5 = (bf16[80,1024]{1,0:T(8,128)(2,1)S(1)}, bf16[80,1024]{1,0:T(8,128)(2,1)S(1)}, u32[]{:S(2)}, u32[]{:S(2)}) collective-permute-start(bf16[80,1024]{1,0:T(8,128)(2,1)S(1)} %collective-permute-done.4.refs_0_), channel_id=1, source_target_pairs={{1,0},{0,1},{3,2},{2,3},{5,4},{4,5},{7,6},{6,7},{9,8},{8,9},{11,10... | collective-permute-start | bytes 491528 | tf_op jit(solution)/shard_map/ppermute | solution.py:24
  13.8 0.3 collective-permute-done.refs_1_
  14.0 0.0 collective-permute-done.1.refs_8_
  14.1 0.1 collective-permute-start.2
  14.1 1.4 %collective-permute-done.6.refs_2_ = bf16[80,1024]{1,0:T(8,128)(2,1)S(1)} collective-permute-done((bf16[80,1024]{1,0:T(8,128)(2,1)S(1)}, bf16[80,1024]{1,0:T(8,128)(2,1)S(1)}, u32[]{:S(2)}, u32[]{:S(2)}) %collective-permute-start.6) | collective-permute-done | bytes 163872 | tf_op jit(solution)/shard_map/ppermute | solution.py:33
  15.6 1.5 %collective-permute-start.7 = (bf16[80,1024]{1,0:T(8,128)(2,1)S(1)}, bf16[80,1024]{1,0:T(8,128)(2,1)S(1)}, u32[]{:S(2)}, u32[]{:S(2)}) collective-permute-start(bf16[80,1024]{1,0:T(8,128)(2,1)S(1)} %collective-permute-done.6.refs_2_), channel_id=1, source_target_pairs={{1,0},{0,1},{3,2},{2,3},{5,4},{4,5},{7,6},{6,7},{9,8},{8,9},{11,10... | collective-permute-start | bytes 491528 | tf_op jit(solution)/shard_map/ppermute | solution.py:24
  17.1 3.2 %front_band.1 = (bf16[1024,256]{1,0:T(8,128)(2,1)S(1)}, bf16[1024,16]{1,0:T(8,128)(2,1)S(1)}, f32[16,256]{1,0:T(8,128)S(1)}, f32[16,16]{1,0:T(8,128)S(1)}, f32[1...) custom-call(bf16[104,1024]{1,0:T(8,128)(2,1)S(1)} %get-tuple-element.37.refs_0_, ...), custom_call_target="tpu_custom_call" | custom-call | flops 300000000 | tf_op jit(solution)/shard_map/front_band/pallas_call | solution.py:42
  20.3 0.1 collective-permute-start.3
  20.4 0.8 %attend_band.1 = (f32[256,512]{1,0:T(8,128)S(1)}, f32[256,512]{1,0:T(8,128)S(1)}) custom-call(bf16[256,512]{1,0:T(8,128)(2,1)S(1)} %get-tuple-element.48.query.refs_6_, bf16[2,256,512]{2,1,0:T(8,128)(2,1)S(1)} %get-tuple-element.49.pair), custom_call_target="tpu_custom_call" | custom-call | tf_op jit(solution)/shard_map/attend_band/pallas_call | solution.py:42
  21.2 0.0 collective-permute-done.5.refs_1_
  21.2 1.1 %mix_outer.1.refs_4_ = f32[256,1024]{1,0:T(8,128)S(1)} custom-call(bf16[80,1024]{1,0:T(8,128)(2,1)S(1)} %collective-permute-done.4.refs_0_, bf16[80,1024]{1,0:T(8,128)(2,1)S(1)} %collective-permute-done.5.refs_1_, bf16[1024,256]{1,0:T(8,128)(2,1)S(1)} %get-tuple-element.58.refs_2_, bf16[1024,16]{1,0:T(8,128)(2,1)S(1)} %get-tuple-element.59.refs_3_, ...), custom_call_target="tpu_custom_call" | custom-call | flops 20000000000 | tf_op jit(solution)/shard_map/mix_outer/pallas_call | solution.py:42
  22.3 0.0 collective-permute-done.7.refs_3_
  22.3 2.1 %front_outer.1 = (bf16[2,256,512]{2,1,0:T(8,128)(2,1)S(1)}, bf16[128,1024]{1,0:T(8,128)(2,1)S(1)}) custom-call(bf16[80,1024]{1,0:T(8,128)(2,1)S(1)} %collective-permute-done.4.refs_0_, bf16[80,1024]{1,0:T(8,128)(2,1)S(1)} %collective-permute-done.5.refs_1_, bf16[80,1024]{1,0:T(8,128)(2,1)S(1)} %collective-permute-done.6.refs_2_, ...), custom_call_target="tpu_custom_call" | custom-call | tf_op jit(solution)/shard_map/front_outer/pallas_call | solution.py:42
  24.5 1.0 %collective-permute-start.8 = (bf16[128,1024]{1,0:T(8,128)(2,1)S(1)}, bf16[128,1024]{1,0:T(8,128)(2,1)S(1)}, u32[]{:S(2)}, u32[]{:S(2)}) collective-permute-start(bf16[128,1024]{1,0:T(8,128)(2,1)S(1)} %get-tuple-element.68), channel_id=1, source_target_pairs={{1,0},{0,1},{3,2},{2,3},{5,4},{4,5},{7,6},{6,7},{9,8},{8,9},{11,10... | collective-permute-start | bytes 786440 | tf_op jit(solution)/shard_map/ppermute | solution.py:24
  25.4 1.3 %attend_own.1 = f32[128,1024]{1,0:T(8,128)S(1)} custom-call(bf16[256,512]{1,0:T(8,128)(2,1)S(1)} %get-tuple-element.48.query.refs_6_, f32[256,512]{1,0:T(8,128)S(1)} %get-tuple-element.50.refs_7_.numer, f32[256,512]{1,0:T(8,128)S(1)} %get-tuple-element.51.refs_8_.denom, bf16[2,256,512]{2,1,0:T(8,128)(2,1)S(1)} %collective-permute-done.3.refs_9_.inner, ...), custom_call_target="tpu_custom_call" | custom-call | tf_op jit(solution)/shard_map/attend_own/pallas_call | solution.py:42
  26.7 6.5 %collective-permute-done.8 = bf16[128,1024]{1,0:T(8,128)(2,1)S(1)} collective-permute-done((bf16[128,1024]{1,0:T(8,128)(2,1)S(1)}, bf16[128,1024]{1,0:T(8,128)(2,1)S(1)}, u32[]{:S(2)}, u32[]{:S(2)}) %collective-permute-start.8) | collective-permute-done | bytes 262176 | tf_op jit(solution)/shard_map/ppermute | solution.py:24
  33.3 0.8 %add_convert_fusion = bf16[128,1024]{1,0:T(8,128)(2,1)} fusion(f32[128,1024]{1,0:T(8,128)S(1)} %attend_own.1, bf16[128,1024]{1,0:T(8,128)(2,1)S(1)} %collective-permute-done.8), kind=kLoop, calls=%fused_computation | loop fusion | flops 393216 | bytes 1048576 | tf_op jit(solution)/shard_map/convert_element_type | solution.py:325
  (3 shorter events, 0.0 us)
Async XLA Ops:
  0.0 14.0 %collective-permute-start.1 = (bf16[128,1024]{1,0:T(8,128)(2,1)}, bf16[128,1024]{1,0:T(8,128)(2,1)S(1)}, u32[]{:S(2)}, u32[]{:S(2)}) collective-permute-start(bf16[128,1024]{1,0:T(8,128)(2,1)} %refs_6_.1), channel_id=1, source_target_pairs={{1,0},{0,1},{3,2},{2,3},{5,4},{4,5},{7,6},{6,7},{9,8},{8,9},{11,10... | collective-permute-start | bytes 786440 | tf_op jit(solution)/shard_map/ppermute | solution.py:24
  4.1 9.9 %collective-permute-start = (bf16[104,1024]{1,0:T(8,128)(2,1)S(1)}, bf16[104,1024]{1,0:T(8,128)(2,1)S(1)}, u32[]{:S(2)}, u32[]{:S(2)}) collective-permute-start(bf16[104,1024]{1,0:T(8,128)(2,1)S(1)} %get-tuple-element.37.refs_0_), channel_id=1, source_target_pairs={{1,0},{0,1},{3,2},{2,3},{5,4},{4,5},{7,6},{6,7},{9,8},{8,9},{11,10... | collective-permute-start | bytes 638984 | tf_op jit(solution)/shard_map/ppermute | solution.py:24
  4.2 7.6 %collective-permute-start.4 = (bf16[80,1024]{1,0:T(8,128)(2,1)S(1)}, bf16[80,1024]{1,0:T(8,128)(2,1)S(1)}, u32[]{:S(2)}, u32[]{:S(2)}) collective-permute-start(bf16[80,1024]{1,0:T(8,128)(2,1)S(1)} %get-tuple-element.52), channel_id=1, source_target_pairs={{0,30},{2,4},{4,2},{6,8},{8,6},{10,12},{12,10},{14,16},{16,14},{18... | collective-permute-start | bytes 491528 | tf_op jit(solution)/shard_map/ppermute | solution.py:33
  8.1 7.4 %collective-permute-start.6 = (bf16[80,1024]{1,0:T(8,128)(2,1)S(1)}, bf16[80,1024]{1,0:T(8,128)(2,1)S(1)}, u32[]{:S(2)}, u32[]{:S(2)}) collective-permute-start(bf16[80,1024]{1,0:T(8,128)(2,1)S(1)} %get-tuple-element.56), channel_id=1, source_target_pairs={{0,30},{2,4},{4,2},{6,8},{8,6},{10,12},{12,10},{14,16},{16,14},{18... | collective-permute-start | bytes 491528 | tf_op jit(solution)/shard_map/ppermute | solution.py:33
  11.8 9.4 %collective-permute-start.5 = (bf16[80,1024]{1,0:T(8,128)(2,1)S(1)}, bf16[80,1024]{1,0:T(8,128)(2,1)S(1)}, u32[]{:S(2)}, u32[]{:S(2)}) collective-permute-start(bf16[80,1024]{1,0:T(8,128)(2,1)S(1)} %collective-permute-done.4.refs_0_), channel_id=1, source_target_pairs={{1,0},{0,1},{3,2},{2,3},{5,4},{4,5},{7,6},{6,7},{9,8},{8,9},{11,10... | collective-permute-start | bytes 491528 | tf_op jit(solution)/shard_map/ppermute | solution.py:24
  14.1 3.0 %collective-permute-start.2 = (bf16[64,1024]{1,0:T(8,128)(2,1)S(1)}, bf16[64,1024]{1,0:T(8,128)(2,1)S(1)}, u32[]{:S(2)}, u32[]{:S(2)}) collective-permute-start(bf16[64,1024]{1,0:T(8,128)(2,1)S(1)} %slice.3), channel_id=1, source_target_pairs={{2,0},{0,2},{6,4},{4,6},{10,8},{8,10},{14,12},{12,14},{18,16},{16,... | collective-permute-start | bytes 393224 | tf_op jit(solution)/shard_map/ppermute | solution.py:28
  15.6 6.8 %collective-permute-start.7 = (bf16[80,1024]{1,0:T(8,128)(2,1)S(1)}, bf16[80,1024]{1,0:T(8,128)(2,1)S(1)}, u32[]{:S(2)}, u32[]{:S(2)}) collective-permute-start(bf16[80,1024]{1,0:T(8,128)(2,1)S(1)} %collective-permute-done.6.refs_2_), channel_id=1, source_target_pairs={{1,0},{0,1},{3,2},{2,3},{5,4},{4,5},{7,6},{6,7},{9,8},{8,9},{11,10... | collective-permute-start | bytes 491528 | tf_op jit(solution)/shard_map/ppermute | solution.py:24
  20.3 2.0 %collective-permute-start.3 = (bf16[2,256,512]{2,1,0:T(8,128)(2,1)S(1)}, bf16[2,256,512]{2,1,0:T(8,128)(2,1)S(1)}, u32[]{:S(2)}, u32[]{:S(2)}) collective-permute-start(bf16[2,256,512]{2,1,0:T(8,128)(2,1)S(1)} %get-tuple-element.49.pair), channel_id=1, source_target_pairs={{2,0},{0,2},{6,4},{4,6},{10,8},{8,10},{14,12},{12,14},{18,16},{16,... | collective-permute-start | bytes 1572872 | tf_op jit(solution)/shard_map/ppermute | solution.py:28
  24.5 8.8 %collective-permute-start.8 = (bf16[128,1024]{1,0:T(8,128)(2,1)S(1)}, bf16[128,1024]{1,0:T(8,128)(2,1)S(1)}, u32[]{:S(2)}, u32[]{:S(2)}) collective-permute-start(bf16[128,1024]{1,0:T(8,128)(2,1)S(1)} %get-tuple-element.68), channel_id=1, source_target_pairs={{1,0},{0,1},{3,2},{2,3},{5,4},{4,5},{7,6},{6,7},{9,8},{8,9},{11,10... | collective-permute-start | bytes 786440 | tf_op jit(solution)/shard_map/ppermute | solution.py:24

commit v7 on v6

--- a/solution.py
+++ b/solution.py
@@ -52,8 +52,13 @@
 
 
 def fold(table, offsets, key_t, agg_value):
-    values = jnp.transpose(dot(table, agg_value)).astype(BF16)
-    offset_values = jnp.transpose(dot(offsets, agg_value)).astype(BF16)
+    n_vars, n_heads = offsets.shape[0], key_t.shape[0]
+    both = dot(jnp.concatenate([table, offsets], axis=0), agg_value)
+    values = jnp.transpose(both[: table.shape[0]]).astype(BF16)
+    spread = jnp.broadcast_to(both[table.shape[0] :][:, None, :], (n_vars, n_heads, both.shape[1]))
+    heads = lax.broadcasted_iota(jnp.int32, spread.shape, 1)
+    owners = lax.broadcasted_iota(jnp.int32, spread.shape, 2) // HEAD_DIM
+    offset_values = jnp.where(heads == owners, spread, 0.0).reshape(n_vars * n_heads, -1).astype(BF16)
     return values, offset_values, dot(key_t, table, NT), dot(key_t, offsets, NT)
 
 
@@ -115,15 +120,16 @@
     )
     scores = dot(high, pix) + dot(low, pix) + base
     expos = jnp.exp(scores).reshape(n_vars, n_heads, tok)
-    weights = (expos / jnp.sum(expos, axis=0, keepdims=True)).astype(BF16).astype(F32)
-    points = pix.astype(F32).reshape(n_vars, n_pix, tok)
+    weights = (expos / jnp.sum(expos, axis=0, keepdims=True)).astype(BF16)
+    points = pix.reshape(n_vars, n_pix, tok)
     merged = []
     for h in range(n_heads):
         head = weights[:, h, :]
-        mixed = (head[:, None, :] * points).reshape(n_rows, tok).astype(BF16)
+        mixed = (head[:, None, :] * points).reshape(n_rows, tok)
         own = slice(h * HEAD_DIM, (h + 1) * HEAD_DIM)
-        merged.append(dot(values[own], mixed) + dot(offset_values[own], head.astype(BF16)))
-    return jnp.transpose(jnp.concatenate(merged, axis=0))
+        merged.append(dot(values[own], mixed))
+    shifts = dot(jnp.transpose(weights.reshape(n_vars * n_heads, tok)), offset_values)
+    return jnp.transpose(jnp.concatenate(merged, axis=0)) + shifts
 
 
 def normalize(merged):
@@ -162,7 +168,7 @@
         table[pl.ds(pl.multiple_of((1 - side) * half, half), half)] = other[...]
         parts.append(fold(table[...], pack[depth + half :], key_t[...], agg_value[...]))
     for out, shares in zip(folded, zip(*parts)):
-        out[...] = jnp.concatenate(shares, axis=1)
+        out[...] = jnp.concatenate(shares, axis=0 if out is folded[1] else 1)
     for rows, merged in aggregates(packs, folded, tok, depth):
         spots = positions[rows.start // tok : rows.stop // tok]
         merged = merged + jnp.concatenate([ref[...] for ref in spots], axis=0).astype(F32)
@@ -207,10 +213,11 @@
         stack = jnp.concatenate([jnp.where(lanes == h, block, jnp.zeros_like(block)) for h in range(per)], axis=0)
         numer, denom = 0.0, 0.0
         for pair in pairs:
-            expos = jnp.exp(dot(stack, pair[0, :, cut], NT))
-            denom = denom + jnp.sum(expos, axis=-1, keepdims=True)
-            numer = numer + dot(expos.astype(BF16), pair[1, :, cut])
-        denom = jnp.broadcast_to(denom, numer.shape)
+            expos = jnp.exp(dot(stack, pair[0, :, cut], NT)).astype(BF16)
+            values = jnp.concatenate([pair[1, :, cut], jnp.ones((pair.shape[1], group), BF16)], axis=1)
+            both = dot(expos, values)
+            numer = numer + both[:, :group]
+            denom = denom + both[:, group:]
         top, low = numer[:tok], denom[:tok]
         for h in range(1, per):
             top = jnp.where(lanes == h, numer[h * tok : (h + 1) * tok], top)
@@ -272,7 +279,7 @@
     key_t, agg_value, weight, out_weight, position, *folded = call(
         functools.partial(stage_body, len(moved)),
         [sds(a.shape, a.dtype) for a in moved[2:]]
-        + [sds((d, rows), BF16), sds((d, n_vars), BF16), sds((n_heads, rows), F32), sds((n_heads, n_vars), F32)],
+        + [sds((d, rows), BF16), sds((n_vars * n_heads, d), BF16), sds((n_heads, rows), F32), sds((n_heads, n_vars), F32)],
         moved,
         "stage",
         [pltpu.HBM] * len(moved),
@@ -289,7 +296,7 @@
         functools.partial(band_body, n, depth),
         [
             sds((d, rows * n), BF16),
-            sds((d, all_vars), BF16),
+            sds((all_vars * n_heads, d), BF16),
             sds((n_heads, rows * n), F32),
             sds((n_heads, all_vars), F32),
             sds((tok, d), F32),

time: 34.3 us -> 33.6 us (0.980)
  Pallas kernels: 12.7 us -> 11.7 us
  starting transfers between devices: 12.1 us -> 12.6 us
    pallas_call x7, Pallas kernels: 12.7 us -> 11.7 us  [call(): pl.pallas_call(body, out_shape=outs, in_specs=[pl.BlockSpec(memory_space=...]
    ppermute x5, starting transfers between devices: 7.46 us -> 7.91 us  [shifted(): lax.ppermute(block, axis, [((i + distance) % n, i) for i in range(n)])]
  transfers between devices with their start and end apart: 9 -> 9, of which waited for: 4 -> 4; matrix products, arithmetic and copies ran while one was open for 0% -> 0% of each run, Pallas kernels for 31% -> 30%
where the time goes in v7:
time: 33.6 us; the launch traced here: 33.3 us
  starting transfers between devices  12.6 us (38%)
  Pallas kernels  11.7 us (35%)
  waiting for transfers between devices  8.13 us (24%)
  other arithmetic  0.76 us (2%)
    pallas_call x7, Pallas kernels, call(): pl.pallas_call(body, out_shape=outs, in_specs=[pl.BlockSpec(memory_space=...  11.7 us
    ppermute x5, starting transfers between devices, shifted(): lax.ppermute(block, axis, [((i + distance) % n, i) for i in range(n)])  7.91 us
    ppermute x5, waiting for transfers between devices, shifted(): lax.ppermute(block, axis, [((i + distance) % n, i) for i in range(n)])  6.6 us
    ppermute x2, starting transfers between devices, outward(): lax.ppermute(block, 'band', [(i, (i + 1 if i % 2 else i - 1) % n) for i i...  4.51 us
    ppermute x2, waiting for transfers between devices, outward(): lax.ppermute(block, 'band', [(i, (i + 1 if i % 2 else i - 1) % n) for i i...  1.53 us
    convert_element_type x1, other arithmetic, shards(): return update.astype(BF16)  0.76 us
  transfers between devices with their start and end apart: 9, of which 4 were waited for; matrix products, arithmetic and copies ran while one was open for 0% of the time, Pallas kernels for 30%

profile of v7, /device:TPU:0, one launch (start us, length us, event | category | flops | bytes accessed | tf_op | source)
XLA Modules:
  0.0 33.3 jit_solution(18079066885164145588)
XLA Ops:
  0.0 3.0 %collective-permute-start.1 = (bf16[128,1024]{1,0:T(8,128)(2,1)}, bf16[128,1024]{1,0:T(8,128)(2,1)S(1)}, u32[]{:S(2)}, u32[]{:S(2)}) collective-permute-start(bf16[128,1024]{1,0:T(8,128)(2,1)} %refs_6_.1), channel_id=1, source_target_pairs={{1,0},{0,1},{3,2},{2,3},{5,4},{4,5},{7,6},{6,7},{9,8},{8,9},{11,10... | collective-permute-start | bytes 786440 | tf_op jit(solution)/shard_map/ppermute | solution.py:24
  3.0 1.2 %pack.1 = (bf16[104,1024]{1,0:T(8,128)(2,1)S(1)}, bf16[80,1024]{1,0:T(8,128)(2,1)S(1)}, bf16[80,1024]{1,0:T(8,128)(2,1)S(1)}) custom-call(bf16[128,1024]{1,0:T(8,128)(2,1)} %bitcast.5, bf16[8,1024]{1,0:T(8,128)(2,1)} %refs_1_.1, bf16[128,256]{1,0:T(8,128)(2,1)} %bitcast.7, bf16[128,1024]{1,0:T(8,128)(2,1)} %refs_6_.1), custom_call_target="tpu_custom_call" | custom-call | tf_op jit(solution)/shard_map/pack/pallas_call | solution.py:42
  4.1 0.1 collective-permute-start
  4.2 3.9 %collective-permute-start.4 = (bf16[80,1024]{1,0:T(8,128)(2,1)S(1)}, bf16[80,1024]{1,0:T(8,128)(2,1)S(1)}, u32[]{:S(2)}, u32[]{:S(2)}) collective-permute-start(bf16[80,1024]{1,0:T(8,128)(2,1)S(1)} %get-tuple-element.52), channel_id=1, source_target_pairs={{0,30},{2,4},{4,2},{6,8},{8,6},{10,12},{12,10},{14,16},{16,14},{18... | collective-permute-start | bytes 491528 | tf_op jit(solution)/shard_map/ppermute | solution.py:33
  8.1 0.6 %collective-permute-start.6 = (bf16[80,1024]{1,0:T(8,128)(2,1)S(1)}, bf16[80,1024]{1,0:T(8,128)(2,1)S(1)}, u32[]{:S(2)}, u32[]{:S(2)}) collective-permute-start(bf16[80,1024]{1,0:T(8,128)(2,1)S(1)} %get-tuple-element.56), channel_id=1, source_target_pairs={{0,30},{2,4},{4,2},{6,8},{8,6},{10,12},{12,10},{14,16},{16,14},{18... | collective-permute-start | bytes 491528 | tf_op jit(solution)/shard_map/ppermute | solution.py:33
  8.7 3.0 %stage.1 = (bf16[16,1024]{1,0:T(8,128)(2,1)S(1)}, bf16[1024,1024]{1,0:T(8,128)(2,1)S(1)}, bf16[3,1024,512]{2,1,0:T(8,128)(2,1)S(1)}, bf16[512,1024]{1,0:T(8,128)...) custom-call(bf16[128,1024]{1,0:T(8,128)(2,1)} %bitcast.6, ...), custom_call_target="tpu_custom_call" | custom-call | tf_op jit(solution)/shard_map/stage/pallas_call | solution.py:42
  11.7 0.1 collective-permute-done.4.refs_0_
  11.8 1.9 %collective-permute-start.5 = (bf16[80,1024]{1,0:T(8,128)(2,1)S(1)}, bf16[80,1024]{1,0:T(8,128)(2,1)S(1)}, u32[]{:S(2)}, u32[]{:S(2)}) collective-permute-start(bf16[80,1024]{1,0:T(8,128)(2,1)S(1)} %collective-permute-done.4.refs_0_), channel_id=1, source_target_pairs={{1,0},{0,1},{3,2},{2,3},{5,4},{4,5},{7,6},{6,7},{9,8},{8,9},{11,10... | collective-permute-start | bytes 491528 | tf_op jit(solution)/shard_map/ppermute | solution.py:24
  13.8 0.3 collective-permute-done.refs_1_
  14.0 0.0 collective-permute-done.1.refs_8_
  14.1 0.1 collective-permute-start.2
  14.1 1.4 %collective-permute-done.6.refs_2_ = bf16[80,1024]{1,0:T(8,128)(2,1)S(1)} collective-permute-done((bf16[80,1024]{1,0:T(8,128)(2,1)S(1)}, bf16[80,1024]{1,0:T(8,128)(2,1)S(1)}, u32[]{:S(2)}, u32[]{:S(2)}) %collective-permute-start.6) | collective-permute-done | bytes 163872 | tf_op jit(solution)/shard_map/ppermute | solution.py:33
  15.6 1.5 %collective-permute-start.7 = (bf16[80,1024]{1,0:T(8,128)(2,1)S(1)}, bf16[80,1024]{1,0:T(8,128)(2,1)S(1)}, u32[]{:S(2)}, u32[]{:S(2)}) collective-permute-start(bf16[80,1024]{1,0:T(8,128)(2,1)S(1)} %collective-permute-done.6.refs_2_), channel_id=1, source_target_pairs={{1,0},{0,1},{3,2},{2,3},{5,4},{4,5},{7,6},{6,7},{9,8},{8,9},{11,10... | collective-permute-start | bytes 491528 | tf_op jit(solution)/shard_map/ppermute | solution.py:24
  17.1 0.0 collective-permute-done.2.refs_2_
  17.1 2.8 %front_band.1 = (bf16[1024,256]{1,0:T(8,128)(2,1)S(1)}, bf16[256,1024]{1,0:T(8,128)(2,1)S(1)}, f32[16,256]{1,0:T(8,128)S(1)}, f32[16,16]{1,0:T(8,128)S(1)}, f32[...) custom-call(bf16[104,1024]{1,0:T(8,128)(2,1)S(1)} %get-tuple-element.37.refs_0_, ...), custom_call_target="tpu_custom_call" | custom-call | flops 300000000 | tf_op jit(solution)/shard_map/front_band/pallas_call | solution.py:42
  19.9 0.1 collective-permute-start.3
  20.0 0.8 %attend_band.1 = (f32[256,512]{1,0:T(8,128)S(1)}, f32[256,512]{1,0:T(8,128)S(1)}) custom-call(bf16[256,512]{1,0:T(8,128)(2,1)S(1)} %get-tuple-element.48.query.refs_6_, bf16[2,256,512]{2,1,0:T(8,128)(2,1)S(1)} %get-tuple-element.49.pair), custom_call_target="tpu_custom_call" | custom-call | tf_op jit(solution)/shard_map/attend_band/pallas_call | solution.py:42
  20.8 1.1 %mix_outer.1.refs_4_ = f32[256,1024]{1,0:T(8,128)S(1)} custom-call(bf16[80,1024]{1,0:T(8,128)(2,1)S(1)} %collective-permute-done.4.refs_0_, bf16[80,1024]{1,0:T(8,128)(2,1)S(1)} %collective-permute-done.5.refs_1_, bf16[1024,256]{1,0:T(8,128)(2,1)S(1)} %get-tuple-element.58.refs_2_, bf16[256,1024]{1,0:T(8,128)(2,1)S(1)} %get-tuple-element.59.refs_3_, ...), custom_call_target="tpu_custom_call" | custom-call | flops 20000000000 | tf_op jit(solution)/shard_map/mix_outer/pallas_call | solution.py:42
  21.9 0.0 collective-permute-done.7.refs_3_
  21.9 1.9 %front_outer.1 = (bf16[2,256,512]{2,1,0:T(8,128)(2,1)S(1)}, bf16[128,1024]{1,0:T(8,128)(2,1)S(1)}) custom-call(bf16[80,1024]{1,0:T(8,128)(2,1)S(1)} %collective-permute-done.4.refs_0_, bf16[80,1024]{1,0:T(8,128)(2,1)S(1)} %collective-permute-done.5.refs_1_, bf16[80,1024]{1,0:T(8,128)(2,1)S(1)} %collective-permute-done.6.refs_2_, ...), custom_call_target="tpu_custom_call" | custom-call | tf_op jit(solution)/shard_map/front_outer/pallas_call | solution.py:42
  23.8 1.4 %collective-permute-start.8 = (bf16[128,1024]{1,0:T(8,128)(2,1)S(1)}, bf16[128,1024]{1,0:T(8,128)(2,1)S(1)}, u32[]{:S(2)}, u32[]{:S(2)}) collective-permute-start(bf16[128,1024]{1,0:T(8,128)(2,1)S(1)} %get-tuple-element.68), channel_id=1, source_target_pairs={{1,0},{0,1},{3,2},{2,3},{5,4},{4,5},{7,6},{6,7},{9,8},{8,9},{11,10... | collective-permute-start | bytes 786440 | tf_op jit(solution)/shard_map/ppermute | solution.py:24
  25.2 1.0 %attend_own.1 = f32[128,1024]{1,0:T(8,128)S(1)} custom-call(bf16[256,512]{1,0:T(8,128)(2,1)S(1)} %get-tuple-element.48.query.refs_6_, f32[256,512]{1,0:T(8,128)S(1)} %get-tuple-element.50.refs_7_.numer, f32[256,512]{1,0:T(8,128)S(1)} %get-tuple-element.51.refs_8_.denom, bf16[2,256,512]{2,1,0:T(8,128)(2,1)S(1)} %collective-permute-done.3.refs_9_.inner, ...), custom_call_target="tpu_custom_call" | custom-call | tf_op jit(solution)/shard_map/attend_own/pallas_call | solution.py:42
  26.2 6.3 %collective-permute-done.8 = bf16[128,1024]{1,0:T(8,128)(2,1)S(1)} collective-permute-done((bf16[128,1024]{1,0:T(8,128)(2,1)S(1)}, bf16[128,1024]{1,0:T(8,128)(2,1)S(1)}, u32[]{:S(2)}, u32[]{:S(2)}) %collective-permute-start.8) | collective-permute-done | bytes 262176 | tf_op jit(solution)/shard_map/ppermute | solution.py:24
  32.5 0.8 %add_convert_fusion = bf16[128,1024]{1,0:T(8,128)(2,1)} fusion(f32[128,1024]{1,0:T(8,128)S(1)} %attend_own.1, bf16[128,1024]{1,0:T(8,128)(2,1)S(1)} %collective-permute-done.8), kind=kLoop, calls=%fused_computation | loop fusion | flops 393216 | bytes 1048576 | tf_op jit(solution)/shard_map/convert_element_type | solution.py:332
  (3 shorter events, 0.0 us)
Async XLA Ops:
  0.0 14.0 %collective-permute-start.1 = (bf16[128,1024]{1,0:T(8,128)(2,1)}, bf16[128,1024]{1,0:T(8,128)(2,1)S(1)}, u32[]{:S(2)}, u32[]{:S(2)}) collective-permute-start(bf16[128,1024]{1,0:T(8,128)(2,1)} %refs_6_.1), channel_id=1, source_target_pairs={{1,0},{0,1},{3,2},{2,3},{5,4},{4,5},{7,6},{6,7},{9,8},{8,9},{11,10... | collective-permute-start | bytes 786440 | tf_op jit(solution)/shard_map/ppermute | solution.py:24
  4.1 9.9 %collective-permute-start = (bf16[104,1024]{1,0:T(8,128)(2,1)S(1)}, bf16[104,1024]{1,0:T(8,128)(2,1)S(1)}, u32[]{:S(2)}, u32[]{:S(2)}) collective-permute-start(bf16[104,1024]{1,0:T(8,128)(2,1)S(1)} %get-tuple-element.37.refs_0_), channel_id=1, source_target_pairs={{1,0},{0,1},{3,2},{2,3},{5,4},{4,5},{7,6},{6,7},{9,8},{8,9},{11,10... | collective-permute-start | bytes 638984 | tf_op jit(solution)/shard_map/ppermute | solution.py:24
  4.2 7.6 %collective-permute-start.4 = (bf16[80,1024]{1,0:T(8,128)(2,1)S(1)}, bf16[80,1024]{1,0:T(8,128)(2,1)S(1)}, u32[]{:S(2)}, u32[]{:S(2)}) collective-permute-start(bf16[80,1024]{1,0:T(8,128)(2,1)S(1)} %get-tuple-element.52), channel_id=1, source_target_pairs={{0,30},{2,4},{4,2},{6,8},{8,6},{10,12},{12,10},{14,16},{16,14},{18... | collective-permute-start | bytes 491528 | tf_op jit(solution)/shard_map/ppermute | solution.py:33
  8.1 7.4 %collective-permute-start.6 = (bf16[80,1024]{1,0:T(8,128)(2,1)S(1)}, bf16[80,1024]{1,0:T(8,128)(2,1)S(1)}, u32[]{:S(2)}, u32[]{:S(2)}) collective-permute-start(bf16[80,1024]{1,0:T(8,128)(2,1)S(1)} %get-tuple-element.56), channel_id=1, source_target_pairs={{0,30},{2,4},{4,2},{6,8},{8,6},{10,12},{12,10},{14,16},{16,14},{18... | collective-permute-start | bytes 491528 | tf_op jit(solution)/shard_map/ppermute | solution.py:33
  11.8 9.0 %collective-permute-start.5 = (bf16[80,1024]{1,0:T(8,128)(2,1)S(1)}, bf16[80,1024]{1,0:T(8,128)(2,1)S(1)}, u32[]{:S(2)}, u32[]{:S(2)}) collective-permute-start(bf16[80,1024]{1,0:T(8,128)(2,1)S(1)} %collective-permute-done.4.refs_0_), channel_id=1, source_target_pairs={{1,0},{0,1},{3,2},{2,3},{5,4},{4,5},{7,6},{6,7},{9,8},{8,9},{11,10... | collective-permute-start | bytes 491528 | tf_op jit(solution)/shard_map/ppermute | solution.py:24
  14.1 3.0 %collective-permute-start.2 = (bf16[64,1024]{1,0:T(8,128)(2,1)S(1)}, bf16[64,1024]{1,0:T(8,128)(2,1)S(1)}, u32[]{:S(2)}, u32[]{:S(2)}) collective-permute-start(bf16[64,1024]{1,0:T(8,128)(2,1)S(1)} %slice.3), channel_id=1, source_target_pairs={{2,0},{0,2},{6,4},{4,6},{10,8},{8,10},{14,12},{12,14},{18,16},{16,... | collective-permute-start | bytes 393224 | tf_op jit(solution)/shard_map/ppermute | solution.py:28
  15.6 6.3 %collective-permute-start.7 = (bf16[80,1024]{1,0:T(8,128)(2,1)S(1)}, bf16[80,1024]{1,0:T(8,128)(2,1)S(1)}, u32[]{:S(2)}, u32[]{:S(2)}) collective-permute-start(bf16[80,1024]{1,0:T(8,128)(2,1)S(1)} %collective-permute-done.6.refs_2_), channel_id=1, source_target_pairs={{1,0},{0,1},{3,2},{2,3},{5,4},{4,5},{7,6},{6,7},{9,8},{8,9},{11,10... | collective-permute-start | bytes 491528 | tf_op jit(solution)/shard_map/ppermute | solution.py:24
  19.9 2.0 %collective-permute-start.3 = (bf16[2,256,512]{2,1,0:T(8,128)(2,1)S(1)}, bf16[2,256,512]{2,1,0:T(8,128)(2,1)S(1)}, u32[]{:S(2)}, u32[]{:S(2)}) collective-permute-start(bf16[2,256,512]{2,1,0:T(8,128)(2,1)S(1)} %get-tuple-element.49.pair), channel_id=1, source_target_pairs={{2,0},{0,2},{6,4},{4,6},{10,8},{8,10},{14,12},{12,14},{18,16},{16,... | collective-permute-start | bytes 1572872 | tf_op jit(solution)/shard_map/ppermute | solution.py:28
  23.8 8.8 %collective-permute-start.8 = (bf16[128,1024]{1,0:T(8,128)(2,1)S(1)}, bf16[128,1024]{1,0:T(8,128)(2,1)S(1)}, u32[]{:S(2)}, u32[]{:S(2)}) collective-permute-start(bf16[128,1024]{1,0:T(8,128)(2,1)S(1)} %get-tuple-element.68), channel_id=1, source_target_pairs={{1,0},{0,1},{3,2},{2,3},{5,4},{4,5},{7,6},{6,7},{9,8},{8,9},{11,10... | collective-permute-start | bytes 786440 | tf_op jit(solution)/shard_map/ppermute | solution.py:24

commit v8 on v7

--- a/solution.py
+++ b/solution.py
@@ -198,7 +198,7 @@
         for c in range(2):
             pair_out[c, rows] = dot(normed, weight[c + 1]).astype(BF16)
     if share:
-        finish_body(1, query, numer, denom, inner, pair_out, out_weight, share[0])
+        finish_body(tok, query, numer, denom, inner, pair_out, out_weight, share[0])
 
 
 def absorb(query, pairs):
@@ -233,10 +233,9 @@
         numer[rows], denom[rows] = absorb(query[rows], [pair])
 
 
-def finish_body(distance, query, numer, denom, inner, outer, out_weight, *refs):
+def finish_body(first, query, numer, denom, inner, outer, out_weight, *refs):
     out = refs[-1]
-    tok = out.shape[0]
-    rows = slice(distance * tok, (distance + 1) * tok)
+    rows = slice(first, first + out.shape[0])
     top, low = absorb(query[rows], [inner, outer])
     context = ((numer[rows] + top) / (denom[rows] + low)).astype(BF16)
     update = dot(context, out_weight[...])
@@ -314,21 +313,25 @@
         functools.partial(outer_mix_body, n, depth), [sds((band_tok, d), F32)], (*firsts, *folded), "mix_outer"
     )
     *seconds, mixed = lax.optimization_barrier((*seconds, mixed))
+    spans = [(0, tok * 5 // 8), (tok * 5 // 8, tok)]
     outer_pair, *share = call(
         functools.partial(outer_body, n, depth),
-        [sds((2, band_tok, width), BF16)] + [sds((tok, d), BF16)] * (n > 1),
+        [sds((2, band_tok, width), BF16)] + [sds((spans[0][1], d), BF16)] * (n > 1),
         (*firsts, *seconds, mixed, weight, query, *totals, inner, out_weight),
         "front_outer",
     )
     attended = (query, *totals, inner, outer_pair, out_weight)
-    for r in range(2, n):
-        share += call(functools.partial(finish_body, r), [sds((tok, d), BF16)], attended, "attend_later")
-    ending = [shifted(x, "var", n - r) for r, x in enumerate(share, 1)]
-    (update,) = call(
-        functools.partial(finish_body, 0), [sds((tok, d), F32)], (*attended, merged), "attend_own"
-    )
-    for x in ending:
-        update = update + x.astype(F32)
+    pieces = [[None] * len(spans) for _ in others]
+    for r in others:
+        for i, (start, stop) in enumerate(spans):
+            if r > 1 or i > 0:
+                share = call(
+                    functools.partial(finish_body, r * tok + start), [sds((stop - start, d), BF16)], attended, "attend_later"
+                )
+            pieces[r - 1][i] = shifted(share[0], "var", n - r)
+    (update,) = call(functools.partial(finish_body, 0), [sds((tok, d), F32)], (*attended, merged), "attend_own")
+    for parts in pieces:
+        update = update + jnp.concatenate(parts, axis=0).astype(F32)
     return update.astype(BF16)
 
 

time: 33.6 us -> 33.4 us (level)
  waiting for transfers between devices: 8.13 us -> 6.63 us
  starting transfers between devices: 12.6 us -> 13.3 us
  Pallas kernels: 11.7 us -> 12.3 us
    ppermute x5 -> x6, waiting for transfers between devices: 6.6 us -> 5.09 us  [shifted(): lax.ppermute(block, axis, [((i + distance) % n, i) for i in range(n)])]
    ppermute x5 -> x6, starting transfers between devices: 7.91 us -> 8.66 us  [shifted(): lax.ppermute(block, axis, [((i + distance) % n, i) for i in range(n)])]
    pallas_call x7 -> x8, Pallas kernels: 11.7 us -> 12.3 us  [call(): pl.pallas_call(body, out_shape=outs, in_specs=[pl.BlockSpec(memory_space=...]
  transfers between devices with their start and end apart: 9 -> 10, of which waited for: 4 -> 4; matrix products, arithmetic and copies ran while one was open for 0% -> 0% of each run, Pallas kernels for 30% -> 32%
where the time goes in v8:
time: 33.4 us; the launch traced here: 33.1 us
  starting transfers between devices  13.3 us (40%)
  Pallas kernels  12.3 us (37%)
  waiting for transfers between devices  6.63 us (20%)
  other arithmetic  0.78 us (2%)
    pallas_call x8, Pallas kernels, call(): pl.pallas_call(body, out_shape=outs, in_specs=[pl.BlockSpec(memory_space=...  12.3 us
    ppermute x6, starting transfers between devices, shifted(): lax.ppermute(block, axis, [((i + distance) % n, i) for i in range(n)])  8.66 us
    ppermute x6, waiting for transfers between devices, shifted(): lax.ppermute(block, axis, [((i + distance) % n, i) for i in range(n)])  5.09 us
    ppermute x2, starting transfers between devices, outward(): lax.ppermute(block, 'band', [(i, (i + 1 if i % 2 else i - 1) % n) for i i...  4.51 us
    ppermute x2, waiting for transfers between devices, outward(): lax.ppermute(block, 'band', [(i, (i + 1 if i % 2 else i - 1) % n) for i i...  1.53 us
    convert_element_type x1, other arithmetic, shards(): return update.astype(BF16)  0.78 us
  transfers between devices with their start and end apart: 10, of which 4 were waited for; matrix products, arithmetic and copies ran while one was open for 0% of the time, Pallas kernels for 32%

profile of v8, /device:TPU:0, one launch (start us, length us, event | category | flops | bytes accessed | tf_op | source)
XLA Modules:
  0.0 33.1 jit_solution(5451487420554454854)
XLA Ops:
  0.0 3.0 %collective-permute-start.1 = (bf16[128,1024]{1,0:T(8,128)(2,1)}, bf16[128,1024]{1,0:T(8,128)(2,1)S(1)}, u32[]{:S(2)}, u32[]{:S(2)}) collective-permute-start(bf16[128,1024]{1,0:T(8,128)(2,1)} %refs_6_.1), channel_id=1, source_target_pairs={{1,0},{0,1},{3,2},{2,3},{5,4},{4,5},{7,6},{6,7},{9,8},{8,9},{11,10... | collective-permute-start | bytes 786440 | tf_op jit(solution)/shard_map/ppermute | solution.py:24
  3.0 1.2 %pack.1 = (bf16[104,1024]{1,0:T(8,128)(2,1)S(1)}, bf16[80,1024]{1,0:T(8,128)(2,1)S(1)}, bf16[80,1024]{1,0:T(8,128)(2,1)S(1)}) custom-call(bf16[128,1024]{1,0:T(8,128)(2,1)} %bitcast.5, bf16[8,1024]{1,0:T(8,128)(2,1)} %refs_1_.1, bf16[128,256]{1,0:T(8,128)(2,1)} %bitcast.7, bf16[128,1024]{1,0:T(8,128)(2,1)} %refs_6_.1), custom_call_target="tpu_custom_call" | custom-call | tf_op jit(solution)/shard_map/pack/pallas_call | solution.py:42
  4.1 0.1 collective-permute-start
  4.2 3.9 %collective-permute-start.4 = (bf16[80,1024]{1,0:T(8,128)(2,1)S(1)}, bf16[80,1024]{1,0:T(8,128)(2,1)S(1)}, u32[]{:S(2)}, u32[]{:S(2)}) collective-permute-start(bf16[80,1024]{1,0:T(8,128)(2,1)S(1)} %get-tuple-element.52), channel_id=1, source_target_pairs={{0,30},{2,4},{4,2},{6,8},{8,6},{10,12},{12,10},{14,16},{16,14},{18... | collective-permute-start | bytes 491528 | tf_op jit(solution)/shard_map/ppermute | solution.py:33
  8.1 0.6 %collective-permute-start.6 = (bf16[80,1024]{1,0:T(8,128)(2,1)S(1)}, bf16[80,1024]{1,0:T(8,128)(2,1)S(1)}, u32[]{:S(2)}, u32[]{:S(2)}) collective-permute-start(bf16[80,1024]{1,0:T(8,128)(2,1)S(1)} %get-tuple-element.56), channel_id=1, source_target_pairs={{0,30},{2,4},{4,2},{6,8},{8,6},{10,12},{12,10},{14,16},{16,14},{18... | collective-permute-start | bytes 491528 | tf_op jit(solution)/shard_map/ppermute | solution.py:33
  8.7 3.0 %stage.1 = (bf16[16,1024]{1,0:T(8,128)(2,1)S(1)}, bf16[1024,1024]{1,0:T(8,128)(2,1)S(1)}, bf16[3,1024,512]{2,1,0:T(8,128)(2,1)S(1)}, bf16[512,1024]{1,0:T(8,128)...) custom-call(bf16[128,1024]{1,0:T(8,128)(2,1)} %bitcast.6, ...), custom_call_target="tpu_custom_call" | custom-call | tf_op jit(solution)/shard_map/stage/pallas_call | solution.py:42
  11.7 0.1 collective-permute-done.4.refs_0_
  11.8 1.9 %collective-permute-start.5 = (bf16[80,1024]{1,0:T(8,128)(2,1)S(1)}, bf16[80,1024]{1,0:T(8,128)(2,1)S(1)}, u32[]{:S(2)}, u32[]{:S(2)}) collective-permute-start(bf16[80,1024]{1,0:T(8,128)(2,1)S(1)} %collective-permute-done.4.refs_0_), channel_id=1, source_target_pairs={{1,0},{0,1},{3,2},{2,3},{5,4},{4,5},{7,6},{6,7},{9,8},{8,9},{11,10... | collective-permute-start | bytes 491528 | tf_op jit(solution)/shard_map/ppermute | solution.py:24
  13.8 0.3 collective-permute-done.refs_1_
  14.1 0.1 collective-permute-start.2
  14.1 1.4 %collective-permute-done.6.refs_2_ = bf16[80,1024]{1,0:T(8,128)(2,1)S(1)} collective-permute-done((bf16[80,1024]{1,0:T(8,128)(2,1)S(1)}, bf16[80,1024]{1,0:T(8,128)(2,1)S(1)}, u32[]{:S(2)}, u32[]{:S(2)}) %collective-permute-start.6) | collective-permute-done | bytes 163872 | tf_op jit(solution)/shard_map/ppermute | solution.py:33
  15.6 1.5 %collective-permute-start.7 = (bf16[80,1024]{1,0:T(8,128)(2,1)S(1)}, bf16[80,1024]{1,0:T(8,128)(2,1)S(1)}, u32[]{:S(2)}, u32[]{:S(2)}) collective-permute-start(bf16[80,1024]{1,0:T(8,128)(2,1)S(1)} %collective-permute-done.6.refs_2_), channel_id=1, source_target_pairs={{1,0},{0,1},{3,2},{2,3},{5,4},{4,5},{7,6},{6,7},{9,8},{8,9},{11,10... | collective-permute-start | bytes 491528 | tf_op jit(solution)/shard_map/ppermute | solution.py:24
  17.1 2.8 %front_band.1 = (bf16[1024,256]{1,0:T(8,128)(2,1)S(1)}, bf16[256,1024]{1,0:T(8,128)(2,1)S(1)}, f32[16,256]{1,0:T(8,128)S(1)}, f32[16,16]{1,0:T(8,128)S(1)}, f32[...) custom-call(bf16[104,1024]{1,0:T(8,128)(2,1)S(1)} %get-tuple-element.37.refs_0_, ...), custom_call_target="tpu_custom_call" | custom-call | flops 300000000 | tf_op jit(solution)/shard_map/front_band/pallas_call | solution.py:42
  19.9 0.1 collective-permute-start.3
  20.0 0.8 %attend_band.1 = (f32[256,512]{1,0:T(8,128)S(1)}, f32[256,512]{1,0:T(8,128)S(1)}) custom-call(bf16[256,512]{1,0:T(8,128)(2,1)S(1)} %get-tuple-element.48.query.refs_6_, bf16[2,256,512]{2,1,0:T(8,128)(2,1)S(1)} %get-tuple-element.49.pair), custom_call_target="tpu_custom_call" | custom-call | tf_op jit(solution)/shard_map/attend_band/pallas_call | solution.py:42
  20.8 1.0 %mix_outer.1.refs_4_ = f32[256,1024]{1,0:T(8,128)S(1)} custom-call(bf16[80,1024]{1,0:T(8,128)(2,1)S(1)} %collective-permute-done.4.refs_0_, bf16[80,1024]{1,0:T(8,128)(2,1)S(1)} %collective-permute-done.5.refs_1_, bf16[1024,256]{1,0:T(8,128)(2,1)S(1)} %get-tuple-element.58.refs_2_, bf16[256,1024]{1,0:T(8,128)(2,1)S(1)} %get-tuple-element.59.refs_3_, ...), custom_call_target="tpu_custom_call" | custom-call | flops 20000000000 | tf_op jit(solution)/shard_map/mix_outer/pallas_call | solution.py:42
  21.9 0.0 collective-permute-done.3.refs_9_.inner
  21.9 1.7 %front_outer.1 = (bf16[2,256,512]{2,1,0:T(8,128)(2,1)S(1)}, bf16[80,1024]{1,0:T(8,128)(2,1)S(1)}) custom-call(bf16[80,1024]{1,0:T(8,128)(2,1)S(1)} %collective-permute-done.4.refs_0_, bf16[80,1024]{1,0:T(8,128)(2,1)S(1)} %collective-permute-done.5.refs_1_, bf16[80,1024]{1,0:T(8,128)(2,1)S(1)} %collective-permute-done.6.refs_2_, ...), custom_call_target="tpu_custom_call" | custom-call | tf_op jit(solution)/shard_map/front_outer/pallas_call | solution.py:42
  23.5 1.4 %collective-permute-start.8 = (bf16[80,1024]{1,0:T(8,128)(2,1)S(1)}, bf16[80,1024]{1,0:T(8,128)(2,1)S(1)}, u32[]{:S(2)}, u32[]{:S(2)}) collective-permute-start(bf16[80,1024]{1,0:T(8,128)(2,1)S(1)} %get-tuple-element.68), channel_id=1, source_target_pairs={{1,0},{0,1},{3,2},{2,3},{5,4},{4,5},{7,6},{6,7},{9,8},{8,9},{11,10... | collective-permute-start | bytes 491528 | tf_op jit(solution)/shard_map/ppermute | solution.py:24
  25.0 0.8 %attend_later.1 = bf16[48,1024]{1,0:T(8,128)(2,1)S(1)} custom-call(bf16[256,512]{1,0:T(8,128)(2,1)S(1)} %get-tuple-element.48.query.refs_6_, f32[256,512]{1,0:T(8,128)S(1)} %get-tuple-element.50.refs_7_.numer, f32[256,512]{1,0:T(8,128)S(1)} %get-tuple-element.51.refs_8_.denom, bf16[2,256,512]{2,1,0:T(8,128)(2,1)S(1)} %collective-permute-done.3.refs_9_.inner, ...), custom_call_target="tpu_custom_call" | custom-call | tf_op jit(solution)/shard_map/attend_later/pallas_call | solution.py:42
  25.7 0.7 %collective-permute-start.9 = (bf16[48,1024]{1,0:T(8,128)(2,1)S(1)}, bf16[48,1024]{1,0:T(8,128)(2,1)S(1)}, u32[]{:S(2)}, u32[]{:S(2)}) collective-permute-start(bf16[48,1024]{1,0:T(8,128)(2,1)S(1)} %attend_later.1), channel_id=1, source_target_pairs={{1,0},{0,1},{3,2},{2,3},{5,4},{4,5},{7,6},{6,7},{9,8},{8,9},{11,10... | collective-permute-start | bytes 294920 | tf_op jit(solution)/shard_map/ppermute | solution.py:24
  26.5 1.0 %attend_own.1 = f32[128,1024]{1,0:T(8,128)S(1)} custom-call(bf16[256,512]{1,0:T(8,128)(2,1)S(1)} %get-tuple-element.48.query.refs_6_, f32[256,512]{1,0:T(8,128)S(1)} %get-tuple-element.50.refs_7_.numer, f32[256,512]{1,0:T(8,128)S(1)} %get-tuple-element.51.refs_8_.denom, bf16[2,256,512]{2,1,0:T(8,128)(2,1)S(1)} %collective-permute-done.3.refs_9_.inner, ...), custom_call_target="tpu_custom_call" | custom-call | tf_op jit(solution)/shard_map/attend_own/pallas_call | solution.py:42
  27.5 4.8 %collective-permute-done.9 = bf16[48,1024]{1,0:T(8,128)(2,1)S(1)} collective-permute-done((bf16[48,1024]{1,0:T(8,128)(2,1)S(1)}, bf16[48,1024]{1,0:T(8,128)(2,1)S(1)}, u32[]{:S(2)}, u32[]{:S(2)}) %collective-permute-start.9) | collective-permute-done | bytes 98336 | tf_op jit(solution)/shard_map/ppermute | solution.py:24
  32.3 0.8 %add_convert_fusion = bf16[128,1024]{1,0:T(8,128)(2,1)} fusion(f32[128,1024]{1,0:T(8,128)S(1)} %attend_own.1, bf16[48,1024]{1,0:T(8,128)(2,1)S(1)} %collective-permute-done.9, bf16[80,1024]{1,0:T(8,128)(2,1)S(1)} %collective-permute-done.8), kind=kLoop, calls=%fused_computation | loop fusion | flops 786432 | bytes 1048576 | tf_op jit(solution)/shard_map/convert_element_type | solution.py:335
  (6 shorter events, 0.0 us)
Async XLA Ops:
  0.0 14.0 %collective-permute-start.1 = (bf16[128,1024]{1,0:T(8,128)(2,1)}, bf16[128,1024]{1,0:T(8,128)(2,1)S(1)}, u32[]{:S(2)}, u32[]{:S(2)}) collective-permute-start(bf16[128,1024]{1,0:T(8,128)(2,1)} %refs_6_.1), channel_id=1, source_target_pairs={{1,0},{0,1},{3,2},{2,3},{5,4},{4,5},{7,6},{6,7},{9,8},{8,9},{11,10... | collective-permute-start | bytes 786440 | tf_op jit(solution)/shard_map/ppermute | solution.py:24
  4.1 9.9 %collective-permute-start = (bf16[104,1024]{1,0:T(8,128)(2,1)S(1)}, bf16[104,1024]{1,0:T(8,128)(2,1)S(1)}, u32[]{:S(2)}, u32[]{:S(2)}) collective-permute-start(bf16[104,1024]{1,0:T(8,128)(2,1)S(1)} %get-tuple-element.37.refs_0_), channel_id=1, source_target_pairs={{1,0},{0,1},{3,2},{2,3},{5,4},{4,5},{7,6},{6,7},{9,8},{8,9},{11,10... | collective-permute-start | bytes 638984 | tf_op jit(solution)/shard_map/ppermute | solution.py:24
  4.2 7.6 %collective-permute-start.4 = (bf16[80,1024]{1,0:T(8,128)(2,1)S(1)}, bf16[80,1024]{1,0:T(8,128)(2,1)S(1)}, u32[]{:S(2)}, u32[]{:S(2)}) collective-permute-start(bf16[80,1024]{1,0:T(8,128)(2,1)S(1)} %get-tuple-element.52), channel_id=1, source_target_pairs={{0,30},{2,4},{4,2},{6,8},{8,6},{10,12},{12,10},{14,16},{16,14},{18... | collective-permute-start | bytes 491528 | tf_op jit(solution)/shard_map/ppermute | solution.py:33
  8.1 7.4 %collective-permute-start.6 = (bf16[80,1024]{1,0:T(8,128)(2,1)S(1)}, bf16[80,1024]{1,0:T(8,128)(2,1)S(1)}, u32[]{:S(2)}, u32[]{:S(2)}) collective-permute-start(bf16[80,1024]{1,0:T(8,128)(2,1)S(1)} %get-tuple-element.56), channel_id=1, source_target_pairs={{0,30},{2,4},{4,2},{6,8},{8,6},{10,12},{12,10},{14,16},{16,14},{18... | collective-permute-start | bytes 491528 | tf_op jit(solution)/shard_map/ppermute | solution.py:33
  11.8 9.0 %collective-permute-start.5 = (bf16[80,1024]{1,0:T(8,128)(2,1)S(1)}, bf16[80,1024]{1,0:T(8,128)(2,1)S(1)}, u32[]{:S(2)}, u32[]{:S(2)}) collective-permute-start(bf16[80,1024]{1,0:T(8,128)(2,1)S(1)} %collective-permute-done.4.refs_0_), channel_id=1, source_target_pairs={{1,0},{0,1},{3,2},{2,3},{5,4},{4,5},{7,6},{6,7},{9,8},{8,9},{11,10... | collective-permute-start | bytes 491528 | tf_op jit(solution)/shard_map/ppermute | solution.py:24
  14.1 3.0 %collective-permute-start.2 = (bf16[64,1024]{1,0:T(8,128)(2,1)S(1)}, bf16[64,1024]{1,0:T(8,128)(2,1)S(1)}, u32[]{:S(2)}, u32[]{:S(2)}) collective-permute-start(bf16[64,1024]{1,0:T(8,128)(2,1)S(1)} %slice.3), channel_id=1, source_target_pairs={{2,0},{0,2},{6,4},{4,6},{10,8},{8,10},{14,12},{12,14},{18,16},{16,... | collective-permute-start | bytes 393224 | tf_op jit(solution)/shard_map/ppermute | solution.py:28
  15.6 6.3 %collective-permute-start.7 = (bf16[80,1024]{1,0:T(8,128)(2,1)S(1)}, bf16[80,1024]{1,0:T(8,128)(2,1)S(1)}, u32[]{:S(2)}, u32[]{:S(2)}) collective-permute-start(bf16[80,1024]{1,0:T(8,128)(2,1)S(1)} %collective-permute-done.6.refs_2_), channel_id=1, source_target_pairs={{1,0},{0,1},{3,2},{2,3},{5,4},{4,5},{7,6},{6,7},{9,8},{8,9},{11,10... | collective-permute-start | bytes 491528 | tf_op jit(solution)/shard_map/ppermute | solution.py:24
  19.9 2.0 %collective-permute-start.3 = (bf16[2,256,512]{2,1,0:T(8,128)(2,1)S(1)}, bf16[2,256,512]{2,1,0:T(8,128)(2,1)S(1)}, u32[]{:S(2)}, u32[]{:S(2)}) collective-permute-start(bf16[2,256,512]{2,1,0:T(8,128)(2,1)S(1)} %get-tuple-element.49.pair), channel_id=1, source_target_pairs={{2,0},{0,2},{6,4},{4,6},{10,8},{8,10},{14,12},{12,14},{18,16},{16,... | collective-permute-start | bytes 1572872 | tf_op jit(solution)/shard_map/ppermute | solution.py:28
  23.5 8.8 %collective-permute-start.8 = (bf16[80,1024]{1,0:T(8,128)(2,1)S(1)}, bf16[80,1024]{1,0:T(8,128)(2,1)S(1)}, u32[]{:S(2)}, u32[]{:S(2)}) collective-permute-start(bf16[80,1024]{1,0:T(8,128)(2,1)S(1)} %get-tuple-element.68), channel_id=1, source_target_pairs={{1,0},{0,1},{3,2},{2,3},{5,4},{4,5},{7,6},{6,7},{9,8},{8,9},{11,10... | collective-permute-start | bytes 491528 | tf_op jit(solution)/shard_map/ppermute | solution.py:24
  25.7 6.6 %collective-permute-start.9 = (bf16[48,1024]{1,0:T(8,128)(2,1)S(1)}, bf16[48,1024]{1,0:T(8,128)(2,1)S(1)}, u32[]{:S(2)}, u32[]{:S(2)}) collective-permute-start(bf16[48,1024]{1,0:T(8,128)(2,1)S(1)} %attend_later.1), channel_id=1, source_target_pairs={{1,0},{0,1},{3,2},{2,3},{5,4},{4,5},{7,6},{6,7},{9,8},{8,9},{11,10... | collective-permute-start | bytes 294920 | tf_op jit(solution)/shard_map/ppermute | solution.py:24

commit v9 on v8

--- a/solution.py
+++ b/solution.py
@@ -33,7 +33,7 @@
     return lax.ppermute(block, "band", [(i, (i + 1 if i % 2 else i - 1) % n) for i in range(n)])
 
 
-COST = {"mix_outer": 20.0, "front_band": 0.3}
+COST = {"gate": 20.0, "front_band": 0.3}
 
 
 def call(body, outs, args, name, spaces=None, scratch=()):
@@ -62,24 +62,22 @@
     return values, offset_values, dot(key_t, table, NT), dot(key_t, offsets, NT)
 
 
-def pack_body(table, offsets, pix, position, shared, first, second, offsets_in, sems):
+def pack_body(table, offsets, pix, position, shared, placed, offsets_in, sems):
     rows, band_tok = pix.shape
     tok, d = position.shape
     half = table.shape[0] // 2
     blocks = d // band_tok
     depth = rows // blocks
-    cut = first.shape[0] - depth
     side = lax.rem(lax.axis_index("band"), 2)
     moves = [
         (offsets, offsets_in),
         (table.at[pl.ds(pl.multiple_of(side * half, half), half)], shared.at[pl.ds(depth, half)]),
-        (position.at[pl.ds(0, cut)], first.at[pl.ds(depth, cut)]),
-        (position.at[pl.ds(cut, tok - cut)], second),
+        (position, placed.at[pl.ds(depth, tok)]),
     ]
     for k in range(blocks):
         lanes = pl.ds(k * band_tok, band_tok)
         moves.append((pix.at[pl.ds(k * depth, depth)], shared.at[pl.ds(0, depth), lanes]))
-        moves.append((pix.at[pl.ds(k * depth, depth)], first.at[pl.ds(0, depth), lanes]))
+        moves.append((pix.at[pl.ds(k * depth, depth)], placed.at[pl.ds(0, depth), lanes]))
     copies = [pltpu.make_async_copy(a, b, sems.at[i]) for i, (a, b) in enumerate(moves)]
     for copy in copies:
         copy.start()
@@ -186,15 +184,19 @@
         out[rows] = merged
 
 
-def outer_body(n, depth, *refs):
-    firsts, seconds, (mixed, weight) = refs[:n], refs[n : 2 * n], refs[2 * n : 2 * n + 2]
-    query, numer, denom, inner, out_weight, pair_out, *share = refs[2 * n + 2 :]
+def gate_body(*refs):
+    refs[-1][...] = jnp.zeros(refs[-1].shape, F32)
+
+
+def outer_body(n, *refs):
+    spots, (mixed, weight) = refs[:n], refs[n : n + 2]
+    query, numer, denom, inner, out_weight, _, pair_out, *share = refs[n + 2 :]
     tok = mixed.shape[0] // n
     step = min(n, 2)
     for r in range(0, n, step):
         rows = slice(r * tok, (r + step) * tok)
-        spots = [piece for i in range(r, r + step) for piece in (firsts[i][depth:], seconds[i][...])]
-        normed = normalize(mixed[rows] + jnp.concatenate(spots, axis=0).astype(F32))
+        position = jnp.concatenate([ref[...] for ref in spots[r : r + step]], axis=0)
+        normed = normalize(mixed[rows] + position.astype(F32))
         for c in range(2):
             pair_out[c, rows] = dot(normed, weight[c + 1]).astype(BF16)
     if share:
@@ -260,18 +262,17 @@
     key_t = jnp.transpose(agg_key)
     weight = jnp.transpose(qkv_weight, (1, 0, 2))
 
-    cut = (tok - depth) // 2
-    shared, *placed = call(
+    shared, placed = call(
         pack_body,
-        [sds((size, d), BF16) for size in (depth + rows // 2 + n_vars, depth + cut, tok - cut)],
+        [sds((size, d), BF16) for size in (depth + rows // 2 + n_vars, depth + tok)],
         (table, variable_embed, pix, position),
         "pack",
         [pltpu.HBM] * 4,
-        [pltpu.VMEM((n_vars, d), BF16), pltpu.SemaphoreType.DMA((4 + 2 * (d // band_tok),))],
+        [pltpu.VMEM((n_vars, d), BF16), pltpu.SemaphoreType.DMA((3 + 2 * (d // band_tok),))],
     )
     others = range(1, n)
     near = [shifted(shared, "var", r) for r in others]
-    first, second = (outward(x) for x in placed)
+    outer = outward(placed)
     positions = [shifted(position, "var", r) for r in others]
 
     moved = (table, variable_embed, key_t, agg_value, weight, out_weight, position)
@@ -284,13 +285,13 @@
         [pltpu.HBM] * len(moved),
         [pltpu.VMEM((rows, d), BF16), pltpu.VMEM((n_vars, d), BF16), pltpu.SemaphoreType.DMA((len(moved),))],
     )
-    near, positions, _ = lax.optimization_barrier((near, positions, folded[2]))
+    near, _ = lax.optimization_barrier((near, folded[2]))
     packs = [shared] + near
     far = [inward(x[depth : depth + rows // 2]) for x in near]
-    first, _ = lax.optimization_barrier((first, folded[0]))
-    second, _ = lax.optimization_barrier((second, folded[1]))
-    firsts = [first] + [shifted(first, "var", r) for r in others]
-    seconds = [second] + [shifted(second, "var", r) for r in others]
+    outer, _ = lax.optimization_barrier((outer, folded[0]))
+    positions, _ = lax.optimization_barrier((positions, folded[1]))
+    outer_pixs = [outer[:depth]] + [shifted(outer[:depth], "var", r) for r in others]
+    outer_positions = [outer[depth:]] + [outward(x) for x in positions]
     *folded, merged, query, pair = call(
         functools.partial(band_body, n, depth),
         [
@@ -308,16 +309,16 @@
     )
     inner = inward(pair)
     totals = call(begin_body, [sds((band_tok, width), F32)] * 2, (query, pair), "attend_band")
-    *firsts, _ = lax.optimization_barrier((*firsts, totals[0]))
+    *outer_pixs, _ = lax.optimization_barrier((*outer_pixs, totals[0]))
     (mixed,) = call(
-        functools.partial(outer_mix_body, n, depth), [sds((band_tok, d), F32)], (*firsts, *folded), "mix_outer"
-    )
-    *seconds, mixed = lax.optimization_barrier((*seconds, mixed))
+        functools.partial(outer_mix_body, n, depth), [sds((band_tok, d), F32)], (*outer_pixs, *folded), "mix_outer"
+    )
+    (ready,) = call(gate_body, [sds((8, 128), F32)], (mixed, *outer_positions[1:]), "gate")
     spans = [(0, tok * 5 // 8), (tok * 5 // 8, tok)]
     outer_pair, *share = call(
-        functools.partial(outer_body, n, depth),
+        functools.partial(outer_body, n),
         [sds((2, band_tok, width), BF16)] + [sds((spans[0][1], d), BF16)] * (n > 1),
-        (*firsts, *seconds, mixed, weight, query, *totals, inner, out_weight),
+        (*outer_positions, mixed, weight, query, *totals, inner, out_weight, ready),
         "front_outer",
     )
     attended = (query, *totals, inner, outer_pair, out_weight)

time: 33.4 us -> 32.4 us (0.970)
  waiting for transfers between devices: 6.63 us -> 5.87 us
  starting transfers between devices: 13.3 us -> 12.9 us
    ppermute x2, waiting for transfers between devices: 1.53 us -> 0.01 us  [outward(): lax.ppermute(block, 'band', [(i, (i + 1 if i % 2 else i - 1) % n) for i i...]
    ppermute x6 -> x5, starting transfers between devices: 8.66 us -> 7.44 us  [shifted(): lax.ppermute(block, axis, [((i + distance) % n, i) for i in range(n)])]
    ppermute x6 -> x5, waiting for transfers between devices: 5.09 us -> 5.86 us  [shifted(): lax.ppermute(block, axis, [((i + distance) % n, i) for i in range(n)])]
    ppermute x2, starting transfers between devices: 4.51 us -> 5.17 us  [outward(): lax.ppermute(block, 'band', [(i, (i + 1 if i % 2 else i - 1) % n) for i i...]
    pallas_call x8 -> x9, Pallas kernels: 12.3 us -> 12.3 us  [call(): pl.pallas_call(body, out_shape=outs, in_specs=[pl.BlockSpec(memory_space=...]
  transfers between devices with their start and end apart: 10 -> 9, of which waited for: 4 -> 2; matrix products, arithmetic and copies ran while one was open for 0% -> 0% of each run, Pallas kernels for 32% -> 33%
where the time goes in v9:
time: 32.4 us; the launch traced here: 32.1 us
  starting transfers between devices  12.9 us (40%)
  Pallas kernels  12.3 us (38%)
  waiting for transfers between devices  5.87 us (18%)
  other arithmetic  0.77 us (2%)
    pallas_call x9, Pallas kernels, call(): pl.pallas_call(body, out_shape=outs, in_specs=[pl.BlockSpec(memory_space=...  12.3 us
    ppermute x5, starting transfers between devices, shifted(): lax.ppermute(block, axis, [((i + distance) % n, i) for i in range(n)])  7.44 us
    ppermute x5, waiting for transfers between devices, shifted(): lax.ppermute(block, axis, [((i + distance) % n, i) for i in range(n)])  5.86 us
    ppermute x2, starting transfers between devices, outward(): lax.ppermute(block, 'band', [(i, (i + 1 if i % 2 else i - 1) % n) for i i...  5.17 us
    convert_element_type x1, other arithmetic, shards(): return update.astype(BF16)  0.77 us
  transfers between devices with their start and end apart: 9, of which 2 were waited for; matrix products, arithmetic and copies ran while one was open for 0% of the time, Pallas kernels for 33%

profile of v9, /device:TPU:0, one launch (start us, length us, event | category | flops | bytes accessed | tf_op | source)
XLA Modules:
  0.0 32.1 jit_solution(412820383786404332)
XLA Ops:
  0.0 3.0 %collective-permute-start.2 = (bf16[128,1024]{1,0:T(8,128)(2,1)}, bf16[128,1024]{1,0:T(8,128)(2,1)S(1)}, u32[]{:S(2)}, u32[]{:S(2)}) collective-permute-start(bf16[128,1024]{1,0:T(8,128)(2,1)} %refs_6_.1), channel_id=1, source_target_pairs={{1,0},{0,1},{3,2},{2,3},{5,4},{4,5},{7,6},{6,7},{9,8},{8,9},{11,10... | collective-permute-start | bytes 786440 | tf_op jit(solution)/shard_map/ppermute | solution.py:24
  3.0 1.1 %pack.1 = (bf16[104,1024]{1,0:T(8,128)(2,1)S(1)}, bf16[160,1024]{1,0:T(8,128)(2,1)S(1)}) custom-call(bf16[128,1024]{1,0:T(8,128)(2,1)} %bitcast.5, bf16[8,1024]{1,0:T(8,128)(2,1)} %refs_1_.1, bf16[128,256]{1,0:T(8,128)(2,1)} %bitcast.7, bf16[128,1024]{1,0:T(8,128)(2,1)} %refs_6_.1), custom_call_target="tpu_custom_call" | custom-call | tf_op jit(solution)/shard_map/pack/pallas_call | solution.py:42
  4.1 3.8 %collective-permute-start.4 = (bf16[160,1024]{1,0:T(8,128)(2,1)S(1)}, bf16[160,1024]{1,0:T(8,128)(2,1)S(1)}, u32[]{:S(2)}, u32[]{:S(2)}) collective-permute-start(bf16[160,1024]{1,0:T(8,128)(2,1)S(1)} %get-tuple-element.47), channel_id=1, source_target_pairs={{0,30},{2,4},{4,2},{6,8},{8,6},{10,12},{12,10},{14,16},{16,14},{18... | collective-permute-start | bytes 983048 | tf_op jit(solution)/shard_map/ppermute | solution.py:33
  7.9 0.5 %collective-permute-start = (bf16[104,1024]{1,0:T(8,128)(2,1)S(1)}, bf16[104,1024]{1,0:T(8,128)(2,1)S(1)}, u32[]{:S(2)}, u32[]{:S(2)}) collective-permute-start(bf16[104,1024]{1,0:T(8,128)(2,1)S(1)} %get-tuple-element.32.refs_0_), channel_id=1, source_target_pairs={{1,0},{0,1},{3,2},{2,3},{5,4},{4,5},{7,6},{6,7},{9,8},{8,9},{11,10... | collective-permute-start | bytes 638984 | tf_op jit(solution)/shard_map/ppermute | solution.py:24
  8.4 3.0 %stage.1 = (bf16[16,1024]{1,0:T(8,128)(2,1)S(1)}, bf16[1024,1024]{1,0:T(8,128)(2,1)S(1)}, bf16[3,1024,512]{2,1,0:T(8,128)(2,1)S(1)}, bf16[512,1024]{1,0:T(8,128)...) custom-call(bf16[128,1024]{1,0:T(8,128)(2,1)} %bitcast.6, ...), custom_call_target="tpu_custom_call" | custom-call | tf_op jit(solution)/shard_map/stage/pallas_call | solution.py:42
  11.4 0.0 collective-permute-done.2.refs_8_
  11.4 1.4 %collective-permute-start.5 = (bf16[128,1024]{1,0:T(8,128)(2,1)S(1)}, bf16[128,1024]{1,0:T(8,128)(2,1)S(1)}, u32[]{:S(2)}, u32[]{:S(2)}) collective-permute-start(bf16[128,1024]{1,0:T(8,128)(2,1)S(1)} %collective-permute-done.2.refs_8_), channel_id=1, source_target_pairs={{0,30},{2,4},{4,2},{6,8},{8,6},{10,12},{12,10},{14,16},{16,14},{18... | collective-permute-start | bytes 786440 | tf_op jit(solution)/shard_map/ppermute | solution.py:33
  12.8 1.2 %collective-permute-done.refs_1_ = bf16[104,1024]{1,0:T(8,128)(2,1)S(1)} collective-permute-done((bf16[104,1024]{1,0:T(8,128)(2,1)S(1)}, bf16[104,1024]{1,0:T(8,128)(2,1)S(1)}, u32[]{:S(2)}, u32[]{:S(2)}) %collective-permute-start) | collective-permute-done | bytes 213024 | tf_op jit(solution)/shard_map/ppermute | solution.py:24
  14.1 0.1 collective-permute-start.1
  14.1 0.0 collective-permute-done.4
  14.2 1.8 %collective-permute-start.6 = (bf16[32,1024]{1,0:T(8,128)(2,1)S(1)}, bf16[32,1024]{1,0:T(8,128)(2,1)S(1)}, u32[]{:S(2)}, u32[]{:S(2)}) collective-permute-start(bf16[32,1024]{1,0:T(8,128)(2,1)S(1)} %slice.12.refs_0_), channel_id=1, source_target_pairs={{1,0},{0,1},{3,2},{2,3},{5,4},{4,5},{7,6},{6,7},{9,8},{8,9},{11,10... | collective-permute-start | bytes 196616 | tf_op jit(solution)/shard_map/ppermute | solution.py:24
  16.0 0.0 collective-permute-done.1.refs_2_
  16.0 2.8 %front_band.1 = (bf16[1024,256]{1,0:T(8,128)(2,1)S(1)}, bf16[256,1024]{1,0:T(8,128)(2,1)S(1)}, f32[16,256]{1,0:T(8,128)S(1)}, f32[16,16]{1,0:T(8,128)S(1)}, f32[...) custom-call(bf16[104,1024]{1,0:T(8,128)(2,1)S(1)} %get-tuple-element.32.refs_0_, ...), custom_call_target="tpu_custom_call" | custom-call | flops 300000000 | tf_op jit(solution)/shard_map/front_band/pallas_call | solution.py:42
  18.8 0.3 collective-permute-start.3
  19.1 0.8 %attend_band.1 = (f32[256,512]{1,0:T(8,128)S(1)}, f32[256,512]{1,0:T(8,128)S(1)}) custom-call(bf16[256,512]{1,0:T(8,128)(2,1)S(1)} %get-tuple-element.43.query.refs_4_, bf16[2,256,512]{2,1,0:T(8,128)(2,1)S(1)} %get-tuple-element.44.pair), custom_call_target="tpu_custom_call" | custom-call | tf_op jit(solution)/shard_map/attend_band/pallas_call | solution.py:42
  19.9 1.1 %mix_outer.1.refs_0_.refs_2_ = f32[256,1024]{1,0:T(8,128)S(1)} custom-call(bf16[32,1024]{1,0:T(8,128)(2,1)S(1)} %slice.12.refs_0_, bf16[32,1024]{1,0:T(8,128)(2,1)S(1)} %collective-permute-done.6.refs_1_, bf16[1024,256]{1,0:T(8,128)(2,1)S(1)} %get-tuple-element.51.refs_2_, bf16[256,1024]{1,0:T(8,128)(2,1)S(1)} %get-tuple-element.52.refs_3_, ...), custom_call_target="tpu_custom_call" | custom-call | tf_op jit(solution)/shard_map/mix_outer/pallas_call | solution.py:42
  21.0 0.0 collective-permute-done.5.refs_1_
  21.0 1.7 %front_outer.1 = (bf16[2,256,512]{2,1,0:T(8,128)(2,1)S(1)}, bf16[80,1024]{1,0:T(8,128)(2,1)S(1)}) custom-call(bf16[128,1024]{1,0:T(8,128)(2,1)S(1)} %slice.11.refs_0_, bf16[128,1024]{1,0:T(8,128)(2,1)S(1)} %collective-permute-done.5.refs_1_, f32[256,1024]{1,0:T(8,128)S(1)} %mix_outer.1.refs_0_.refs_2_, ...), custom_call_target="tpu_custom_call" | custom-call | tf_op jit(solution)/shard_map/front_outer/pallas_call | solution.py:42
  22.7 1.2 %collective-permute-start.7 = (bf16[80,1024]{1,0:T(8,128)(2,1)S(1)}, bf16[80,1024]{1,0:T(8,128)(2,1)S(1)}, u32[]{:S(2)}, u32[]{:S(2)}) collective-permute-start(bf16[80,1024]{1,0:T(8,128)(2,1)S(1)} %get-tuple-element.58), channel_id=1, source_target_pairs={{1,0},{0,1},{3,2},{2,3},{5,4},{4,5},{7,6},{6,7},{9,8},{8,9},{11,10... | collective-permute-start | bytes 491528 | tf_op jit(solution)/shard_map/ppermute | solution.py:24
  23.9 0.8 %attend_later.1 = bf16[48,1024]{1,0:T(8,128)(2,1)S(1)} custom-call(bf16[256,512]{1,0:T(8,128)(2,1)S(1)} %get-tuple-element.43.query.refs_4_, f32[256,512]{1,0:T(8,128)S(1)} %get-tuple-element.45.refs_5_.numer, f32[256,512]{1,0:T(8,128)S(1)} %get-tuple-element.46.refs_6_.denom, bf16[2,256,512]{2,1,0:T(8,128)(2,1)S(1)} %collective-permute-done.3.refs_7_.inner, ...), custom_call_target="tpu_custom_call" | custom-call | tf_op jit(solution)/shard_map/attend_later/pallas_call | solution.py:42
  24.7 0.9 %collective-permute-start.8 = (bf16[48,1024]{1,0:T(8,128)(2,1)S(1)}, bf16[48,1024]{1,0:T(8,128)(2,1)S(1)}, u32[]{:S(2)}, u32[]{:S(2)}) collective-permute-start(bf16[48,1024]{1,0:T(8,128)(2,1)S(1)} %attend_later.1), channel_id=1, source_target_pairs={{1,0},{0,1},{3,2},{2,3},{5,4},{4,5},{7,6},{6,7},{9,8},{8,9},{11,10... | collective-permute-start | bytes 294920 | tf_op jit(solution)/shard_map/ppermute | solution.py:24
  25.6 1.0 %attend_own.1 = f32[128,1024]{1,0:T(8,128)S(1)} custom-call(bf16[256,512]{1,0:T(8,128)(2,1)S(1)} %get-tuple-element.43.query.refs_4_, f32[256,512]{1,0:T(8,128)S(1)} %get-tuple-element.45.refs_5_.numer, f32[256,512]{1,0:T(8,128)S(1)} %get-tuple-element.46.refs_6_.denom, bf16[2,256,512]{2,1,0:T(8,128)(2,1)S(1)} %collective-permute-done.3.refs_7_.inner, ...), custom_call_target="tpu_custom_call" | custom-call | tf_op jit(solution)/shard_map/attend_own/pallas_call | solution.py:42
  26.7 4.6 %collective-permute-done.8 = bf16[48,1024]{1,0:T(8,128)(2,1)S(1)} collective-permute-done((bf16[48,1024]{1,0:T(8,128)(2,1)S(1)}, bf16[48,1024]{1,0:T(8,128)(2,1)S(1)}, u32[]{:S(2)}, u32[]{:S(2)}) %collective-permute-start.8) | collective-permute-done | bytes 98336 | tf_op jit(solution)/shard_map/ppermute | solution.py:24
  31.3 0.8 %add_convert_fusion = bf16[128,1024]{1,0:T(8,128)(2,1)} fusion(f32[128,1024]{1,0:T(8,128)S(1)} %attend_own.1, bf16[48,1024]{1,0:T(8,128)(2,1)S(1)} %collective-permute-done.8, bf16[80,1024]{1,0:T(8,128)(2,1)S(1)} %collective-permute-done.7), kind=kLoop, calls=%fused_computation | loop fusion | flops 786432 | bytes 1048576 | tf_op jit(solution)/shard_map/convert_element_type | solution.py:336
  (7 shorter events, 0.0 us)
Async XLA Ops:
  0.0 11.4 %collective-permute-start.2 = (bf16[128,1024]{1,0:T(8,128)(2,1)}, bf16[128,1024]{1,0:T(8,128)(2,1)S(1)}, u32[]{:S(2)}, u32[]{:S(2)}) collective-permute-start(bf16[128,1024]{1,0:T(8,128)(2,1)} %refs_6_.1), channel_id=1, source_target_pairs={{1,0},{0,1},{3,2},{2,3},{5,4},{4,5},{7,6},{6,7},{9,8},{8,9},{11,10... | collective-permute-start | bytes 786440 | tf_op jit(solution)/shard_map/ppermute | solution.py:24
  4.1 10.0 %collective-permute-start.4 = (bf16[160,1024]{1,0:T(8,128)(2,1)S(1)}, bf16[160,1024]{1,0:T(8,128)(2,1)S(1)}, u32[]{:S(2)}, u32[]{:S(2)}) collective-permute-start(bf16[160,1024]{1,0:T(8,128)(2,1)S(1)} %get-tuple-element.47), channel_id=1, source_target_pairs={{0,30},{2,4},{4,2},{6,8},{8,6},{10,12},{12,10},{14,16},{16,14},{18... | collective-permute-start | bytes 983048 | tf_op jit(solution)/shard_map/ppermute | solution.py:33
  7.9 6.2 %collective-permute-start = (bf16[104,1024]{1,0:T(8,128)(2,1)S(1)}, bf16[104,1024]{1,0:T(8,128)(2,1)S(1)}, u32[]{:S(2)}, u32[]{:S(2)}) collective-permute-start(bf16[104,1024]{1,0:T(8,128)(2,1)S(1)} %get-tuple-element.32.refs_0_), channel_id=1, source_target_pairs={{1,0},{0,1},{3,2},{2,3},{5,4},{4,5},{7,6},{6,7},{9,8},{8,9},{11,10... | collective-permute-start | bytes 638984 | tf_op jit(solution)/shard_map/ppermute | solution.py:24
  11.4 9.6 %collective-permute-start.5 = (bf16[128,1024]{1,0:T(8,128)(2,1)S(1)}, bf16[128,1024]{1,0:T(8,128)(2,1)S(1)}, u32[]{:S(2)}, u32[]{:S(2)}) collective-permute-start(bf16[128,1024]{1,0:T(8,128)(2,1)S(1)} %collective-permute-done.2.refs_8_), channel_id=1, source_target_pairs={{0,30},{2,4},{4,2},{6,8},{8,6},{10,12},{12,10},{14,16},{16,14},{18... | collective-permute-start | bytes 786440 | tf_op jit(solution)/shard_map/ppermute | solution.py:33
  14.1 1.9 %collective-permute-start.1 = (bf16[64,1024]{1,0:T(8,128)(2,1)S(1)}, bf16[64,1024]{1,0:T(8,128)(2,1)S(1)}, u32[]{:S(2)}, u32[]{:S(2)}) collective-permute-start(bf16[64,1024]{1,0:T(8,128)(2,1)S(1)} %slice.10), channel_id=1, source_target_pairs={{2,0},{0,2},{6,4},{4,6},{10,8},{8,10},{14,12},{12,14},{18,16},{16,... | collective-permute-start | bytes 393224 | tf_op jit(solution)/shard_map/ppermute | solution.py:28
  14.2 5.8 %collective-permute-start.6 = (bf16[32,1024]{1,0:T(8,128)(2,1)S(1)}, bf16[32,1024]{1,0:T(8,128)(2,1)S(1)}, u32[]{:S(2)}, u32[]{:S(2)}) collective-permute-start(bf16[32,1024]{1,0:T(8,128)(2,1)S(1)} %slice.12.refs_0_), channel_id=1, source_target_pairs={{1,0},{0,1},{3,2},{2,3},{5,4},{4,5},{7,6},{6,7},{9,8},{8,9},{11,10... | collective-permute-start | bytes 196616 | tf_op jit(solution)/shard_map/ppermute | solution.py:24
  18.8 2.2 %collective-permute-start.3 = (bf16[2,256,512]{2,1,0:T(8,128)(2,1)S(1)}, bf16[2,256,512]{2,1,0:T(8,128)(2,1)S(1)}, u32[]{:S(2)}, u32[]{:S(2)}) collective-permute-start(bf16[2,256,512]{2,1,0:T(8,128)(2,1)S(1)} %get-tuple-element.44.pair), channel_id=1, source_target_pairs={{2,0},{0,2},{6,4},{4,6},{10,8},{8,10},{14,12},{12,14},{18,16},{16,... | collective-permute-start | bytes 1572872 | tf_op jit(solution)/shard_map/ppermute | solution.py:28
  22.7 8.6 %collective-permute-start.7 = (bf16[80,1024]{1,0:T(8,128)(2,1)S(1)}, bf16[80,1024]{1,0:T(8,128)(2,1)S(1)}, u32[]{:S(2)}, u32[]{:S(2)}) collective-permute-start(bf16[80,1024]{1,0:T(8,128)(2,1)S(1)} %get-tuple-element.58), channel_id=1, source_target_pairs={{1,0},{0,1},{3,2},{2,3},{5,4},{4,5},{7,6},{6,7},{9,8},{8,9},{11,10... | collective-permute-start | bytes 491528 | tf_op jit(solution)/shard_map/ppermute | solution.py:24
  24.7 6.6 %collective-permute-start.8 = (bf16[48,1024]{1,0:T(8,128)(2,1)S(1)}, bf16[48,1024]{1,0:T(8,128)(2,1)S(1)}, u32[]{:S(2)}, u32[]{:S(2)}) collective-permute-start(bf16[48,1024]{1,0:T(8,128)(2,1)S(1)} %attend_later.1), channel_id=1, source_target_pairs={{1,0},{0,1},{3,2},{2,3},{5,4},{4,5},{7,6},{6,7},{9,8},{8,9},{11,10... | collective-permute-start | bytes 294920 | tf_op jit(solution)/shard_map/ppermute | solution.py:24

commit v10 on v9

--- a/solution.py
+++ b/solution.py
@@ -188,14 +188,15 @@
     refs[-1][...] = jnp.zeros(refs[-1].shape, F32)
 
 
-def outer_body(n, *refs):
-    spots, (mixed, weight) = refs[:n], refs[n : n + 2]
-    query, numer, denom, inner, out_weight, _, pair_out, *share = refs[n + 2 :]
+def outer_body(n, depth, *refs):
+    heads, tails, (mixed, weight) = refs[:n], refs[n : 2 * n], refs[2 * n : 2 * n + 2]
+    query, numer, denom, inner, out_weight, _, pair_out, *share = refs[2 * n + 2 :]
     tok = mixed.shape[0] // n
     step = min(n, 2)
     for r in range(0, n, step):
         rows = slice(r * tok, (r + step) * tok)
-        position = jnp.concatenate([ref[...] for ref in spots[r : r + step]], axis=0)
+        spots = [piece for i in range(r, r + step) for piece in (heads[i][depth:], tails[i][...])]
+        position = jnp.concatenate(spots, axis=0)
         normed = normalize(mixed[rows] + position.astype(F32))
         for c in range(2):
             pair_out[c, rows] = dot(normed, weight[c + 1]).astype(BF16)
@@ -290,8 +291,10 @@
     far = [inward(x[depth : depth + rows // 2]) for x in near]
     outer, _ = lax.optimization_barrier((outer, folded[0]))
     positions, _ = lax.optimization_barrier((positions, folded[1]))
-    outer_pixs = [outer[:depth]] + [shifted(outer[:depth], "var", r) for r in others]
-    outer_positions = [outer[depth:]] + [outward(x) for x in positions]
+    lead = 16
+    cut = depth + lead
+    outer_heads = [outer[:cut]] + [shifted(outer[:cut], "var", r) for r in others]
+    outer_tails = [outer[cut:]] + [outward(x[lead:]) for x in positions]
     *folded, merged, query, pair = call(
         functools.partial(band_body, n, depth),
         [
@@ -309,16 +312,16 @@
     )
     inner = inward(pair)
     totals = call(begin_body, [sds((band_tok, width), F32)] * 2, (query, pair), "attend_band")
-    *outer_pixs, _ = lax.optimization_barrier((*outer_pixs, totals[0]))
+    *outer_heads, _ = lax.optimization_barrier((*outer_heads, totals[0]))
     (mixed,) = call(
-        functools.partial(outer_mix_body, n, depth), [sds((band_tok, d), F32)], (*outer_pixs, *folded), "mix_outer"
-    )
-    (ready,) = call(gate_body, [sds((8, 128), F32)], (mixed, *outer_positions[1:]), "gate")
+        functools.partial(outer_mix_body, n, depth), [sds((band_tok, d), F32)], (*outer_heads, *folded), "mix_outer"
+    )
+    (ready,) = call(gate_body, [sds((8, 128), F32)], (mixed, *outer_tails[1:]), "gate")
     spans = [(0, tok * 5 // 8), (tok * 5 // 8, tok)]
     outer_pair, *share = call(
-        functools.partial(outer_body, n),
+        functools.partial(outer_body, n, depth),
         [sds((2, band_tok, width), BF16)] + [sds((spans[0][1], d), BF16)] * (n > 1),
-        (*outer_positions, mixed, weight, query, *totals, inner, out_weight, ready),
+        (*outer_heads, *outer_tails, mixed, weight, query, *totals, inner, out_weight, ready),
         "front_outer",
     )
     attended = (query, *totals, inner, outer_pair, out_weight)

time: 32.4 us -> 32.3 us (level)
  no operation moved by 1% of the time
where the time goes in v10:
time: 32.3 us; the launch traced here: 32 us
  starting transfers between devices  13 us (40%)
  Pallas kernels  12.3 us (38%)
  waiting for transfers between devices  5.78 us (18%)
  other arithmetic  0.76 us (2%)
    pallas_call x9, Pallas kernels, call(): pl.pallas_call(body, out_shape=outs, in_specs=[pl.BlockSpec(memory_space=...  12.3 us
    ppermute x5, starting transfers between devices, shifted(): lax.ppermute(block, axis, [((i + distance) % n, i) for i in range(n)])  7.44 us
    ppermute x5, waiting for transfers between devices, shifted(): lax.ppermute(block, axis, [((i + distance) % n, i) for i in range(n)])  5.77 us
    ppermute x2, starting transfers between devices, outward(): lax.ppermute(block, 'band', [(i, (i + 1 if i % 2 else i - 1) % n) for i i...  5.23 us
    convert_element_type x1, other arithmetic, shards(): return update.astype(BF16)  0.76 us
  transfers between devices with their start and end apart: 9, of which 2 were waited for; matrix products, arithmetic and copies ran while one was open for 0% of the time, Pallas kernels for 33%

profile of v10, /device:TPU:0, one launch (start us, length us, event | category | flops | bytes accessed | tf_op | source)
XLA Modules:
  0.0 32.0 jit_solution(5721477377066477523)
XLA Ops:
  0.0 3.0 %collective-permute-start.2 = (bf16[128,1024]{1,0:T(8,128)(2,1)}, bf16[128,1024]{1,0:T(8,128)(2,1)S(1)}, u32[]{:S(2)}, u32[]{:S(2)}) collective-permute-start(bf16[128,1024]{1,0:T(8,128)(2,1)} %refs_6_.1), channel_id=1, source_target_pairs={{1,0},{0,1},{3,2},{2,3},{5,4},{4,5},{7,6},{6,7},{9,8},{8,9},{11,10... | collective-permute-start | bytes 786440 | tf_op jit(solution)/shard_map/ppermute | solution.py:24
  3.0 1.1 %pack.1 = (bf16[104,1024]{1,0:T(8,128)(2,1)S(1)}, bf16[160,1024]{1,0:T(8,128)(2,1)S(1)}) custom-call(bf16[128,1024]{1,0:T(8,128)(2,1)} %bitcast.5, bf16[8,1024]{1,0:T(8,128)(2,1)} %refs_1_.1, bf16[128,256]{1,0:T(8,128)(2,1)} %bitcast.7, bf16[128,1024]{1,0:T(8,128)(2,1)} %refs_6_.1), custom_call_target="tpu_custom_call" | custom-call | tf_op jit(solution)/shard_map/pack/pallas_call | solution.py:42
  4.1 3.8 %collective-permute-start.4 = (bf16[160,1024]{1,0:T(8,128)(2,1)S(1)}, bf16[160,1024]{1,0:T(8,128)(2,1)S(1)}, u32[]{:S(2)}, u32[]{:S(2)}) collective-permute-start(bf16[160,1024]{1,0:T(8,128)(2,1)S(1)} %get-tuple-element.47), channel_id=1, source_target_pairs={{0,30},{2,4},{4,2},{6,8},{8,6},{10,12},{12,10},{14,16},{16,14},{18... | collective-permute-start | bytes 983048 | tf_op jit(solution)/shard_map/ppermute | solution.py:33
  7.9 0.5 %collective-permute-start = (bf16[104,1024]{1,0:T(8,128)(2,1)S(1)}, bf16[104,1024]{1,0:T(8,128)(2,1)S(1)}, u32[]{:S(2)}, u32[]{:S(2)}) collective-permute-start(bf16[104,1024]{1,0:T(8,128)(2,1)S(1)} %get-tuple-element.32.refs_0_), channel_id=1, source_target_pairs={{1,0},{0,1},{3,2},{2,3},{5,4},{4,5},{7,6},{6,7},{9,8},{8,9},{11,10... | collective-permute-start | bytes 638984 | tf_op jit(solution)/shard_map/ppermute | solution.py:24
  8.4 3.0 %stage.1 = (bf16[16,1024]{1,0:T(8,128)(2,1)S(1)}, bf16[1024,1024]{1,0:T(8,128)(2,1)S(1)}, bf16[3,1024,512]{2,1,0:T(8,128)(2,1)S(1)}, bf16[512,1024]{1,0:T(8,128)...) custom-call(bf16[128,1024]{1,0:T(8,128)(2,1)} %bitcast.6, ...), custom_call_target="tpu_custom_call" | custom-call | tf_op jit(solution)/shard_map/stage/pallas_call | solution.py:42
  11.4 0.0 collective-permute-done.2.refs_8_
  11.4 1.5 %collective-permute-start.6 = (bf16[112,1024]{1,0:T(8,128)(2,1)S(1)}, bf16[112,1024]{1,0:T(8,128)(2,1)S(1)}, u32[]{:S(2)}, u32[]{:S(2)}) collective-permute-start(bf16[112,1024]{1,0:T(8,128)(2,1)S(1)} %slice.16), channel_id=1, source_target_pairs={{0,30},{2,4},{4,2},{6,8},{8,6},{10,12},{12,10},{14,16},{16,14},{18... | collective-permute-start | bytes 688136 | tf_op jit(solution)/shard_map/ppermute | solution.py:33
  12.9 1.2 %collective-permute-done.refs_1_ = bf16[104,1024]{1,0:T(8,128)(2,1)S(1)} collective-permute-done((bf16[104,1024]{1,0:T(8,128)(2,1)S(1)}, bf16[104,1024]{1,0:T(8,128)(2,1)S(1)}, u32[]{:S(2)}, u32[]{:S(2)}) %collective-permute-start) | collective-permute-done | bytes 213024 | tf_op jit(solution)/shard_map/ppermute | solution.py:24
  14.1 0.1 collective-permute-start.1
  14.1 0.0 collective-permute-done.4
  14.2 1.8 %collective-permute-start.5 = (bf16[48,1024]{1,0:T(8,128)(2,1)S(1)}, bf16[48,1024]{1,0:T(8,128)(2,1)S(1)}, u32[]{:S(2)}, u32[]{:S(2)}) collective-permute-start(bf16[48,1024]{1,0:T(8,128)(2,1)S(1)} %slice.14.refs_0_), channel_id=1, source_target_pairs={{1,0},{0,1},{3,2},{2,3},{5,4},{4,5},{7,6},{6,7},{9,8},{8,9},{11,10... | collective-permute-start | bytes 294920 | tf_op jit(solution)/shard_map/ppermute | solution.py:24
  16.0 0.0 collective-permute-done.1.refs_2_
  16.0 2.8 %front_band.1 = (bf16[1024,256]{1,0:T(8,128)(2,1)S(1)}, bf16[256,1024]{1,0:T(8,128)(2,1)S(1)}, f32[16,256]{1,0:T(8,128)S(1)}, f32[16,16]{1,0:T(8,128)S(1)}, f32[...) custom-call(bf16[104,1024]{1,0:T(8,128)(2,1)S(1)} %get-tuple-element.32.refs_0_, ...), custom_call_target="tpu_custom_call" | custom-call | flops 300000000 | tf_op jit(solution)/shard_map/front_band/pallas_call | solution.py:42
  18.8 0.3 collective-permute-start.3
  19.1 0.8 %attend_band.1 = (f32[256,512]{1,0:T(8,128)S(1)}, f32[256,512]{1,0:T(8,128)S(1)}) custom-call(bf16[256,512]{1,0:T(8,128)(2,1)S(1)} %get-tuple-element.43.query.refs_6_, bf16[2,256,512]{2,1,0:T(8,128)(2,1)S(1)} %get-tuple-element.44.pair), custom_call_target="tpu_custom_call" | custom-call | tf_op jit(solution)/shard_map/attend_band/pallas_call | solution.py:42
  19.9 0.0 collective-permute-done.5.refs_1_
  19.9 1.0 %mix_outer.1.refs_0_.refs_4_ = f32[256,1024]{1,0:T(8,128)S(1)} custom-call(bf16[48,1024]{1,0:T(8,128)(2,1)S(1)} %slice.14.refs_0_, bf16[48,1024]{1,0:T(8,128)(2,1)S(1)} %collective-permute-done.5.refs_1_, bf16[1024,256]{1,0:T(8,128)(2,1)S(1)} %get-tuple-element.51.refs_2_, bf16[256,1024]{1,0:T(8,128)(2,1)S(1)} %get-tuple-element.52.refs_3_, ...), custom_call_target="tpu_custom_call" | custom-call | tf_op jit(solution)/shard_map/mix_outer/pallas_call | solution.py:42
  21.0 1.7 %front_outer.1 = (bf16[2,256,512]{2,1,0:T(8,128)(2,1)S(1)}, bf16[80,1024]{1,0:T(8,128)(2,1)S(1)}) custom-call(bf16[48,1024]{1,0:T(8,128)(2,1)S(1)} %slice.14.refs_0_, bf16[48,1024]{1,0:T(8,128)(2,1)S(1)} %collective-permute-done.5.refs_1_, bf16[112,1024]{1,0:T(8,128)(2,1)S(1)} %slice.15.refs_2_, ...), custom_call_target="tpu_custom_call" | custom-call | tf_op jit(solution)/shard_map/front_outer/pallas_call | solution.py:42
  22.7 1.3 %collective-permute-start.7 = (bf16[80,1024]{1,0:T(8,128)(2,1)S(1)}, bf16[80,1024]{1,0:T(8,128)(2,1)S(1)}, u32[]{:S(2)}, u32[]{:S(2)}) collective-permute-start(bf16[80,1024]{1,0:T(8,128)(2,1)S(1)} %get-tuple-element.58), channel_id=1, source_target_pairs={{1,0},{0,1},{3,2},{2,3},{5,4},{4,5},{7,6},{6,7},{9,8},{8,9},{11,10... | collective-permute-start | bytes 491528 | tf_op jit(solution)/shard_map/ppermute | solution.py:24
  24.0 0.8 %attend_later.1 = bf16[48,1024]{1,0:T(8,128)(2,1)S(1)} custom-call(bf16[256,512]{1,0:T(8,128)(2,1)S(1)} %get-tuple-element.43.query.refs_6_, f32[256,512]{1,0:T(8,128)S(1)} %get-tuple-element.45.refs_7_.numer, f32[256,512]{1,0:T(8,128)S(1)} %get-tuple-element.46.refs_8_.denom, bf16[2,256,512]{2,1,0:T(8,128)(2,1)S(1)} %collective-permute-done.3.refs_9_.inner, ...), custom_call_target="tpu_custom_call" | custom-call | tf_op jit(solution)/shard_map/attend_later/pallas_call | solution.py:42
  24.7 0.9 %collective-permute-start.8 = (bf16[48,1024]{1,0:T(8,128)(2,1)S(1)}, bf16[48,1024]{1,0:T(8,128)(2,1)S(1)}, u32[]{:S(2)}, u32[]{:S(2)}) collective-permute-start(bf16[48,1024]{1,0:T(8,128)(2,1)S(1)} %attend_later.1), channel_id=1, source_target_pairs={{1,0},{0,1},{3,2},{2,3},{5,4},{4,5},{7,6},{6,7},{9,8},{8,9},{11,10... | collective-permute-start | bytes 294920 | tf_op jit(solution)/shard_map/ppermute | solution.py:24
  25.6 1.0 %attend_own.1 = f32[128,1024]{1,0:T(8,128)S(1)} custom-call(bf16[256,512]{1,0:T(8,128)(2,1)S(1)} %get-tuple-element.43.query.refs_6_, f32[256,512]{1,0:T(8,128)S(1)} %get-tuple-element.45.refs_7_.numer, f32[256,512]{1,0:T(8,128)S(1)} %get-tuple-element.46.refs_8_.denom, bf16[2,256,512]{2,1,0:T(8,128)(2,1)S(1)} %collective-permute-done.3.refs_9_.inner, ...), custom_call_target="tpu_custom_call" | custom-call | tf_op jit(solution)/shard_map/attend_own/pallas_call | solution.py:42
  26.7 4.6 %collective-permute-done.8 = bf16[48,1024]{1,0:T(8,128)(2,1)S(1)} collective-permute-done((bf16[48,1024]{1,0:T(8,128)(2,1)S(1)}, bf16[48,1024]{1,0:T(8,128)(2,1)S(1)}, u32[]{:S(2)}, u32[]{:S(2)}) %collective-permute-start.8) | collective-permute-done | bytes 98336 | tf_op jit(solution)/shard_map/ppermute | solution.py:24
  31.3 0.8 %add_convert_fusion = bf16[128,1024]{1,0:T(8,128)(2,1)} fusion(f32[128,1024]{1,0:T(8,128)S(1)} %attend_own.1, bf16[48,1024]{1,0:T(8,128)(2,1)S(1)} %collective-permute-done.8, bf16[80,1024]{1,0:T(8,128)(2,1)S(1)} %collective-permute-done.7), kind=kLoop, calls=%fused_computation | loop fusion | flops 786432 | bytes 1048576 | tf_op jit(solution)/shard_map/convert_element_type | solution.py:339
  (8 shorter events, 0.1 us)
Async XLA Ops:
  0.0 11.4 %collective-permute-start.2 = (bf16[128,1024]{1,0:T(8,128)(2,1)}, bf16[128,1024]{1,0:T(8,128)(2,1)S(1)}, u32[]{:S(2)}, u32[]{:S(2)}) collective-permute-start(bf16[128,1024]{1,0:T(8,128)(2,1)} %refs_6_.1), channel_id=1, source_target_pairs={{1,0},{0,1},{3,2},{2,3},{5,4},{4,5},{7,6},{6,7},{9,8},{8,9},{11,10... | collective-permute-start | bytes 786440 | tf_op jit(solution)/shard_map/ppermute | solution.py:24
  4.1 10.0 %collective-permute-start.4 = (bf16[160,1024]{1,0:T(8,128)(2,1)S(1)}, bf16[160,1024]{1,0:T(8,128)(2,1)S(1)}, u32[]{:S(2)}, u32[]{:S(2)}) collective-permute-start(bf16[160,1024]{1,0:T(8,128)(2,1)S(1)} %get-tuple-element.47), channel_id=1, source_target_pairs={{0,30},{2,4},{4,2},{6,8},{8,6},{10,12},{12,10},{14,16},{16,14},{18... | collective-permute-start | bytes 983048 | tf_op jit(solution)/shard_map/ppermute | solution.py:33
  7.9 6.2 %collective-permute-start = (bf16[104,1024]{1,0:T(8,128)(2,1)S(1)}, bf16[104,1024]{1,0:T(8,128)(2,1)S(1)}, u32[]{:S(2)}, u32[]{:S(2)}) collective-permute-start(bf16[104,1024]{1,0:T(8,128)(2,1)S(1)} %get-tuple-element.32.refs_0_), channel_id=1, source_target_pairs={{1,0},{0,1},{3,2},{2,3},{5,4},{4,5},{7,6},{6,7},{9,8},{8,9},{11,10... | collective-permute-start | bytes 638984 | tf_op jit(solution)/shard_map/ppermute | solution.py:24
  11.4 9.6 %collective-permute-start.6 = (bf16[112,1024]{1,0:T(8,128)(2,1)S(1)}, bf16[112,1024]{1,0:T(8,128)(2,1)S(1)}, u32[]{:S(2)}, u32[]{:S(2)}) collective-permute-start(bf16[112,1024]{1,0:T(8,128)(2,1)S(1)} %slice.16), channel_id=1, source_target_pairs={{0,30},{2,4},{4,2},{6,8},{8,6},{10,12},{12,10},{14,16},{16,14},{18... | collective-permute-start | bytes 688136 | tf_op jit(solution)/shard_map/ppermute | solution.py:33
  14.1 1.9 %collective-permute-start.1 = (bf16[64,1024]{1,0:T(8,128)(2,1)S(1)}, bf16[64,1024]{1,0:T(8,128)(2,1)S(1)}, u32[]{:S(2)}, u32[]{:S(2)}) collective-permute-start(bf16[64,1024]{1,0:T(8,128)(2,1)S(1)} %slice.13), channel_id=1, source_target_pairs={{2,0},{0,2},{6,4},{4,6},{10,8},{8,10},{14,12},{12,14},{18,16},{16,... | collective-permute-start | bytes 393224 | tf_op jit(solution)/shard_map/ppermute | solution.py:28
  14.2 5.8 %collective-permute-start.5 = (bf16[48,1024]{1,0:T(8,128)(2,1)S(1)}, bf16[48,1024]{1,0:T(8,128)(2,1)S(1)}, u32[]{:S(2)}, u32[]{:S(2)}) collective-permute-start(bf16[48,1024]{1,0:T(8,128)(2,1)S(1)} %slice.14.refs_0_), channel_id=1, source_target_pairs={{1,0},{0,1},{3,2},{2,3},{5,4},{4,5},{7,6},{6,7},{9,8},{8,9},{11,10... | collective-permute-start | bytes 294920 | tf_op jit(solution)/shard_map/ppermute | solution.py:24
  18.8 2.2 %collective-permute-start.3 = (bf16[2,256,512]{2,1,0:T(8,128)(2,1)S(1)}, bf16[2,256,512]{2,1,0:T(8,128)(2,1)S(1)}, u32[]{:S(2)}, u32[]{:S(2)}) collective-permute-start(bf16[2,256,512]{2,1,0:T(8,128)(2,1)S(1)} %get-tuple-element.44.pair), channel_id=1, source_target_pairs={{2,0},{0,2},{6,4},{4,6},{10,8},{8,10},{14,12},{12,14},{18,16},{16,... | collective-permute-start | bytes 1572872 | tf_op jit(solution)/shard_map/ppermute | solution.py:28
  22.7 8.6 %collective-permute-start.7 = (bf16[80,1024]{1,0:T(8,128)(2,1)S(1)}, bf16[80,1024]{1,0:T(8,128)(2,1)S(1)}, u32[]{:S(2)}, u32[]{:S(2)}) collective-permute-start(bf16[80,1024]{1,0:T(8,128)(2,1)S(1)} %get-tuple-element.58), channel_id=1, source_target_pairs={{1,0},{0,1},{3,2},{2,3},{5,4},{4,5},{7,6},{6,7},{9,8},{8,9},{11,10... | collective-permute-start | bytes 491528 | tf_op jit(solution)/shard_map/ppermute | solution.py:24
  24.7 6.5 %collective-permute-start.8 = (bf16[48,1024]{1,0:T(8,128)(2,1)S(1)}, bf16[48,1024]{1,0:T(8,128)(2,1)S(1)}, u32[]{:S(2)}, u32[]{:S(2)}) collective-permute-start(bf16[48,1024]{1,0:T(8,128)(2,1)S(1)} %attend_later.1), channel_id=1, source_target_pairs={{1,0},{0,1},{3,2},{2,3},{5,4},{4,5},{7,6},{6,7},{9,8},{8,9},{11,10... | collective-permute-start | bytes 294920 | tf_op jit(solution)/shard_map/ppermute | solution.py:24

commit v11 on v10

--- a/solution.py
+++ b/solution.py
@@ -137,6 +137,10 @@
     return (centred * lax.rsqrt(spread + EPSILON)).astype(BF16)
 
 
+def query_of(normed, weight):
+    return (dot(normed, weight[0]).astype(BF16) * HEAD_DIM ** (-0.5)).astype(BF16)
+
+
 def aggregates(packs, folded, tok, depth):
     n = len(packs)
     step = min(n, 2)
@@ -156,7 +160,7 @@
 def band_body(n, depth, *refs):
     packs, far, mine = refs[:n], refs[n : 2 * n - 1], refs[2 * n - 1 : 2 * n + 3]
     positions, (key_t, agg_value, weight) = refs[2 * n + 3 : 3 * n + 3], refs[3 * n + 3 : 3 * n + 6]
-    *folded, merged_out, query_out, pair_out, table = refs[3 * n + 6 :]
+    *folded, merged_out, normed_out, query_out, pair_out, table = refs[3 * n + 6 :]
     tok = merged_out.shape[0]
     half = table.shape[0] // 2
     side = lax.rem(lax.axis_index("band"), 2)
@@ -170,10 +174,14 @@
     for rows, merged in aggregates(packs, folded, tok, depth):
         spots = positions[rows.start // tok : rows.stop // tok]
         merged = merged + jnp.concatenate([ref[...] for ref in spots], axis=0).astype(F32)
+        normed = normalize(merged)
+        rest = normed
         if rows.start == 0:
             merged_out[...] = merged[:tok]
-        normed = normalize(merged)
-        query_out[rows] = (dot(normed, weight[0]).astype(BF16) * HEAD_DIM ** (-0.5)).astype(BF16)
+            normed_out[...] = normed[:tok]
+            rest = normed[tok:]
+        if rest.shape[0] > 0:
+            query_out[rows.stop - rest.shape[0] - tok : rows.stop - tok] = query_of(rest, weight)
         for c in range(2):
             pair_out[c, rows] = dot(normed, weight[c + 1]).astype(BF16)
 
@@ -201,7 +209,7 @@
         for c in range(2):
             pair_out[c, rows] = dot(normed, weight[c + 1]).astype(BF16)
     if share:
-        finish_body(tok, query, numer, denom, inner, pair_out, out_weight, share[0])
+        finish_body(0, query, numer, denom, inner, pair_out, out_weight, share[0])
 
 
 def absorb(query, pairs):
@@ -236,15 +244,16 @@
         numer[rows], denom[rows] = absorb(query[rows], [pair])
 
 
-def finish_body(first, query, numer, denom, inner, outer, out_weight, *refs):
-    out = refs[-1]
+def finish_body(first, query, numer, denom, inner, outer, out_weight, out):
     rows = slice(first, first + out.shape[0])
     top, low = absorb(query[rows], [inner, outer])
     context = ((numer[rows] + top) / (denom[rows] + low)).astype(BF16)
-    update = dot(context, out_weight[...])
-    for ref in refs[:-1]:
-        update = update + ref[...]
-    out[...] = update.astype(out.dtype)
+    out[...] = dot(context, out_weight[...]).astype(out.dtype)
+
+
+def own_body(normed, weight, pair, inner, outer, out_weight, merged, out):
+    top, low = absorb(query_of(normed[...], weight), [pair, inner, outer])
+    out[...] = merged[...] + dot((top / low).astype(BF16), out_weight[...])
 
 
 def shards(pixels, embed_weight, variable_embed, agg_key, agg_value, position, qkv_weight, out_weight):
@@ -295,7 +304,7 @@
     cut = depth + lead
     outer_heads = [outer[:cut]] + [shifted(outer[:cut], "var", r) for r in others]
     outer_tails = [outer[cut:]] + [outward(x[lead:]) for x in positions]
-    *folded, merged, query, pair = call(
+    *folded, merged, normed, query, pair = call(
         functools.partial(band_body, n, depth),
         [
             sds((d, rows * n), BF16),
@@ -303,7 +312,8 @@
             sds((n_heads, rows * n), F32),
             sds((n_heads, all_vars), F32),
             sds((tok, d), F32),
-            sds((band_tok, width), BF16),
+            sds((tok, d), BF16),
+            sds((band_tok - tok, width), BF16),
             sds((2, band_tok, width), BF16),
         ],
         (*packs, *far, *folded, position, *positions, key_t, agg_value, weight),
@@ -311,7 +321,7 @@
         scratch=[pltpu.VMEM((rows, d), BF16)],
     )
     inner = inward(pair)
-    totals = call(begin_body, [sds((band_tok, width), F32)] * 2, (query, pair), "attend_band")
+    totals = call(begin_body, [sds((band_tok - tok, width), F32)] * 2, (query, pair), "attend_band")
     *outer_heads, _ = lax.optimization_barrier((*outer_heads, totals[0]))
     (mixed,) = call(
         functools.partial(outer_mix_body, n, depth), [sds((band_tok, d), F32)], (*outer_heads, *folded), "mix_outer"
@@ -330,10 +340,12 @@
         for i, (start, stop) in enumerate(spans):
             if r > 1 or i > 0:
                 share = call(
-                    functools.partial(finish_body, r * tok + start), [sds((stop - start, d), BF16)], attended, "attend_later"
+                    functools.partial(finish_body, (r - 1) * tok + start), [sds((stop - start, d), BF16)], attended, "attend_later"
                 )
             pieces[r - 1][i] = shifted(share[0], "var", n - r)
-    (update,) = call(functools.partial(finish_body, 0), [sds((tok, d), F32)], (*attended, merged), "attend_own")
+    (update,) = call(
+        own_body, [sds((tok, d), F32)], (normed, weight, pair, inner, outer_pair, out_weight, merged), "attend_own"
+    )
     for parts in pieces:
         update = update + jnp.concatenate(parts, axis=0).astype(F32)
     return update.astype(BF16)

time: 32.3 us -> 31.9 us (0.988)
  waiting for transfers between devices: 5.78 us -> 5.31 us
    ppermute x5, waiting for transfers between devices: 5.77 us -> 5.22 us  [shifted(): lax.ppermute(block, axis, [((i + distance) % n, i) for i in range(n)])]
  transfers between devices with their start and end apart: 9 -> 9, of which waited for: 2 -> 3; matrix products, arithmetic and copies ran while one was open for 0% -> 0% of each run, Pallas kernels for 33% -> 34%
where the time goes in v11:
time: 31.9 us; the launch traced here: 31.6 us
  starting transfers between devices  13 us (41%)
  Pallas kernels  12.3 us (39%)
  waiting for transfers between devices  5.31 us (17%)
  other arithmetic  0.77 us (2%)
    pallas_call x9, Pallas kernels, call(): pl.pallas_call(body, out_shape=outs, in_specs=[pl.BlockSpec(memory_space=...  12.3 us
    ppermute x5, starting transfers between devices, shifted(): lax.ppermute(block, axis, [((i + distance) % n, i) for i in range(n)])  7.44 us
    ppermute x2, starting transfers between devices, outward(): lax.ppermute(block, 'band', [(i, (i + 1 if i % 2 else i - 1) % n) for i i...  5.23 us
    ppermute x5, waiting for transfers between devices, shifted(): lax.ppermute(block, axis, [((i + distance) % n, i) for i in range(n)])  5.22 us
    convert_element_type x1, other arithmetic, shards(): return update.astype(BF16)  0.77 us
  transfers between devices with their start and end apart: 9, of which 3 were waited for; matrix products, arithmetic and copies ran while one was open for 0% of the time, Pallas kernels for 34%

profile of v11, /device:TPU:0, one launch (start us, length us, event | category | flops | bytes accessed | tf_op | source)
XLA Modules:
  0.0 31.6 jit_solution(13685246491904373638)
XLA Ops:
  0.0 3.0 %collective-permute-start.2 = (bf16[128,1024]{1,0:T(8,128)(2,1)}, bf16[128,1024]{1,0:T(8,128)(2,1)S(1)}, u32[]{:S(2)}, u32[]{:S(2)}) collective-permute-start(bf16[128,1024]{1,0:T(8,128)(2,1)} %refs_6_.1), channel_id=1, source_target_pairs={{1,0},{0,1},{3,2},{2,3},{5,4},{4,5},{7,6},{6,7},{9,8},{8,9},{11,10... | collective-permute-start | bytes 786440 | tf_op jit(solution)/shard_map/ppermute | solution.py:24
  3.0 1.1 %pack.1 = (bf16[104,1024]{1,0:T(8,128)(2,1)S(1)}, bf16[160,1024]{1,0:T(8,128)(2,1)S(1)}) custom-call(bf16[128,1024]{1,0:T(8,128)(2,1)} %bitcast.5, bf16[8,1024]{1,0:T(8,128)(2,1)} %refs_1_.1, bf16[128,256]{1,0:T(8,128)(2,1)} %bitcast.7, bf16[128,1024]{1,0:T(8,128)(2,1)} %refs_6_.1), custom_call_target="tpu_custom_call" | custom-call | tf_op jit(solution)/shard_map/pack/pallas_call | solution.py:42
  4.1 3.8 %collective-permute-start.4 = (bf16[160,1024]{1,0:T(8,128)(2,1)S(1)}, bf16[160,1024]{1,0:T(8,128)(2,1)S(1)}, u32[]{:S(2)}, u32[]{:S(2)}) collective-permute-start(bf16[160,1024]{1,0:T(8,128)(2,1)S(1)} %get-tuple-element.46), channel_id=1, source_target_pairs={{0,30},{2,4},{4,2},{6,8},{8,6},{10,12},{12,10},{14,16},{16,14},{18... | collective-permute-start | bytes 983048 | tf_op jit(solution)/shard_map/ppermute | solution.py:33
  7.9 0.5 %collective-permute-start = (bf16[104,1024]{1,0:T(8,128)(2,1)S(1)}, bf16[104,1024]{1,0:T(8,128)(2,1)S(1)}, u32[]{:S(2)}, u32[]{:S(2)}) collective-permute-start(bf16[104,1024]{1,0:T(8,128)(2,1)S(1)} %get-tuple-element.33.refs_0_), channel_id=1, source_target_pairs={{1,0},{0,1},{3,2},{2,3},{5,4},{4,5},{7,6},{6,7},{9,8},{8,9},{11,10... | collective-permute-start | bytes 638984 | tf_op jit(solution)/shard_map/ppermute | solution.py:24
  8.4 3.0 %stage.1 = (bf16[16,1024]{1,0:T(8,128)(2,1)S(1)}, bf16[1024,1024]{1,0:T(8,128)(2,1)S(1)}, bf16[3,1024,512]{2,1,0:T(8,128)(2,1)S(1)}, bf16[512,1024]{1,0:T(8,128)...) custom-call(bf16[128,1024]{1,0:T(8,128)(2,1)} %bitcast.6, ...), custom_call_target="tpu_custom_call" | custom-call | tf_op jit(solution)/shard_map/stage/pallas_call | solution.py:42
  11.4 0.0 collective-permute-done.2.refs_8_
  11.4 1.5 %collective-permute-start.6 = (bf16[112,1024]{1,0:T(8,128)(2,1)S(1)}, bf16[112,1024]{1,0:T(8,128)(2,1)S(1)}, u32[]{:S(2)}, u32[]{:S(2)}) collective-permute-start(bf16[112,1024]{1,0:T(8,128)(2,1)S(1)} %slice.16), channel_id=1, source_target_pairs={{0,30},{2,4},{4,2},{6,8},{8,6},{10,12},{12,10},{14,16},{16,14},{18... | collective-permute-start | bytes 688136 | tf_op jit(solution)/shard_map/ppermute | solution.py:33
  12.9 1.2 %collective-permute-done.refs_1_ = bf16[104,1024]{1,0:T(8,128)(2,1)S(1)} collective-permute-done((bf16[104,1024]{1,0:T(8,128)(2,1)S(1)}, bf16[104,1024]{1,0:T(8,128)(2,1)S(1)}, u32[]{:S(2)}, u32[]{:S(2)}) %collective-permute-start) | collective-permute-done | bytes 213024 | tf_op jit(solution)/shard_map/ppermute | solution.py:24
  14.1 0.1 collective-permute-start.1
  14.1 0.0 collective-permute-done.4
  14.2 1.8 %collective-permute-start.5 = (bf16[48,1024]{1,0:T(8,128)(2,1)S(1)}, bf16[48,1024]{1,0:T(8,128)(2,1)S(1)}, u32[]{:S(2)}, u32[]{:S(2)}) collective-permute-start(bf16[48,1024]{1,0:T(8,128)(2,1)S(1)} %slice.14.refs_0_), channel_id=1, source_target_pairs={{1,0},{0,1},{3,2},{2,3},{5,4},{4,5},{7,6},{6,7},{9,8},{8,9},{11,10... | collective-permute-start | bytes 294920 | tf_op jit(solution)/shard_map/ppermute | solution.py:24
  16.0 0.0 collective-permute-done.1.refs_2_
  16.0 2.7 %front_band.1 = (bf16[1024,256]{1,0:T(8,128)(2,1)S(1)}, bf16[256,1024]{1,0:T(8,128)(2,1)S(1)}, f32[16,256]{1,0:T(8,128)S(1)}, f32[16,16]{1,0:T(8,128)S(1)}, f32[...) custom-call(bf16[104,1024]{1,0:T(8,128)(2,1)S(1)} %get-tuple-element, ...), custom_call_target="tpu_custom_call" | custom-call | flops 300000000 | tf_op jit(solution)/shard_map/front_band/pallas_call | solution.py:42
  18.7 0.3 collective-permute-start.3
  18.9 0.5 %attend_band.1 = (f32[128,512]{1,0:T(8,128)S(1)}, f32[128,512]{1,0:T(8,128)S(1)}) custom-call(bf16[128,512]{1,0:T(8,128)(2,1)S(1)} %get-tuple-element.48.query.refs_6_, bf16[2,256,512]{2,1,0:T(8,128)(2,1)S(1)} %get-tuple-element.45.pair), custom_call_target="tpu_custom_call" | custom-call | tf_op jit(solution)/shard_map/attend_band/pallas_call | solution.py:42
  19.5 1.0 %mix_outer.1.refs_0_.refs_4_ = f32[256,1024]{1,0:T(8,128)S(1)} custom-call(bf16[48,1024]{1,0:T(8,128)(2,1)S(1)} %slice.14.refs_0_, bf16[48,1024]{1,0:T(8,128)(2,1)S(1)} %collective-permute-done.5.refs_1_, bf16[1024,256]{1,0:T(8,128)(2,1)S(1)} %get-tuple-element.52.refs_2_, bf16[256,1024]{1,0:T(8,128)(2,1)S(1)} %get-tuple-element.53.refs_3_, ...), custom_call_target="tpu_custom_call" | custom-call | tf_op jit(solution)/shard_map/mix_outer/pallas_call | solution.py:42
  20.6 0.1 collective-permute-done.3.refs_9_.inner
  20.6 1.7 %front_outer.1 = (bf16[2,256,512]{2,1,0:T(8,128)(2,1)S(1)}, bf16[80,1024]{1,0:T(8,128)(2,1)S(1)}) custom-call(bf16[48,1024]{1,0:T(8,128)(2,1)S(1)} %slice.14.refs_0_, bf16[48,1024]{1,0:T(8,128)(2,1)S(1)} %collective-permute-done.5.refs_1_, bf16[112,1024]{1,0:T(8,128)(2,1)S(1)} %slice.15.refs_2_, ...), custom_call_target="tpu_custom_call" | custom-call | tf_op jit(solution)/shard_map/front_outer/pallas_call | solution.py:42
  22.3 1.7 %collective-permute-start.7 = (bf16[80,1024]{1,0:T(8,128)(2,1)S(1)}, bf16[80,1024]{1,0:T(8,128)(2,1)S(1)}, u32[]{:S(2)}, u32[]{:S(2)}) collective-permute-start(bf16[80,1024]{1,0:T(8,128)(2,1)S(1)} %get-tuple-element.60), channel_id=1, source_target_pairs={{1,0},{0,1},{3,2},{2,3},{5,4},{4,5},{7,6},{6,7},{9,8},{8,9},{11,10... | collective-permute-start | bytes 491528 | tf_op jit(solution)/shard_map/ppermute | solution.py:24
  24.0 0.8 %attend_later.1 = bf16[48,1024]{1,0:T(8,128)(2,1)S(1)} custom-call(bf16[128,512]{1,0:T(8,128)(2,1)S(1)} %get-tuple-element.48.query.refs_6_, f32[128,512]{1,0:T(8,128)S(1)} %get-tuple-element.49.refs_7_.numer, f32[128,512]{1,0:T(8,128)S(1)} %get-tuple-element.56.refs_8_.denom, bf16[2,256,512]{2,1,0:T(8,128)(2,1)S(1)} %collective-permute-done.3.refs_9_.inner, ...), custom_call_target="tpu_custom_call" | custom-call | tf_op jit(solution)/shard_map/attend_later/pallas_call | solution.py:42
  24.8 0.5 %collective-permute-start.8 = (bf16[48,1024]{1,0:T(8,128)(2,1)S(1)}, bf16[48,1024]{1,0:T(8,128)(2,1)S(1)}, u32[]{:S(2)}, u32[]{:S(2)}) collective-permute-start(bf16[48,1024]{1,0:T(8,128)(2,1)S(1)} %attend_later.1), channel_id=1, source_target_pairs={{1,0},{0,1},{3,2},{2,3},{5,4},{4,5},{7,6},{6,7},{9,8},{8,9},{11,10... | collective-permute-start | bytes 294920 | tf_op jit(solution)/shard_map/ppermute | solution.py:24
  25.2 1.5 %attend_own.1 = f32[128,1024]{1,0:T(8,128)S(1)} custom-call(bf16[128,1024]{1,0:T(8,128)(2,1)S(1)} %get-tuple-element.44.normed, bf16[3,1024,512]{2,1,0:T(8,128)(2,1)S(1)} %get-tuple-element.43.refs_11_.refs_5_.weight, bf16[2,256,512]{2,1,0:T(8,128)(2,1)S(1)} %get-tuple-element.45.pair, bf16[2,256,512]{2,1,0:T(8,128)(2,1)S(1)} %collective-permute-done.3.refs_9_.inner, ...), custom_call_target="tpu_custom_call" | custom-call | tf_op jit(solution)/shard_map/attend_own/pallas_call | solution.py:42
  26.8 4.1 %collective-permute-done.8 = bf16[48,1024]{1,0:T(8,128)(2,1)S(1)} collective-permute-done((bf16[48,1024]{1,0:T(8,128)(2,1)S(1)}, bf16[48,1024]{1,0:T(8,128)(2,1)S(1)}, u32[]{:S(2)}, u32[]{:S(2)}) %collective-permute-start.8) | collective-permute-done | bytes 98336 | tf_op jit(solution)/shard_map/ppermute | solution.py:24
  30.9 0.8 %add_convert_fusion = bf16[128,1024]{1,0:T(8,128)(2,1)} fusion(f32[128,1024]{1,0:T(8,128)S(1)} %attend_own.1, bf16[48,1024]{1,0:T(8,128)(2,1)S(1)} %collective-permute-done.8, bf16[80,1024]{1,0:T(8,128)(2,1)S(1)} %collective-permute-done.7), kind=kLoop, calls=%fused_computation | loop fusion | flops 786432 | bytes 1048576 | tf_op jit(solution)/shard_map/convert_element_type | solution.py:351
  (8 shorter events, 0.1 us)
Async XLA Ops:
  0.0 11.4 %collective-permute-start.2 = (bf16[128,1024]{1,0:T(8,128)(2,1)}, bf16[128,1024]{1,0:T(8,128)(2,1)S(1)}, u32[]{:S(2)}, u32[]{:S(2)}) collective-permute-start(bf16[128,1024]{1,0:T(8,128)(2,1)} %refs_6_.1), channel_id=1, source_target_pairs={{1,0},{0,1},{3,2},{2,3},{5,4},{4,5},{7,6},{6,7},{9,8},{8,9},{11,10... | collective-permute-start | bytes 786440 | tf_op jit(solution)/shard_map/ppermute | solution.py:24
  4.1 10.0 %collective-permute-start.4 = (bf16[160,1024]{1,0:T(8,128)(2,1)S(1)}, bf16[160,1024]{1,0:T(8,128)(2,1)S(1)}, u32[]{:S(2)}, u32[]{:S(2)}) collective-permute-start(bf16[160,1024]{1,0:T(8,128)(2,1)S(1)} %get-tuple-element.46), channel_id=1, source_target_pairs={{0,30},{2,4},{4,2},{6,8},{8,6},{10,12},{12,10},{14,16},{16,14},{18... | collective-permute-start | bytes 983048 | tf_op jit(solution)/shard_map/ppermute | solution.py:33
  7.9 6.2 %collective-permute-start = (bf16[104,1024]{1,0:T(8,128)(2,1)S(1)}, bf16[104,1024]{1,0:T(8,128)(2,1)S(1)}, u32[]{:S(2)}, u32[]{:S(2)}) collective-permute-start(bf16[104,1024]{1,0:T(8,128)(2,1)S(1)} %get-tuple-element.33.refs_0_), channel_id=1, source_target_pairs={{1,0},{0,1},{3,2},{2,3},{5,4},{4,5},{7,6},{6,7},{9,8},{8,9},{11,10... | collective-permute-start | bytes 638984 | tf_op jit(solution)/shard_map/ppermute | solution.py:24
  11.4 9.1 %collective-permute-start.6 = (bf16[112,1024]{1,0:T(8,128)(2,1)S(1)}, bf16[112,1024]{1,0:T(8,128)(2,1)S(1)}, u32[]{:S(2)}, u32[]{:S(2)}) collective-permute-start(bf16[112,1024]{1,0:T(8,128)(2,1)S(1)} %slice.16), channel_id=1, source_target_pairs={{0,30},{2,4},{4,2},{6,8},{8,6},{10,12},{12,10},{14,16},{16,14},{18... | collective-permute-start | bytes 688136 | tf_op jit(solution)/shard_map/ppermute | solution.py:33
  14.1 1.9 %collective-permute-start.1 = (bf16[64,1024]{1,0:T(8,128)(2,1)S(1)}, bf16[64,1024]{1,0:T(8,128)(2,1)S(1)}, u32[]{:S(2)}, u32[]{:S(2)}) collective-permute-start(bf16[64,1024]{1,0:T(8,128)(2,1)S(1)} %slice.13), channel_id=1, source_target_pairs={{2,0},{0,2},{6,4},{4,6},{10,8},{8,10},{14,12},{12,14},{18,16},{16,... | collective-permute-start | bytes 393224 | tf_op jit(solution)/shard_map/ppermute | solution.py:28
  14.2 5.3 %collective-permute-start.5 = (bf16[48,1024]{1,0:T(8,128)(2,1)S(1)}, bf16[48,1024]{1,0:T(8,128)(2,1)S(1)}, u32[]{:S(2)}, u32[]{:S(2)}) collective-permute-start(bf16[48,1024]{1,0:T(8,128)(2,1)S(1)} %slice.14.refs_0_), channel_id=1, source_target_pairs={{1,0},{0,1},{3,2},{2,3},{5,4},{4,5},{7,6},{6,7},{9,8},{8,9},{11,10... | collective-permute-start | bytes 294920 | tf_op jit(solution)/shard_map/ppermute | solution.py:24
  18.7 2.0 %collective-permute-start.3 = (bf16[2,256,512]{2,1,0:T(8,128)(2,1)S(1)}, bf16[2,256,512]{2,1,0:T(8,128)(2,1)S(1)}, u32[]{:S(2)}, u32[]{:S(2)}) collective-permute-start(bf16[2,256,512]{2,1,0:T(8,128)(2,1)S(1)} %get-tuple-element.45.pair), channel_id=1, source_target_pairs={{2,0},{0,2},{6,4},{4,6},{10,8},{8,10},{14,12},{12,14},{18,16},{16,... | collective-permute-start | bytes 1572872 | tf_op jit(solution)/shard_map/ppermute | solution.py:28
  22.3 8.5 %collective-permute-start.7 = (bf16[80,1024]{1,0:T(8,128)(2,1)S(1)}, bf16[80,1024]{1,0:T(8,128)(2,1)S(1)}, u32[]{:S(2)}, u32[]{:S(2)}) collective-permute-start(bf16[80,1024]{1,0:T(8,128)(2,1)S(1)} %get-tuple-element.60), channel_id=1, source_target_pairs={{1,0},{0,1},{3,2},{2,3},{5,4},{4,5},{7,6},{6,7},{9,8},{8,9},{11,10... | collective-permute-start | bytes 491528 | tf_op jit(solution)/shard_map/ppermute | solution.py:24
  24.8 6.1 %collective-permute-start.8 = (bf16[48,1024]{1,0:T(8,128)(2,1)S(1)}, bf16[48,1024]{1,0:T(8,128)(2,1)S(1)}, u32[]{:S(2)}, u32[]{:S(2)}) collective-permute-start(bf16[48,1024]{1,0:T(8,128)(2,1)S(1)} %attend_later.1), channel_id=1, source_target_pairs={{1,0},{0,1},{3,2},{2,3},{5,4},{4,5},{7,6},{6,7},{9,8},{8,9},{11,10... | collective-permute-start | bytes 294920 | tf_op jit(solution)/shard_map/ppermute | solution.py:24

commit v12 on v11

--- a/solution.py
+++ b/solution.py
@@ -173,7 +173,7 @@
         out[...] = jnp.concatenate(shares, axis=0 if out is folded[1] else 1)
     for rows, merged in aggregates(packs, folded, tok, depth):
         spots = positions[rows.start // tok : rows.stop // tok]
-        merged = merged + jnp.concatenate([ref[...] for ref in spots], axis=0).astype(F32)
+        merged = merged + jnp.concatenate([ref[ref.shape[0] - tok :] for ref in spots], axis=0).astype(F32)
         normed = normalize(merged)
         rest = normed
         if rows.start == 0:
@@ -240,7 +240,7 @@
 
 def begin_body(query, pair, numer, denom):
     for r in range(0, query.shape[0], 256):
-        rows = slice(r, r + 256)
+        rows = slice(r, min(r + 256, query.shape[0]))
         numer[rows], denom[rows] = absorb(query[rows], [pair])
 
 
@@ -285,8 +285,8 @@
     outer = outward(placed)
     positions = [shifted(position, "var", r) for r in others]
 
-    moved = (table, variable_embed, key_t, agg_value, weight, out_weight, position)
-    key_t, agg_value, weight, out_weight, position, *folded = call(
+    moved = (table, variable_embed, key_t, agg_value, weight, out_weight)
+    key_t, agg_value, weight, out_weight, *folded = call(
         functools.partial(stage_body, len(moved)),
         [sds(a.shape, a.dtype) for a in moved[2:]]
         + [sds((d, rows), BF16), sds((n_vars * n_heads, d), BF16), sds((n_heads, rows), F32), sds((n_heads, n_vars), F32)],
@@ -316,7 +316,7 @@
             sds((band_tok - tok, width), BF16),
             sds((2, band_tok, width), BF16),
         ],
-        (*packs, *far, *folded, position, *positions, key_t, agg_value, weight),
+        (*packs, *far, *folded, placed, *positions, key_t, agg_value, weight),
         "front_band",
         scratch=[pltpu.VMEM((rows, d), BF16)],
     )

time: 31.9 us -> 31.9 us (level)
  no operation moved by 1% of the time
where the time goes in v12:
time: 31.9 us; the launch traced here: 31.6 us
  starting transfers between devices  13 us (41%)
  Pallas kernels  12.3 us (39%)
  waiting for transfers between devices  5.31 us (17%)
  other arithmetic  0.76 us (2%)
    pallas_call x9, Pallas kernels, call(): pl.pallas_call(body, out_shape=outs, in_specs=[pl.BlockSpec(memory_space=...  12.3 us
    ppermute x5, starting transfers between devices, shifted(): lax.ppermute(block, axis, [((i + distance) % n, i) for i in range(n)])  7.44 us
    ppermute x2, starting transfers between devices, outward(): lax.ppermute(block, 'band', [(i, (i + 1 if i % 2 else i - 1) % n) for i i...  5.25 us
    ppermute x5, waiting for transfers between devices, shifted(): lax.ppermute(block, axis, [((i + distance) % n, i) for i in range(n)])  5.23 us
    convert_element_type x1, other arithmetic, shards(): return update.astype(BF16)  0.76 us
  transfers between devices with their start and end apart: 9, of which 3 were waited for; matrix products, arithmetic and copies ran while one was open for 0% of the time, Pallas kernels for 34%

profile of v12, /device:TPU:0, one launch (start us, length us, event | category | flops | bytes accessed | tf_op | source)
XLA Modules:
  0.0 31.6 jit_solution(17797606984366648449)
XLA Ops:
  0.0 3.0 %collective-permute-start.2 = (bf16[128,1024]{1,0:T(8,128)(2,1)}, bf16[128,1024]{1,0:T(8,128)(2,1)S(1)}, u32[]{:S(2)}, u32[]{:S(2)}) collective-permute-start(bf16[128,1024]{1,0:T(8,128)(2,1)} %position.1), channel_id=1, source_target_pairs={{1,0},{0,1},{3,2},{2,3},{5,4},{4,5},{7,6},{6,7},{9,8},{8,9},{11,10... | collective-permute-start | bytes 786440 | tf_op jit(solution)/shard_map/ppermute | solution.py:24
  3.0 1.1 %pack.1 = (bf16[104,1024]{1,0:T(8,128)(2,1)S(1)}, bf16[160,1024]{1,0:T(8,128)(2,1)S(1)}) custom-call(bf16[128,1024]{1,0:T(8,128)(2,1)} %bitcast.5, bf16[8,1024]{1,0:T(8,128)(2,1)} %refs_1_.1, bf16[128,256]{1,0:T(8,128)(2,1)} %bitcast.7, bf16[128,1024]{1,0:T(8,128)(2,1)} %position.1), custom_call_target="tpu_custom_call" | custom-call | tf_op jit(solution)/shard_map/pack/pallas_call | solution.py:42
  4.1 3.8 %collective-permute-start.4 = (bf16[160,1024]{1,0:T(8,128)(2,1)S(1)}, bf16[160,1024]{1,0:T(8,128)(2,1)S(1)}, u32[]{:S(2)}, u32[]{:S(2)}) collective-permute-start(bf16[160,1024]{1,0:T(8,128)(2,1)S(1)} %get-tuple-element.38.refs_7_), channel_id=1, source_target_pairs={{0,30},{2,4},{4,2},{6,8},{8,6},{10,12},{12,10},{14,16},{16,14},{18... | collective-permute-start | bytes 983048 | tf_op jit(solution)/shard_map/ppermute | solution.py:33
  7.9 0.5 %collective-permute-start = (bf16[104,1024]{1,0:T(8,128)(2,1)S(1)}, bf16[104,1024]{1,0:T(8,128)(2,1)S(1)}, u32[]{:S(2)}, u32[]{:S(2)}) collective-permute-start(bf16[104,1024]{1,0:T(8,128)(2,1)S(1)} %get-tuple-element.32.refs_0_), channel_id=1, source_target_pairs={{1,0},{0,1},{3,2},{2,3},{5,4},{4,5},{7,6},{6,7},{9,8},{8,9},{11,10... | collective-permute-start | bytes 638984 | tf_op jit(solution)/shard_map/ppermute | solution.py:24
  8.4 3.0 %stage.1 = (bf16[16,1024]{1,0:T(8,128)(2,1)S(1)}, bf16[1024,1024]{1,0:T(8,128)(2,1)S(1)}, bf16[3,1024,512]{2,1,0:T(8,128)(2,1)S(1)}, bf16[512,1024]{1,0:T(8,128)...) custom-call(bf16[128,1024]{1,0:T(8,128)(2,1)} %bitcast.6, ...), custom_call_target="tpu_custom_call" | custom-call | tf_op jit(solution)/shard_map/stage/pallas_call | solution.py:42
  11.3 0.0 collective-permute-done.2.refs_8_
  11.4 1.5 %collective-permute-start.6 = (bf16[112,1024]{1,0:T(8,128)(2,1)S(1)}, bf16[112,1024]{1,0:T(8,128)(2,1)S(1)}, u32[]{:S(2)}, u32[]{:S(2)}) collective-permute-start(bf16[112,1024]{1,0:T(8,128)(2,1)S(1)} %slice.16), channel_id=1, source_target_pairs={{0,30},{2,4},{4,2},{6,8},{8,6},{10,12},{12,10},{14,16},{16,14},{18... | collective-permute-start | bytes 688136 | tf_op jit(solution)/shard_map/ppermute | solution.py:33
  12.9 1.2 %collective-permute-done.refs_1_ = bf16[104,1024]{1,0:T(8,128)(2,1)S(1)} collective-permute-done((bf16[104,1024]{1,0:T(8,128)(2,1)S(1)}, bf16[104,1024]{1,0:T(8,128)(2,1)S(1)}, u32[]{:S(2)}, u32[]{:S(2)}) %collective-permute-start) | collective-permute-done | bytes 213024 | tf_op jit(solution)/shard_map/ppermute | solution.py:24
  14.1 0.1 collective-permute-start.1
  14.2 1.8 %collective-permute-start.5 = (bf16[48,1024]{1,0:T(8,128)(2,1)S(1)}, bf16[48,1024]{1,0:T(8,128)(2,1)S(1)}, u32[]{:S(2)}, u32[]{:S(2)}) collective-permute-start(bf16[48,1024]{1,0:T(8,128)(2,1)S(1)} %slice.14.refs_0_), channel_id=1, source_target_pairs={{1,0},{0,1},{3,2},{2,3},{5,4},{4,5},{7,6},{6,7},{9,8},{8,9},{11,10... | collective-permute-start | bytes 294920 | tf_op jit(solution)/shard_map/ppermute | solution.py:24
  16.0 0.0 collective-permute-done.1.refs_2_
  16.0 2.7 %front_band.1 = (bf16[1024,256]{1,0:T(8,128)(2,1)S(1)}, bf16[256,1024]{1,0:T(8,128)(2,1)S(1)}, f32[16,256]{1,0:T(8,128)S(1)}, f32[16,16]{1,0:T(8,128)S(1)}, f32[...) custom-call(bf16[104,1024]{1,0:T(8,128)(2,1)S(1)} %get-tuple-element, ...), custom_call_target="tpu_custom_call" | custom-call | flops 300000000 | tf_op jit(solution)/shard_map/front_band/pallas_call | solution.py:42
  18.7 0.3 collective-permute-start.3
  18.9 0.5 %attend_band.1 = (f32[128,512]{1,0:T(8,128)S(1)}, f32[128,512]{1,0:T(8,128)S(1)}) custom-call(bf16[128,512]{1,0:T(8,128)(2,1)S(1)} %get-tuple-element.46.query.refs_6_, bf16[2,256,512]{2,1,0:T(8,128)(2,1)S(1)} %get-tuple-element.44.pair), custom_call_target="tpu_custom_call" | custom-call | tf_op jit(solution)/shard_map/attend_band/pallas_call | solution.py:42
  19.5 1.0 %mix_outer.1.refs_0_.refs_4_ = f32[256,1024]{1,0:T(8,128)S(1)} custom-call(bf16[48,1024]{1,0:T(8,128)(2,1)S(1)} %slice.14.refs_0_, bf16[48,1024]{1,0:T(8,128)(2,1)S(1)} %collective-permute-done.5.refs_1_, bf16[1024,256]{1,0:T(8,128)(2,1)S(1)} %get-tuple-element.50.refs_2_, bf16[256,1024]{1,0:T(8,128)(2,1)S(1)} %get-tuple-element.51.refs_3_, ...), custom_call_target="tpu_custom_call" | custom-call | tf_op jit(solution)/shard_map/mix_outer/pallas_call | solution.py:42
  20.5 0.0 collective-permute-done.6.refs_1_.refs_3_
  20.6 0.1 collective-permute-done.3.refs_9_.inner
  20.6 1.7 %front_outer.1 = (bf16[2,256,512]{2,1,0:T(8,128)(2,1)S(1)}, bf16[80,1024]{1,0:T(8,128)(2,1)S(1)}) custom-call(bf16[48,1024]{1,0:T(8,128)(2,1)S(1)} %slice.14.refs_0_, bf16[48,1024]{1,0:T(8,128)(2,1)S(1)} %collective-permute-done.5.refs_1_, bf16[112,1024]{1,0:T(8,128)(2,1)S(1)} %slice.15.refs_2_, ...), custom_call_target="tpu_custom_call" | custom-call | tf_op jit(solution)/shard_map/front_outer/pallas_call | solution.py:42
  22.3 1.7 %collective-permute-start.7 = (bf16[80,1024]{1,0:T(8,128)(2,1)S(1)}, bf16[80,1024]{1,0:T(8,128)(2,1)S(1)}, u32[]{:S(2)}, u32[]{:S(2)}) collective-permute-start(bf16[80,1024]{1,0:T(8,128)(2,1)S(1)} %get-tuple-element.58), channel_id=1, source_target_pairs={{1,0},{0,1},{3,2},{2,3},{5,4},{4,5},{7,6},{6,7},{9,8},{8,9},{11,10... | collective-permute-start | bytes 491528 | tf_op jit(solution)/shard_map/ppermute | solution.py:24
  24.0 0.8 %attend_later.1 = bf16[48,1024]{1,0:T(8,128)(2,1)S(1)} custom-call(bf16[128,512]{1,0:T(8,128)(2,1)S(1)} %get-tuple-element.46.query.refs_6_, f32[128,512]{1,0:T(8,128)S(1)} %get-tuple-element.47.refs_7_.numer, f32[128,512]{1,0:T(8,128)S(1)} %get-tuple-element.54.refs_8_.denom, bf16[2,256,512]{2,1,0:T(8,128)(2,1)S(1)} %collective-permute-done.3.refs_9_.inner, ...), custom_call_target="tpu_custom_call" | custom-call | tf_op jit(solution)/shard_map/attend_later/pallas_call | solution.py:42
  24.8 0.5 %collective-permute-start.8 = (bf16[48,1024]{1,0:T(8,128)(2,1)S(1)}, bf16[48,1024]{1,0:T(8,128)(2,1)S(1)}, u32[]{:S(2)}, u32[]{:S(2)}) collective-permute-start(bf16[48,1024]{1,0:T(8,128)(2,1)S(1)} %attend_later.1), channel_id=1, source_target_pairs={{1,0},{0,1},{3,2},{2,3},{5,4},{4,5},{7,6},{6,7},{9,8},{8,9},{11,10... | collective-permute-start | bytes 294920 | tf_op jit(solution)/shard_map/ppermute | solution.py:24
  25.2 1.5 %attend_own.1 = f32[128,1024]{1,0:T(8,128)S(1)} custom-call(bf16[128,1024]{1,0:T(8,128)(2,1)S(1)} %get-tuple-element.43.normed, bf16[3,1024,512]{2,1,0:T(8,128)(2,1)S(1)} %get-tuple-element.42.refs_11_.refs_5_.weight, bf16[2,256,512]{2,1,0:T(8,128)(2,1)S(1)} %get-tuple-element.44.pair, bf16[2,256,512]{2,1,0:T(8,128)(2,1)S(1)} %collective-permute-done.3.refs_9_.inner, ...), custom_call_target="tpu_custom_call" | custom-call | tf_op jit(solution)/shard_map/attend_own/pallas_call | solution.py:42
  26.8 4.1 %collective-permute-done.8 = bf16[48,1024]{1,0:T(8,128)(2,1)S(1)} collective-permute-done((bf16[48,1024]{1,0:T(8,128)(2,1)S(1)}, bf16[48,1024]{1,0:T(8,128)(2,1)S(1)}, u32[]{:S(2)}, u32[]{:S(2)}) %collective-permute-start.8) | collective-permute-done | bytes 98336 | tf_op jit(solution)/shard_map/ppermute | solution.py:24
  30.9 0.8 %add_convert_fusion = bf16[128,1024]{1,0:T(8,128)(2,1)} fusion(f32[128,1024]{1,0:T(8,128)S(1)} %attend_own.1, bf16[48,1024]{1,0:T(8,128)(2,1)S(1)} %collective-permute-done.8, bf16[80,1024]{1,0:T(8,128)(2,1)S(1)} %collective-permute-done.7), kind=kLoop, calls=%fused_computation | loop fusion | flops 786432 | bytes 1048576 | tf_op jit(solution)/shard_map/convert_element_type | solution.py:351
  (8 shorter events, 0.1 us)
Async XLA Ops:
  0.0 11.4 %collective-permute-start.2 = (bf16[128,1024]{1,0:T(8,128)(2,1)}, bf16[128,1024]{1,0:T(8,128)(2,1)S(1)}, u32[]{:S(2)}, u32[]{:S(2)}) collective-permute-start(bf16[128,1024]{1,0:T(8,128)(2,1)} %position.1), channel_id=1, source_target_pairs={{1,0},{0,1},{3,2},{2,3},{5,4},{4,5},{7,6},{6,7},{9,8},{8,9},{11,10... | collective-permute-start | bytes 786440 | tf_op jit(solution)/shard_map/ppermute | solution.py:24
  4.1 10.0 %collective-permute-start.4 = (bf16[160,1024]{1,0:T(8,128)(2,1)S(1)}, bf16[160,1024]{1,0:T(8,128)(2,1)S(1)}, u32[]{:S(2)}, u32[]{:S(2)}) collective-permute-start(bf16[160,1024]{1,0:T(8,128)(2,1)S(1)} %get-tuple-element.38.refs_7_), channel_id=1, source_target_pairs={{0,30},{2,4},{4,2},{6,8},{8,6},{10,12},{12,10},{14,16},{16,14},{18... | collective-permute-start | bytes 983048 | tf_op jit(solution)/shard_map/ppermute | solution.py:33
  7.9 6.2 %collective-permute-start = (bf16[104,1024]{1,0:T(8,128)(2,1)S(1)}, bf16[104,1024]{1,0:T(8,128)(2,1)S(1)}, u32[]{:S(2)}, u32[]{:S(2)}) collective-permute-start(bf16[104,1024]{1,0:T(8,128)(2,1)S(1)} %get-tuple-element.32.refs_0_), channel_id=1, source_target_pairs={{1,0},{0,1},{3,2},{2,3},{5,4},{4,5},{7,6},{6,7},{9,8},{8,9},{11,10... | collective-permute-start | bytes 638984 | tf_op jit(solution)/shard_map/ppermute | solution.py:24
  11.4 9.2 %collective-permute-start.6 = (bf16[112,1024]{1,0:T(8,128)(2,1)S(1)}, bf16[112,1024]{1,0:T(8,128)(2,1)S(1)}, u32[]{:S(2)}, u32[]{:S(2)}) collective-permute-start(bf16[112,1024]{1,0:T(8,128)(2,1)S(1)} %slice.16), channel_id=1, source_target_pairs={{0,30},{2,4},{4,2},{6,8},{8,6},{10,12},{12,10},{14,16},{16,14},{18... | collective-permute-start | bytes 688136 | tf_op jit(solution)/shard_map/ppermute | solution.py:33
  14.1 1.9 %collective-permute-start.1 = (bf16[64,1024]{1,0:T(8,128)(2,1)S(1)}, bf16[64,1024]{1,0:T(8,128)(2,1)S(1)}, u32[]{:S(2)}, u32[]{:S(2)}) collective-permute-start(bf16[64,1024]{1,0:T(8,128)(2,1)S(1)} %slice.13), channel_id=1, source_target_pairs={{2,0},{0,2},{6,4},{4,6},{10,8},{8,10},{14,12},{12,14},{18,16},{16,... | collective-permute-start | bytes 393224 | tf_op jit(solution)/shard_map/ppermute | solution.py:28
  14.2 5.3 %collective-permute-start.5 = (bf16[48,1024]{1,0:T(8,128)(2,1)S(1)}, bf16[48,1024]{1,0:T(8,128)(2,1)S(1)}, u32[]{:S(2)}, u32[]{:S(2)}) collective-permute-start(bf16[48,1024]{1,0:T(8,128)(2,1)S(1)} %slice.14.refs_0_), channel_id=1, source_target_pairs={{1,0},{0,1},{3,2},{2,3},{5,4},{4,5},{7,6},{6,7},{9,8},{8,9},{11,10... | collective-permute-start | bytes 294920 | tf_op jit(solution)/shard_map/ppermute | solution.py:24
  18.7 2.0 %collective-permute-start.3 = (bf16[2,256,512]{2,1,0:T(8,128)(2,1)S(1)}, bf16[2,256,512]{2,1,0:T(8,128)(2,1)S(1)}, u32[]{:S(2)}, u32[]{:S(2)}) collective-permute-start(bf16[2,256,512]{2,1,0:T(8,128)(2,1)S(1)} %get-tuple-element.44.pair), channel_id=1, source_target_pairs={{2,0},{0,2},{6,4},{4,6},{10,8},{8,10},{14,12},{12,14},{18,16},{16,... | collective-permute-start | bytes 1572872 | tf_op jit(solution)/shard_map/ppermute | solution.py:28
  22.3 8.5 %collective-permute-start.7 = (bf16[80,1024]{1,0:T(8,128)(2,1)S(1)}, bf16[80,1024]{1,0:T(8,128)(2,1)S(1)}, u32[]{:S(2)}, u32[]{:S(2)}) collective-permute-start(bf16[80,1024]{1,0:T(8,128)(2,1)S(1)} %get-tuple-element.58), channel_id=1, source_target_pairs={{1,0},{0,1},{3,2},{2,3},{5,4},{4,5},{7,6},{6,7},{9,8},{8,9},{11,10... | collective-permute-start | bytes 491528 | tf_op jit(solution)/shard_map/ppermute | solution.py:24
  24.8 6.1 %collective-permute-start.8 = (bf16[48,1024]{1,0:T(8,128)(2,1)S(1)}, bf16[48,1024]{1,0:T(8,128)(2,1)S(1)}, u32[]{:S(2)}, u32[]{:S(2)}) collective-permute-start(bf16[48,1024]{1,0:T(8,128)(2,1)S(1)} %attend_later.1), channel_id=1, source_target_pairs={{1,0},{0,1},{3,2},{2,3},{5,4},{4,5},{7,6},{6,7},{9,8},{8,9},{11,10... | collective-permute-start | bytes 294920 | tf_op jit(solution)/shard_map/ppermute | solution.py:24
